TPU v7x, 128 devices: a whole 4x4x4 slice. The times are simulated.
128 devices in a mesh: dp: 16 (over y, z), head: 8 (over x, core).
Axes of the slice: x: 4, y: 4, z: 4, core: 2. Of those that a mesh axis runs over, the one named last changes fastest.
Arguments:
- queries: bfloat16 [768, 128, 576], P('dp', 'head'), may hold values from -48 to 48
- kv_pool: bfloat16 [2048, 64, 576], P('dp'), may hold values from -6.1 to 6.1
- page_table: int32 [256, 8], P('dp'), may hold values from 0 to 2047, as said below
- cache_len: int32 [256], P('dp'), may hold values from 1 to 509, as said below
- accepted: int32 [256], P('dp'), may hold values from 0 to 2
- w_uv: bfloat16 [128, 512, 128], P('head'), may hold values from -0.75 to 0.75
- w_o: bfloat16 [16384, 7168], P('head', 'dp'), may hold values from -0.125 to 0.125
- residual: bfloat16 [768, 7168], P('dp'), may hold values from -6 to 6
- norm_gain: float32 [7168], replicated, may hold values from 0.5 to 1.5
- expert_ids: int32 [768, 8], P('dp'), may hold values from 0 to 15, all different within a row; in each aligned block of 48 rows (0 to 47, 48 to 95, ...) at most 32 rows name the same one
- gate_weights: float32 [768, 8], P('dp'), may hold values from 0.1 to 0.5
- w_gate: bfloat16 [16, 7168, 2048], P('dp', None, 'head'), may hold values from -0.0625 to 0.0625
- w_up: bfloat16 [16, 7168, 2048], P('dp', None, 'head'), may hold values from -0.0625 to 0.0625
- w_down: bfloat16 [16, 2048, 7168], P('dp', 'head'), may hold values from -0.125 to 0.125
Outputs:
- attended: bfloat16 [768, 7168], P('dp')
- routed: bfloat16 [768, 7168], P('dp', 'head')
Inputs may be any that keep to these rules, and one draw needn't show every extreme that they name: `page_table`: A global page number is a dp index times 128 plus one of that index's pages; no page serves two requests, and one request's pages lie on one dp index. On every dp index exactly 8 requests have their pages on other indices, each on a different one; among the indices that lend to index d are d + 1, d - 1 and d + 16 / 2 (modulo 16); every index lends to exactly 8 requests. cache_len + accepted is at most 509 for every request and equals it for some request in every draw. `expert_ids`: within the tokens of one dp index (aligned blocks of 48 rows) no expert is named more than 32 times.
All inputs are finite; a program needn't handle non-finite values.
Results may differ from a plain program's by a relative error of at most 0.035.
Values may be sent and summed in bfloat16 or wider, within the bound.
No kernel may reach another device: no remote copies, remote signals or barrier semaphores. Data moves between devices by JAX's collectives and lax.ppermute only.
A program may use at most 192 MiB of HBM per device.

v0:
```python
import jax
import jax.numpy as jnp
from jax import lax
from jax.experimental import pallas as pl
from jax.experimental.pallas import tpu as pltpu
from jax.sharding import Mesh
from jax.sharding import PartitionSpec as P

LAT = 512
DP = ("y", "z")
HEAD = ("x", "core")
ALL = ("y", "z", "x", "core")
RING = 4
DP_N = 16
HEAD_N = 8
PAGES = 128
CAP = 32

softmax_scale = 192.0 ** (-0.5)
norm_eps = 1e-06
bf16 = jnp.bfloat16
f32 = jnp.float32
i32 = jnp.int32


def hop(array, axis, step):
    return lax.ppermute(array, axis, [((i + step) % RING, i) for i in range(RING)])


def send(array, axis, step):
    return lax.ppermute(array, axis, [(i, (i + step) % RING) for i in range(RING)])


def other_core(array):
    return lax.ppermute(array, "core", [(0, 1), (1, 0)])


def pack_kernel(me_ref, page_ref, held_ref, taken_ref, query_ref, ids_ref, gate_ref, out_ref, who_ref):
    me = me_ref[0]
    width = query_ref.shape[2]
    requests, per = page_ref.shape
    rows = ids_ref.shape[0]
    lanes = out_ref.shape[2] - width

    def put(block, first):
        row = lax.broadcasted_iota(i32, (block.shape[1], lanes), 0)
        lane = lax.broadcasted_iota(i32, (block.shape[1], lanes), 1)
        spot = jnp.where(lane == row + first, 1.0, 0.0).astype(bf16)
        return jnp.dot(block.astype(bf16), spot, preferred_element_type=f32)

    gates = gate_ref[...]
    coarse = gates.astype(bf16).astype(f32)
    base = put(ids_ref[...].astype(f32), 0) + put(coarse, 40) + put(gates - coarse, 48)
    row = lax.broadcasted_iota(i32, (rows, lanes), 0)
    lane = lax.broadcasted_iota(i32, (rows, lanes), 1)

    def clear(i, carry):
        who_ref[i] = -1
        return carry

    lax.fori_loop(0, DP_N, clear, 0)
    lane = jnp.where(row == 0, lane, -1)
    for r in range(requests):
        lender = page_ref[r, 0] // PAGES
        base = jnp.where(lane == 24 + r, lender.astype(f32), base)

        @pl.when(lender != me)
        def _():
            who_ref[lender] = r

    def one(i, carry):
        found = who_ref[i]
        r = jnp.maximum(found, 0)
        seen = held_ref[r] + taken_ref[r]
        told = [page_ref[r, k] - page_ref[r, 0] // PAGES * PAGES for k in range(per)]
        told += [seen // 2, seen % 2, jnp.where(found >= 0, 1, 0)]
        line = base
        for k, value in enumerate(told):
            line = jnp.where(lane == 8 + k, value.astype(f32), line)
        out_ref[i, :, :width] = query_ref[r]
        out_ref[i, :, width:] = line.astype(bf16)
        return carry

    lax.fori_loop(0, DP_N, one, 0)


def pack(me, page_table, cache_len, accepted, query_rows, expert_ids, gate_weights):
    count, rows, width = query_rows.shape
    scalar, vector = (pl.BlockSpec(memory_space=m) for m in (pltpu.SMEM, pltpu.VMEM))
    return pl.pallas_call(
        pack_kernel,
        out_shape=jax.ShapeDtypeStruct((DP_N, rows, width + 64), bf16),
        in_specs=[scalar] * 4 + [vector] * 3,
        out_specs=vector,
        scratch_shapes=[pltpu.SMEM((DP_N,), i32)],
        compiler_params=pltpu.CompilerParams(vmem_limit_bytes=32 * 2**20),
        name="pack",
    )(me, page_table, cache_len, accepted, query_rows, expert_ids, gate_weights)


def attend_kernel(
    me_ref, page_ref, held_ref, taken_ref, told_ref, own_ref, far_ref, pool_ref, out_ref,
    which_ref, list_ref, seen_ref, keys_ref, sems,
):
    me = me_ref[0]
    count, rows, width = own_ref.shape
    per = page_ref.shape[1]
    page_rows = pool_ref.shape[1]
    pair = keys_ref.shape[1]

    def plan(r, found):
        own_at, far_at = found
        mine = page_ref[r, 0] // PAGES == me
        lent = told_ref[r, 10] > 0

        @pl.when(mine)
        def _():
            at = jnp.minimum(own_at, 7)
            which_ref[at] = r
            seen_ref[at] = held_ref[r] + taken_ref[r]
            for k in range(per):
                list_ref[at * per + k] = page_ref[r, k] - me * PAGES

        @pl.when(lent)
        def _():
            at = 8 + jnp.minimum(far_at, 7)
            which_ref[at] = r
            seen_ref[at] = told_ref[r, 8] * 2 + told_ref[r, 9]
            for k in range(per):
                list_ref[at * per + k] = told_ref[r, k]

        return own_at + mine.astype(i32), far_at + lent.astype(i32)

    lax.fori_loop(0, count, plan, (jnp.int32(0), jnp.int32(0)))

    def copies(turn, slot):
        made = []
        for n in range(pair):
            for k in range(per):
                page = list_ref[(turn * pair + n) * per + k]
                made.append(
                    pltpu.make_async_copy(
                        pool_ref.at[page],
                        keys_ref.at[slot, n, pl.ds(k * page_rows, page_rows)],
                        sems.at[slot, n, k],
                    )
                )
        return made

    for copy in copies(0, 0):
        copy.start()
    position = lax.broadcasted_iota(i32, (rows, per * page_rows), 1)
    draft = lax.broadcasted_iota(i32, (rows, per * page_rows), 0) // (rows // 3)
    turns = count // pair

    def turn_step(turn, carry):
        slot = lax.rem(turn, 2)

        @pl.when(turn + 1 < turns)
        def _():
            for copy in copies(turn + 1, 1 - slot):
                copy.start()

        for copy in copies(turn, slot):
            copy.wait()
        for n in range(pair):
            at = turn * pair + n
            which = which_ref[at]
            queries = jnp.where(at < 8, own_ref[which], far_ref[which, :, :width])
            keys = keys_ref[slot, n]
            scores = (
                lax.dot_general(queries, keys, (((1,), (1,)), ((), ())), preferred_element_type=f32)
                * softmax_scale
            )
            allowed = position <= seen_ref[at] + draft
            highest = jnp.max(jnp.where(allowed, scores, -1e30), axis=-1, keepdims=True)
            weights = jnp.where(allowed, jnp.exp(jnp.where(allowed, scores - highest, 0.0)), 0.0)
            probs = (weights / jnp.sum(weights, axis=-1, keepdims=True)).astype(bf16)
            out_ref[at] = lax.dot_general(
                probs, keys[:, :LAT], (((1,), (0,)), ((), ())), preferred_element_type=f32
            ).astype(bf16)
        return carry

    lax.fori_loop(0, turns, turn_step, 0)


def attend(me, page_table, cache_len, accepted, told, own_queries, far_queries, kv_pool):
    count, rows, width = own_queries.shape
    per, page_rows = page_table.shape[1], kv_pool.shape[1]
    pair = 2
    scalar, vector = (pl.BlockSpec(memory_space=m) for m in (pltpu.SMEM, pltpu.VMEM))
    return pl.pallas_call(
        attend_kernel,
        out_shape=jax.ShapeDtypeStruct((count, rows, LAT), bf16),
        in_specs=[scalar] * 5 + [vector] * 2 + [pl.BlockSpec(memory_space=pl.ANY)],
        out_specs=vector,
        scratch_shapes=[
            pltpu.SMEM((count,), i32),
            pltpu.SMEM((count * per,), i32),
            pltpu.SMEM((count,), i32),
            pltpu.VMEM((2, pair, per * page_rows, width), bf16),
            pltpu.SemaphoreType.DMA((2, pair, per)),
        ],
        compiler_params=pltpu.CompilerParams(vmem_limit_bytes=32 * 2**20),
        cost_estimate=pl.CostEstimate(
            flops=count * rows * 512 * 1088 * 2, bytes_accessed=12_000_000, transcendentals=0
        ),
        name="attend",
    )(me, page_table, cache_len, accepted, told, own_queries, far_queries, kv_pool)


def sort_kernel(spot_ref, gate_ref, up_ref, down_ref, own_ref, other_ref, down_own_ref, down_other_ref, sems):
    wide = down_own_ref.shape[1] // RING
    units = gate_ref.shape[2]
    made = []
    for side, (rows_ref, cols_ref) in enumerate(
        ((own_ref, down_own_ref), (other_ref, down_other_ref))
    ):
        for k in range(RING):
            start = pl.multiple_of(spot_ref[side * RING + k] * wide, 128)
            there = pl.ds(start, wide)
            here = pl.ds(k * wide, wide)
            made.append(
                (gate_ref.at[0, there], rows_ref.at[here, pl.ds(0, units)], sems.at[side, k, 0])
            )
            made.append(
                (up_ref.at[0, there], rows_ref.at[here, pl.ds(units, units)], sems.at[side, k, 1])
            )
            made.append((down_ref.at[0, :, there], cols_ref.at[:, here], sems.at[side, k, 2]))
    made = [pltpu.make_async_copy(*one) for one in made]
    for copy in made:
        copy.start()
    for copy in made:
        copy.wait()


def sort_weights(spots, w_gate, w_up, w_down):
    units, model = w_down.shape[1:]
    anywhere = pl.BlockSpec(memory_space=pl.ANY)
    return pl.pallas_call(
        sort_kernel,
        out_shape=[jax.ShapeDtypeStruct((model // 2, 2 * units), bf16)] * 2
        + [jax.ShapeDtypeStruct((units, model // 2), bf16)] * 2,
        in_specs=[pl.BlockSpec(memory_space=pltpu.SMEM)] + [anywhere] * 3,
        out_specs=[anywhere] * 4,
        scratch_shapes=[pltpu.SemaphoreType.DMA((2, RING, 3))],
        cost_estimate=pl.CostEstimate(flops=0, bytes_accessed=22_000_000, transcendentals=0),
        name="sort_weights",
    )(spots, w_gate, w_up, w_down)


def before(count):
    at = jnp.arange(count, dtype=i32)
    return at[:, None] < at[None, :]


def shards(
    queries,
    kv_pool,
    page_table,
    cache_len,
    accepted,
    w_uv,
    w_o,
    residual,
    norm_gain,
    expert_ids,
    gate_weights,
    w_gate,
    w_up,
    w_down,
):
    at_x, at_y, at_z = lax.axis_index("x"), lax.axis_index("y"), lax.axis_index("z")
    at_core = lax.axis_index("core")
    dp_index = at_y * RING + at_z
    requests = page_table.shape[0]
    tokens, head_group, width = queries.shape
    query_rows = queries.reshape(requests, 3 * head_group, width)
    dps = jnp.arange(DP_N, dtype=i32)
    me = dp_index.astype(i32)[None]

    packed = pack(me, page_table, cache_len, accepted, query_rows, expert_ids, gate_weights)
    arrived = lax.all_to_all(packed, DP, 0, 0, tiled=True)

    _, w_gate, w_up, w_down = lax.optimization_barrier((packed, w_gate, w_up, w_down))
    ring_at = (at_x + jnp.arange(RING, dtype=i32)) % RING * 2
    spots = jnp.concatenate([ring_at + at_core, ring_at + 1 - at_core])
    in_own, in_give, out_own, out_give = sort_weights(spots, w_gate, w_up, w_down)
    in_other, out_other = other_core(in_give), other_core(out_give)

    told = arrived[:, :, width:]
    all_ids = told[:, :, :8].astype(i32)
    all_weights = told[:, :, 40:48].astype(f32) + told[:, :, 48:56].astype(f32)
    lenders = told[:, 0, 24:40].astype(i32)
    line = told[:, 0, 8:24].astype(i32)
    latent = attend(me, page_table, cache_len, accepted, line, query_rows, arrived, kv_pool)
    values = jnp.einsum(
        "thc,hcv->thv",
        latent.reshape(tokens, head_group, LAT),
        w_uv,
        preferred_element_type=f32,
    ).astype(bf16)
    values = values.reshape(tokens, head_group * w_uv.shape[2])

    values, in_own, in_other, out_own, out_other = lax.optimization_barrier(
        (values, in_own, in_other, out_own, out_other)
    )

    half = values.shape[1] // 2

    def spread(block, first, second):
        line = jnp.concatenate([block] + [hop(block, first, k) for k in (1, 2, 3)], axis=0)
        return [line] + [hop(line, second, k) for k in (1, 2, 3)]

    zy = spread(values[:, :half], "z", "y")
    yz = spread(values[:, half:], "y", "z")
    part_zy = jnp.concatenate(
        [jnp.dot(a, w_o[:half], preferred_element_type=f32) for a in zy], axis=0
    )
    part_yz = jnp.concatenate(
        [jnp.dot(a, w_o[half:], preferred_element_type=f32) for a in yz], axis=0
    )
    columns = w_o.shape[1]
    part_yz = part_yz.reshape(RING, RING, tokens, columns).transpose(1, 0, 2, 3)
    projected = (part_zy + part_yz.reshape(-1, columns)).astype(bf16)

    is_own = (lenders == dps[:, None]).astype(i32)
    own_slot = jnp.sum(is_own[:, :, None] * before(requests)[None], axis=1)
    at_lender = (lenders[:, :, None] == dps[None, None, :]).astype(i32)
    away = at_lender * (dps[:, None, None] != dps[None, None, :])
    lends = jnp.sum(away, axis=1)
    lend_rank = jnp.sum(before(DP_N)[:, :, None] * lends[:, None, :], axis=0)
    far_slot = 8 + jnp.sum(at_lender * lend_rank[:, None, :], axis=2)
    slot = jnp.where(is_own > 0, own_slot, far_slot)
    turned = ((lenders // RING - at_y) % RING) * RING + (lenders % RING - at_z) % RING
    first_row = (turned * requests + slot) * 3
    source = (first_row[:, :, None] + jnp.arange(3, dtype=i32)).reshape(RING, 2, 2 * tokens)
    source = lax.dynamic_slice_in_dim(jnp.concatenate([source, source], 0), at_x, RING, 0)
    source = lax.dynamic_slice_in_dim(jnp.concatenate([source, source], 1), at_core, 2, 1)
    source = source.transpose(1, 0, 2).reshape(-1)
    rows_all = projected.shape[0]
    moves = (source[:, None] == jnp.arange(rows_all, dtype=i32)[None, :]).astype(bf16)
    homed = jnp.dot(moves, projected, preferred_element_type=f32)
    kept = homed[: rows_all // 2] + other_core(homed[rows_all // 2 :].astype(bf16)).astype(f32)
    kept = kept.reshape(RING, 2 * tokens, columns)
    mine = kept[0]
    for k in (2, 1, 3):
        mine = mine + send(kept[k].astype(bf16), "x", k).astype(f32)
    mine = mine.astype(bf16)

    odd = dp_index % 2
    low, high = mine[:tokens], mine[tokens:]
    got = []
    for turn in (0, 1):
        pairs = []
        for d in range(DP_N):
            for h in range(HEAD_N):
                pairs.append((d * HEAD_N + h, (2 * h + (turn + d) % 2) * HEAD_N + d // 2))
        block = jnp.where((odd + turn) % 2 == 0, low, high)
        got.append(lax.ppermute(block, ALL, pairs))
    attention = jnp.concatenate(
        [jnp.where(odd == 0, got[0], got[1]), jnp.where(odd == 0, got[1], got[0])], axis=1
    )
    wide_piece = 2 * columns
    head_index = at_x * 2 + at_core
    near = lax.dynamic_slice_in_dim(residual, head_index * wide_piece, wide_piece, 1)
    piece = (near.astype(f32) + attention.astype(f32)).astype(bf16)

    part = tokens // 3

    def ring(block, axis, along):
        return jnp.concatenate([block] + [hop(block, axis, k) for k in (1, 2, 3)], axis=along)

    pa, pb, pc = piece[:part], piece[part : 2 * part], piece[2 * part :]
    pa, pb, pc = ring(pa, "z", 0), ring(pb, "y", 0), ring(pc, "x", 1)
    out_c = pc
    pa, pb, pc = ring(pa, "y", 0), ring(pb, "x", 1), ring(pc, "z", 0)
    out_b = pb[:part]
    pa, pb, pc = ring(pa, "x", 1), ring(pb, "z", 0), ring(pc, "y", 0)
    out_a = pa[:part]
    here = jnp.concatenate([out_a, out_b, out_c], axis=0)
    there = other_core(here)
    first = jnp.where(at_core == 0, here, there)
    second = jnp.where(at_core == 0, there, here)
    blocks = []
    for k in range(RING):
        for side in (first, second):
            blocks.append(side[:, k * wide_piece : (k + 1) * wide_piece])
    row = jnp.concatenate(blocks, axis=1)
    row = jnp.concatenate([row, row], axis=1)
    attended = lax.dynamic_slice_in_dim(
        row, (RING - at_x) % RING * 2 * wide_piece, residual.shape[1], 1
    )

    units = w_gate.shape[2]
    gains = jnp.concatenate([norm_gain, norm_gain]).reshape(2 * RING, 2, wide_piece)
    gains = lax.dynamic_slice(gains, (at_x, at_core, 0), (RING, 1, wide_piece)).reshape(1, -1)

    weight = jnp.sum(jnp.where(all_ids == dp_index, all_weights, 0.0), axis=2)
    weight = weight.reshape(RING, RING, tokens)
    weight = lax.dynamic_slice_in_dim(jnp.concatenate([weight, weight], 0), at_y, RING, 0)
    weight = lax.dynamic_slice_in_dim(jnp.concatenate([weight, weight], 1), at_z, RING, 1)
    parts = []
    for n, block in enumerate((pa, pb, pc)):
        scale = weight[:, :, n * part : (n + 1) * part]
        scale = (scale.transpose(1, 0, 2) if n == 1 else scale).reshape(-1, 1)
        wide = block.astype(f32)
        squares = jnp.sum(wide * wide, axis=1, keepdims=True)
        gained = lax.optimization_barrier((wide * gains).astype(bf16))
        sums = jnp.dot(gained, in_own, preferred_element_type=f32)
        give = jnp.dot(gained, in_other, preferred_element_type=f32)
        swapped = other_core(jnp.concatenate([give, sums], axis=1).astype(bf16)).astype(f32)
        squares = squares + other_core(squares)
        root = lax.rsqrt(squares / residual.shape[1] + norm_eps)
        own_sum = (sums + swapped[:, : 2 * units]) * root
        other_sum = (give + swapped[:, 2 * units :]) * root
        hidden = [jax.nn.silu(a[:, :units]) * a[:, units:] * scale for a in (own_sum, other_sum)]
        hidden = lax.optimization_barrier([a.astype(bf16) for a in hidden])
        parts.append(
            (
                jnp.dot(hidden[0], out_own, preferred_element_type=f32)
                + jnp.dot(hidden[1], out_other, preferred_element_type=f32)
            ).astype(bf16)
        )

    def gather_sum(block, axis, along):
        size = block.shape[along] // RING
        cuts = [lax.slice_in_dim(block, k * size, (k + 1) * size, axis=along) for k in range(RING)]
        total = cuts[0].astype(f32)
        for k in (2, 1, 3):
            total = total + send(cuts[k].astype(bf16), axis, k).astype(f32)
        return total

    ra, rb, rc = parts
    ra, rb, rc = gather_sum(ra, "x", 1), gather_sum(rb, "z", 0), gather_sum(rc, "y", 0)
    ra, rb, rc = gather_sum(ra, "y", 0), gather_sum(rb, "x", 1), gather_sum(rc, "z", 0)
    ra, rb, rc = gather_sum(ra, "z", 0), gather_sum(rb, "y", 0), gather_sum(rc, "x", 1)
    routed = jnp.concatenate([ra, rb, rc], axis=0).astype(bf16)
    return (attended, routed)


def solution(mesh):
    grid = Mesh(mesh.devices.reshape(RING, RING, RING, 2), ALL)
    return jax.shard_map(
        shards,
        mesh=grid,
        in_specs=(
            P(DP, HEAD, None),
            P(DP, None, None),
            P(DP, None),
            P(DP),
            P(DP),
            P(HEAD, None, None),
            P(HEAD, DP),
            P(DP, None),
            P(),
            P(DP, None),
            P(DP, None),
            P(DP, None, HEAD),
            P(DP, None, HEAD),
            P(DP, HEAD, None),
        ),
        out_specs=(P(DP, None), P(DP, HEAD)),
        check_vma=False,
    )
```

profile of v0, /device:TPU:0, one launch (start us, length us, event | category | flops | bytes accessed | tf_op | source)
XLA Modules:
  0.0 644.5 jit_solution(7776989224244064363)
XLA Ops:
  5.6 2.4 pack.1
  9.6 335.5 %sort_weights.1 = (bf16[3584,512]{1,0:T(8,128)(2,1)}, bf16[3584,512]{1,0:T(8,128)(2,1)}, bf16[256,3584]{1,0:T(8,128)(2,1)}, bf16[256,3584]{1,0:T(8,128)(2,1)}) custom-call(s32[8]{0:T(128)} %pad_add_fusion.spot_ref, bf16[1,7168,256]{2,1,0:T(8,128)(2,1)} %gate_ref.1, bf16[1,7168,256]{2,1,0:T(8,128)(2,1)} %up_ref, bf16[1,256,7168]{2,1,0:T(8,128)(2,1)} %down_ref), custom_call_target="tpu_custom_call" | custom-call | bytes 22000000 | tf_op jit(solution)/shard_map/sort_weights/pallas_call | solution.py:240
  345.2 8.1 %all-to-all-start = ((bf16[16,48,640]{2,1,0:T(8,128)(2,1)}), bf16[16,48,640]{2,1,0:T(8,128)(2,1)S(1)}, u32[]{:S(2)}, u32[]{:S(2)}) async-start(bf16[16,48,640]{2,1,0:T(8,128)(2,1)} %copy-done.3), calls=%async_computation | async-start | bytes 1966080 | tf_op jit(solution)/shard_map/all_to_all | solution.py:283
  353.6 14.8 %copy.64.pool_ref = bf16[128,64,576]{2,1,0:T(8,128)(2,1)} copy(bf16[128,64,576]{0,2,1:T(8,128)(2,1)} %param.15) | data formatting | bytes 18874368 | tf_op args[1]
  368.4 2.5 all-to-all-done.far_ref
  372.1 4.0 copy-done.2
  377.3 25.5 %attend.1 = bf16[16,48,512]{2,1,0:T(8,128)(2,1)S(1)} custom-call(s32[1]{0:T(128)} %bitcast.me_ref, s32[16,8]{1,0:T(8,128)S(1)} %copy.59.page_ref, s32[16]{0:T(128)S(1)} %copy-done.7, s32[16]{0:T(128)S(1)} %copy-done.9, s32[16,16]{1,0:T(8,128)S(1)} %bitcast.62, bf16[16,48,576]{2,1,0:T(8,128)(2,1)S(1)} %bitcast.60, ...), custom_call_target="tpu_custom_call" | custom-call | flops 855638016 | bytes 12000000 | tf_op jit(solution)/shard_map/attend/pallas_call | solution.py:192
  404.0 2.4 collective-permute-start.9
  408.8 2.7 collective-permute-start.3
  414.1 2.2 collective-permute-start.11
  416.4 7.2 %collective-permute-done.2 = bf16[48,1024]{1,0:T(8,128)(2,1)S(1)} collective-permute-done((bf16[48,1024]{1,0:T(8,128)(2,1)S(1)}, bf16[48,1024]{1,0:T(8,128)(2,1)S(1)}, u32[]{:S(2)}, u32[]{:S(2)}) %collective-permute-start.2) | collective-permute-done | bytes 98336 | tf_op jit(solution)/shard_map/ppermute | solution.py:27
  423.9 3.1 collective-permute-start.5
  429.8 3.4 collective-permute-done.11
  436.2 2.7 collective-permute-done.7
  443.9 3.1 collective-permute-start.15
  449.0 2.2 collective-permute-done.15
  456.8 3.1 collective-permute-done.19
  461.1 8.3 %collective-permute-start.31 = (bf16[16,896]{1,0:T(8,128)(2,1)S(1)}, bf16[16,896]{1,0:T(8,128)(2,1)S(1)}, u32[]{:S(2)}, u32[]{:S(2)}) collective-permute-start(bf16[16,896]{1,0:T(8,128)(2,1)S(1)} %get-tuple-element.117), channel_id=1, source_target_pairs={{96,0},{0,32},{32,64},{64,96},{97,1},{1,33},{33,65},{65,97},{98,2}... | collective-permute-start | bytes 86024 | tf_op jit(solution)/shard_map/ppermute | solution.py:27
  469.4 6.9 %collective-permute-start.30 = (bf16[16,896]{1,0:T(8,128)(2,1)S(1)}, bf16[16,896]{1,0:T(8,128)(2,1)S(1)}, u32[]{:S(2)}, u32[]{:S(2)}) collective-permute-start(bf16[16,896]{1,0:T(8,128)(2,1)S(1)} %get-tuple-element.117), channel_id=1, source_target_pairs={{64,0},{96,32},{0,64},{32,96},{65,1},{97,33},{1,65},{33,97},{66,2}... | collective-permute-start | bytes 86024 | tf_op jit(solution)/shard_map/ppermute | solution.py:27
  478.0 2.9 collective-permute-start.21
  482.6 4.3 collective-permute-start.36
  489.1 2.8 collective-permute-start.32
  495.0 2.6 collective-permute-start.23
  497.7 2.3 collective-permute-start.66
  503.2 2.1 collective-permute-start.27
  507.8 3.5 collective-permute-start.67
  511.3 10.2 %collective-permute-done.28 = bf16[256,896]{1,0:T(8,128)(2,1)S(1)} collective-permute-done((bf16[256,896]{1,0:T(8,128)(2,1)S(1)}, bf16[256,896]{1,0:T(8,128)(2,1)S(1)}, u32[]{:S(2)}, u32[]{:S(2)}) %collective-permute-start.28) | collective-permute-done | bytes 458784 | tf_op jit(solution)/shard_map/ppermute | solution.py:27
  525.2 2.1 collective-permute-start.69
  527.8 2.5 collective-permute-start.68
  530.3 14.6 %collective-permute-done.68 = bf16[64,3584]{1,0:T(8,128)(2,1)S(1)} collective-permute-done((bf16[64,3584]{1,0:T(8,128)(2,1)S(1)}, bf16[64,3584]{1,0:T(8,128)(2,1)S(1)}, u32[]{:S(2)}, u32[]{:S(2)}) %collective-permute-start.68) | collective-permute-done | bytes 458784 | tf_op jit(solution)/shard_map/ppermute | solution.py:27
  545.0 3.1 fusion.6
  549.5 3.3 fusion.112
  554.0 3.1 fusion.114
  558.2 3.1 fusion.116
  567.9 2.3 fusion.118
  574.9 2.1 fusion.117
  579.1 3.1 collective-permute-start.43
  582.2 2.1 fusion.119
  587.5 7.6 %collective-permute-done.57 = bf16[64,3584]{1,0:T(8,128)(2,1)S(1)} collective-permute-done((bf16[64,3584]{1,0:T(8,128)(2,1)S(1)}, bf16[64,3584]{1,0:T(8,128)(2,1)S(1)}, u32[]{:S(2)}, u32[]{:S(2)}) %collective-permute-start.57) | collective-permute-done | bytes 458784 | tf_op jit(solution)/shard_map/ppermute | solution.py:31
  596.5 2.1 collective-permute-start.73
  598.6 3.5 collective-permute-done.43
  603.3 2.0 collective-permute-start.60
  605.6 4.5 collective-permute-done.72
  612.8 6.7 %collective-permute-done.73 = bf16[64,3584]{1,0:T(8,128)(2,1)S(1)} collective-permute-done((bf16[64,3584]{1,0:T(8,128)(2,1)S(1)}, bf16[64,3584]{1,0:T(8,128)(2,1)S(1)}, u32[]{:S(2)}, u32[]{:S(2)}) %collective-permute-start.73) | collective-permute-done | bytes 458784 | tf_op jit(solution)/shard_map/ppermute | solution.py:31
  623.2 2.1 collective-permute-start.77
  631.6 2.5 collective-permute-start.49
  635.3 3.1 collective-permute-start.80
  641.0 2.6 collective-permute-done.79
  (293 shorter events, 93.3 us)
Async XLA Ops:
  345.1 58.8 %collective-permute-start = (bf16[3584,512]{1,0:T(8,128)(2,1)}, bf16[3584,512]{1,0:T(8,128)(2,1)}, u32[]{:S(2)}, u32[]{:S(2)}) collective-permute-start(bf16[3584,512]{1,0:T(8,128)(2,1)} %get-tuple-element.24), channel_id=1, source_target_pairs={{0,1},{1,0},{2,3},{3,2},{4,5},{5,4},{6,7},{7,6},{8,9},{9,8},{10,11... | collective-permute-start | bytes 11010056 | tf_op jit(solution)/shard_map/ppermute | solution.py:35
  345.2 25.8 %all-to-all-start = ((bf16[16,48,640]{2,1,0:T(8,128)(2,1)}), bf16[16,48,640]{2,1,0:T(8,128)(2,1)S(1)}, u32[]{:S(2)}, u32[]{:S(2)}) async-start(bf16[16,48,640]{2,1,0:T(8,128)(2,1)} %copy-done.3), calls=%async_computation | async-start | bytes 1966080 | tf_op jit(solution)/shard_map/all_to_all | solution.py:283
  353.3 50.5 %collective-permute-start.1 = (bf16[256,3584]{1,0:T(8,128)(2,1)}, bf16[256,3584]{1,0:T(8,128)(2,1)}, u32[]{:S(2)}, u32[]{:S(2)}) collective-permute-start(bf16[256,3584]{1,0:T(8,128)(2,1)} %get-tuple-element.26), channel_id=1, source_target_pairs={{0,1},{1,0},{2,3},{3,2},{4,5},{5,4},{6,7},{7,6},{8,9},{9,8},{10,11... | collective-permute-start | bytes 5505032 | tf_op jit(solution)/shard_map/ppermute | solution.py:35
  404.0 9.0 %collective-permute-start.9 = (bf16[48,1024]{1,0:T(8,128)(2,1)S(1)}, bf16[48,1024]{1,0:T(8,128)(2,1)S(1)}, u32[]{:S(2)}, u32[]{:S(2)}) collective-permute-start(bf16[48,1024]{1,0:T(8,128)(2,1)S(1)} %get-tuple-element.99), channel_id=1, source_target_pairs={{64,0},{96,32},{0,64},{32,96},{65,1},{97,33},{1,65},{33,97},{66,2}... | collective-permute-start | bytes 294920 | tf_op jit(solution)/shard_map/ppermute | solution.py:27
  407.6 8.7 %collective-permute-start.4 = (bf16[48,1024]{1,0:T(8,128)(2,1)S(1)}, bf16[48,1024]{1,0:T(8,128)(2,1)S(1)}, u32[]{:S(2)}, u32[]{:S(2)}) collective-permute-start(bf16[48,1024]{1,0:T(8,128)(2,1)S(1)} %get-tuple-element.100), channel_id=1, source_target_pairs={{24,0},{0,8},{8,16},{16,24},{25,1},{1,9},{9,17},{17,25},{26,2},{2,... | collective-permute-start | bytes 294920 | tf_op jit(solution)/shard_map/ppermute | solution.py:27
  411.5 12.1 %collective-permute-start.2 = (bf16[48,1024]{1,0:T(8,128)(2,1)S(1)}, bf16[48,1024]{1,0:T(8,128)(2,1)S(1)}, u32[]{:S(2)}, u32[]{:S(2)}) collective-permute-start(bf16[48,1024]{1,0:T(8,128)(2,1)S(1)} %get-tuple-element.100), channel_id=1, source_target_pairs={{8,0},{16,8},{24,16},{0,24},{9,1},{17,9},{25,17},{1,25},{10,2},{18... | collective-permute-start | bytes 294920 | tf_op jit(solution)/shard_map/ppermute | solution.py:27
  413.0 16.0 %collective-permute-start.12 = (bf16[192,1024]{1,0:T(8,128)(2,1)S(1)}, bf16[192,1024]{1,0:T(8,128)(2,1)S(1)}, u32[]{:S(2)}, u32[]{:S(2)}) collective-permute-start(bf16[192,1024]{1,0:T(8,128)(2,1)S(1)} %pad_maximum_fusion.9), channel_id=1, source_target_pairs={{16,0},{24,8},{0,16},{8,24},{17,1},{25,9},{1,17},{9,25},{18,2},{26... | collective-permute-start | bytes 1179656 | tf_op jit(solution)/shard_map/ppermute | solution.py:27
  414.1 19.1 %collective-permute-start.11 = (bf16[192,1024]{1,0:T(8,128)(2,1)S(1)}, bf16[192,1024]{1,0:T(8,128)(2,1)S(1)}, u32[]{:S(2)}, u32[]{:S(2)}) collective-permute-start(bf16[192,1024]{1,0:T(8,128)(2,1)S(1)} %pad_maximum_fusion.9), channel_id=1, source_target_pairs={{8,0},{16,8},{24,16},{0,24},{9,1},{17,9},{25,17},{1,25},{10,2},{18... | collective-permute-start | bytes 1179656 | tf_op jit(solution)/shard_map/ppermute | solution.py:27
  416.3 17.3 %collective-permute-start.13 = (bf16[192,1024]{1,0:T(8,128)(2,1)S(1)}, bf16[192,1024]{1,0:T(8,128)(2,1)S(1)}, u32[]{:S(2)}, u32[]{:S(2)}) collective-permute-start(bf16[192,1024]{1,0:T(8,128)(2,1)S(1)} %pad_maximum_fusion.9), channel_id=1, source_target_pairs={{24,0},{0,8},{8,16},{16,24},{25,1},{1,9},{9,17},{17,25},{26,2},{2,... | collective-permute-start | bytes 1179656 | tf_op jit(solution)/shard_map/ppermute | solution.py:27
  423.6 10.5 %collective-permute-start.6 = (bf16[192,1024]{1,0:T(8,128)(2,1)S(1)}, bf16[192,1024]{1,0:T(8,128)(2,1)S(1)}, u32[]{:S(2)}, u32[]{:S(2)}) collective-permute-start(bf16[192,1024]{1,0:T(8,128)(2,1)S(1)} %pad_maximum_fusion.8), channel_id=1, source_target_pairs={{64,0},{96,32},{0,64},{32,96},{65,1},{97,33},{1,65},{33,97},{66,2}... | collective-permute-start | bytes 1179656 | tf_op jit(solution)/shard_map/ppermute | solution.py:27
  423.9 11.9 %collective-permute-start.5 = (bf16[192,1024]{1,0:T(8,128)(2,1)S(1)}, bf16[192,1024]{1,0:T(8,128)(2,1)S(1)}, u32[]{:S(2)}, u32[]{:S(2)}) collective-permute-start(bf16[192,1024]{1,0:T(8,128)(2,1)S(1)} %pad_maximum_fusion.8), channel_id=1, source_target_pairs={{32,0},{64,32},{96,64},{0,96},{33,1},{65,33},{97,65},{1,97},{34,2}... | collective-permute-start | bytes 1179656 | tf_op jit(solution)/shard_map/ppermute | solution.py:27
  429.1 9.8 %collective-permute-start.7 = (bf16[192,1024]{1,0:T(8,128)(2,1)S(1)}, bf16[192,1024]{1,0:T(8,128)(2,1)S(1)}, u32[]{:S(2)}, u32[]{:S(2)}) collective-permute-start(bf16[192,1024]{1,0:T(8,128)(2,1)S(1)} %pad_maximum_fusion.8), channel_id=1, source_target_pairs={{96,0},{0,32},{32,64},{64,96},{97,1},{1,33},{33,65},{65,97},{98,2}... | collective-permute-start | bytes 1179656 | tf_op jit(solution)/shard_map/ppermute | solution.py:27
  461.1 19.9 %collective-permute-start.31 = (bf16[16,896]{1,0:T(8,128)(2,1)S(1)}, bf16[16,896]{1,0:T(8,128)(2,1)S(1)}, u32[]{:S(2)}, u32[]{:S(2)}) collective-permute-start(bf16[16,896]{1,0:T(8,128)(2,1)S(1)} %get-tuple-element.117), channel_id=1, source_target_pairs={{96,0},{0,32},{32,64},{64,96},{97,1},{1,33},{33,65},{65,97},{98,2}... | collective-permute-start | bytes 86024 | tf_op jit(solution)/shard_map/ppermute | solution.py:27
  469.4 13.2 %collective-permute-start.30 = (bf16[16,896]{1,0:T(8,128)(2,1)S(1)}, bf16[16,896]{1,0:T(8,128)(2,1)S(1)}, u32[]{:S(2)}, u32[]{:S(2)}) collective-permute-start(bf16[16,896]{1,0:T(8,128)(2,1)S(1)} %get-tuple-element.117), channel_id=1, source_target_pairs={{64,0},{96,32},{0,64},{32,96},{65,1},{97,33},{1,65},{33,97},{66,2}... | collective-permute-start | bytes 86024 | tf_op jit(solution)/shard_map/ppermute | solution.py:27
  478.0 8.9 %collective-permute-start.22 = (bf16[16,896]{1,0:T(8,128)(2,1)S(1)}, bf16[16,896]{1,0:T(8,128)(2,1)S(1)}, u32[]{:S(2)}, u32[]{:S(2)}) collective-permute-start(bf16[16,896]{1,0:T(8,128)(2,1)S(1)} %get-tuple-element.114), channel_id=1, source_target_pairs={{24,0},{0,8},{8,16},{16,24},{25,1},{1,9},{9,17},{17,25},{26,2},{2,... | collective-permute-start | bytes 86024 | tf_op jit(solution)/shard_map/ppermute | solution.py:27
  478.0 9.0 %collective-permute-start.21 = (bf16[16,896]{1,0:T(8,128)(2,1)S(1)}, bf16[16,896]{1,0:T(8,128)(2,1)S(1)}, u32[]{:S(2)}, u32[]{:S(2)}) collective-permute-start(bf16[16,896]{1,0:T(8,128)(2,1)S(1)} %get-tuple-element.114), channel_id=1, source_target_pairs={{16,0},{24,8},{0,16},{8,24},{17,1},{25,9},{1,17},{9,25},{18,2},{26... | collective-permute-start | bytes 86024 | tf_op jit(solution)/shard_map/ppermute | solution.py:27
  481.0 8.1 %collective-permute-start.20 = (bf16[16,896]{1,0:T(8,128)(2,1)S(1)}, bf16[16,896]{1,0:T(8,128)(2,1)S(1)}, u32[]{:S(2)}, u32[]{:S(2)}) collective-permute-start(bf16[16,896]{1,0:T(8,128)(2,1)S(1)} %get-tuple-element.114), channel_id=1, source_target_pairs={{8,0},{16,8},{24,16},{0,24},{9,1},{17,9},{25,17},{1,25},{10,2},{18... | collective-permute-start | bytes 86024 | tf_op jit(solution)/shard_map/ppermute | solution.py:27
  482.6 9.3 %collective-permute-start.36 = (bf16[16,896]{1,0:T(8,128)(2,1)S(1)}, bf16[16,896]{1,0:T(8,128)(2,1)S(1)}, u32[]{:S(2)}, u32[]{:S(2)}) collective-permute-start(bf16[16,896]{1,0:T(8,128)(2,1)S(1)} %get-tuple-element.116), channel_id=1, source_target_pairs={{4,0},{6,2},{0,4},{2,6},{5,1},{7,3},{1,5},{3,7},{12,8},{14,10},{8,... | collective-permute-start | bytes 86024 | tf_op jit(solution)/shard_map/ppermute | solution.py:27
  487.0 7.9 %collective-permute-start.34 = (bf16[64,896]{1,0:T(8,128)(2,1)S(1)}, bf16[64,896]{1,0:T(8,128)(2,1)S(1)}, u32[]{:S(2)}, u32[]{:S(2)}) collective-permute-start(bf16[64,896]{1,0:T(8,128)(2,1)S(1)} %pad_maximum_fusion.11), channel_id=1, source_target_pairs={{6,0},{0,2},{2,4},{4,6},{7,1},{1,3},{3,5},{5,7},{14,8},{8,10},{10,... | collective-permute-start | bytes 344072 | tf_op jit(solution)/shard_map/ppermute | solution.py:27
  489.0 8.6 %collective-permute-start.33 = (bf16[64,896]{1,0:T(8,128)(2,1)S(1)}, bf16[64,896]{1,0:T(8,128)(2,1)S(1)}, u32[]{:S(2)}, u32[]{:S(2)}) collective-permute-start(bf16[64,896]{1,0:T(8,128)(2,1)S(1)} %pad_maximum_fusion.11), channel_id=1, source_target_pairs={{4,0},{6,2},{0,4},{2,6},{5,1},{7,3},{1,5},{3,7},{12,8},{14,10},{8,... | collective-permute-start | bytes 344072 | tf_op jit(solution)/shard_map/ppermute | solution.py:27
  489.1 8.6 %collective-permute-start.32 = (bf16[64,896]{1,0:T(8,128)(2,1)S(1)}, bf16[64,896]{1,0:T(8,128)(2,1)S(1)}, u32[]{:S(2)}, u32[]{:S(2)}) collective-permute-start(bf16[64,896]{1,0:T(8,128)(2,1)S(1)} %pad_maximum_fusion.11), channel_id=1, source_target_pairs={{2,0},{4,2},{6,4},{0,6},{3,1},{5,3},{7,5},{1,7},{10,8},{12,10},{14... | collective-permute-start | bytes 344072 | tf_op jit(solution)/shard_map/ppermute | solution.py:27
  491.9 10.5 %collective-permute-start.25 = (bf16[64,896]{1,0:T(8,128)(2,1)S(1)}, bf16[64,896]{1,0:T(8,128)(2,1)S(1)}, u32[]{:S(2)}, u32[]{:S(2)}) collective-permute-start(bf16[64,896]{1,0:T(8,128)(2,1)S(1)} %pad_maximum_fusion.10), channel_id=1, source_target_pairs={{96,0},{0,32},{32,64},{64,96},{97,1},{1,33},{33,65},{65,97},{98,2}... | collective-permute-start | bytes 344072 | tf_op jit(solution)/shard_map/ppermute | solution.py:27
  493.1 8.3 %collective-permute-start.24 = (bf16[64,896]{1,0:T(8,128)(2,1)S(1)}, bf16[64,896]{1,0:T(8,128)(2,1)S(1)}, u32[]{:S(2)}, u32[]{:S(2)}) collective-permute-start(bf16[64,896]{1,0:T(8,128)(2,1)S(1)} %pad_maximum_fusion.10), channel_id=1, source_target_pairs={{64,0},{96,32},{0,64},{32,96},{65,1},{97,33},{1,65},{33,97},{66,2}... | collective-permute-start | bytes 344072 | tf_op jit(solution)/shard_map/ppermute | solution.py:27
  500.1 7.7 %collective-permute-start.65 = (bf16[16,3584]{1,0:T(8,128)(2,1)S(1)}, bf16[16,3584]{1,0:T(8,128)(2,1)S(1)}, u32[]{:S(2)}, u32[]{:S(2)}) collective-permute-start(bf16[16,3584]{1,0:T(8,128)(2,1)S(1)} %get-tuple-element.110), channel_id=1, source_target_pairs={{16,0},{24,8},{0,16},{8,24},{17,1},{25,9},{1,17},{9,25},{18,2},{26... | collective-permute-start | bytes 344072 | tf_op jit(solution)/shard_map/ppermute | solution.py:27
  501.4 43.5 %collective-permute-start.52 = (bf16[64,3584]{1,0:T(8,128)(2,1)S(1)}, bf16[64,3584]{1,0:T(8,128)(2,1)S(1)}, u32[]{:S(2)}, u32[]{:S(2)}) collective-permute-start(bf16[64,3584]{1,0:T(8,128)(2,1)S(1)} %pad_maximum_fusion.6), channel_id=1, source_target_pairs={{24,0},{0,8},{8,16},{16,24},{25,1},{1,9},{9,17},{17,25},{26,2},{2,... | collective-permute-start | bytes 1376264 | tf_op jit(solution)/shard_map/ppermute | solution.py:27
  502.5 19.1 %collective-permute-start.28 = (bf16[256,896]{1,0:T(8,128)(2,1)S(1)}, bf16[256,896]{1,0:T(8,128)(2,1)S(1)}, u32[]{:S(2)}, u32[]{:S(2)}) collective-permute-start(bf16[256,896]{1,0:T(8,128)(2,1)S(1)} %constant_dynamic-update-slice_fusion), channel_id=1, source_target_pairs={{6,0},{0,2},{2,4},{4,6},{7,1},{1,3},{3,5},{5,7},{14,8},{8,10},{10,... | collective-permute-start | bytes 1376264 | tf_op jit(solution)/shard_map/ppermute | solution.py:27
  503.2 20.4 %collective-permute-start.27 = (bf16[256,896]{1,0:T(8,128)(2,1)S(1)}, bf16[256,896]{1,0:T(8,128)(2,1)S(1)}, u32[]{:S(2)}, u32[]{:S(2)}) collective-permute-start(bf16[256,896]{1,0:T(8,128)(2,1)S(1)} %constant_dynamic-update-slice_fusion), channel_id=1, source_target_pairs={{4,0},{6,2},{0,4},{2,6},{5,1},{7,3},{1,5},{3,7},{12,8},{14,10},{8,... | collective-permute-start | bytes 1376264 | tf_op jit(solution)/shard_map/ppermute | solution.py:27
  505.3 19.8 %collective-permute-start.26 = (bf16[256,896]{1,0:T(8,128)(2,1)S(1)}, bf16[256,896]{1,0:T(8,128)(2,1)S(1)}, u32[]{:S(2)}, u32[]{:S(2)}) collective-permute-start(bf16[256,896]{1,0:T(8,128)(2,1)S(1)} %constant_dynamic-update-slice_fusion), channel_id=1, source_target_pairs={{2,0},{4,2},{6,4},{0,6},{3,1},{5,3},{7,5},{1,7},{10,8},{12,10},{14... | collective-permute-start | bytes 1376264 | tf_op jit(solution)/shard_map/ppermute | solution.py:27
  507.8 20.0 %collective-permute-start.67 = (bf16[64,3584]{1,0:T(8,128)(2,1)S(1)}, bf16[64,3584]{1,0:T(8,128)(2,1)S(1)}, u32[]{:S(2)}, u32[]{:S(2)}) collective-permute-start(bf16[64,3584]{1,0:T(8,128)(2,1)S(1)} %pad_maximum_fusion.7), channel_id=1, source_target_pairs={{32,0},{64,32},{96,64},{0,96},{33,1},{65,33},{97,65},{1,97},{34,2}... | collective-permute-start | bytes 1376264 | tf_op jit(solution)/shard_map/ppermute | solution.py:27
  521.6 23.4 %collective-permute-start.51 = (bf16[64,3584]{1,0:T(8,128)(2,1)S(1)}, bf16[64,3584]{1,0:T(8,128)(2,1)S(1)}, u32[]{:S(2)}, u32[]{:S(2)}) collective-permute-start(bf16[64,3584]{1,0:T(8,128)(2,1)S(1)} %pad_maximum_fusion.6), channel_id=1, source_target_pairs={{16,0},{24,8},{0,16},{8,24},{17,1},{25,9},{1,17},{9,25},{18,2},{26... | collective-permute-start | bytes 1376264 | tf_op jit(solution)/shard_map/ppermute | solution.py:27
  523.6 21.4 %collective-permute-start.50 = (bf16[64,3584]{1,0:T(8,128)(2,1)S(1)}, bf16[64,3584]{1,0:T(8,128)(2,1)S(1)}, u32[]{:S(2)}, u32[]{:S(2)}) collective-permute-start(bf16[64,3584]{1,0:T(8,128)(2,1)S(1)} %pad_maximum_fusion.6), channel_id=1, source_target_pairs={{8,0},{16,8},{24,16},{0,24},{9,1},{17,9},{25,17},{1,25},{10,2},{18... | collective-permute-start | bytes 1376264 | tf_op jit(solution)/shard_map/ppermute | solution.py:27
  525.2 19.7 %collective-permute-start.69 = (bf16[64,3584]{1,0:T(8,128)(2,1)S(1)}, bf16[64,3584]{1,0:T(8,128)(2,1)S(1)}, u32[]{:S(2)}, u32[]{:S(2)}) collective-permute-start(bf16[64,3584]{1,0:T(8,128)(2,1)S(1)} %pad_maximum_fusion.7), channel_id=1, source_target_pairs={{96,0},{0,32},{32,64},{64,96},{97,1},{1,33},{33,65},{65,97},{98,2}... | collective-permute-start | bytes 1376264 | tf_op jit(solution)/shard_map/ppermute | solution.py:27
  527.8 17.1 %collective-permute-start.68 = (bf16[64,3584]{1,0:T(8,128)(2,1)S(1)}, bf16[64,3584]{1,0:T(8,128)(2,1)S(1)}, u32[]{:S(2)}, u32[]{:S(2)}) collective-permute-start(bf16[64,3584]{1,0:T(8,128)(2,1)S(1)} %pad_maximum_fusion.7), channel_id=1, source_target_pairs={{64,0},{96,32},{0,64},{32,96},{65,1},{97,33},{1,65},{33,97},{66,2}... | collective-permute-start | bytes 1376264 | tf_op jit(solution)/shard_map/ppermute | solution.py:27
  571.0 15.0 %collective-permute-start.55 = (bf16[64,3584]{1,0:T(8,128)(2,1)S(1)}, bf16[64,3584]{1,0:T(8,128)(2,1)S(1)}, u32[]{:S(2)}, u32[]{:S(2)}) collective-permute-start(bf16[64,3584]{1,0:T(8,128)(2,1)S(1)} %get-tuple-element.67), channel_id=1, source_target_pairs={{0,16},{8,24},{16,0},{24,8},{1,17},{9,25},{17,1},{25,9},{2,18},{10... | collective-permute-start | bytes 1376264 | tf_op jit(solution)/shard_map/ppermute | solution.py:31
  572.9 22.3 %collective-permute-start.57 = (bf16[64,3584]{1,0:T(8,128)(2,1)S(1)}, bf16[64,3584]{1,0:T(8,128)(2,1)S(1)}, u32[]{:S(2)}, u32[]{:S(2)}) collective-permute-start(bf16[64,3584]{1,0:T(8,128)(2,1)S(1)} %get-tuple-element.68), channel_id=1, source_target_pairs={{0,24},{8,0},{16,8},{24,16},{1,25},{9,1},{17,9},{25,17},{2,26},{10... | collective-permute-start | bytes 1376264 | tf_op jit(solution)/shard_map/ppermute | solution.py:31
  573.8 22.4 %collective-permute-start.56 = (bf16[64,3584]{1,0:T(8,128)(2,1)S(1)}, bf16[64,3584]{1,0:T(8,128)(2,1)S(1)}, u32[]{:S(2)}, u32[]{:S(2)}) collective-permute-start(bf16[64,3584]{1,0:T(8,128)(2,1)S(1)} %get-tuple-element.69), channel_id=1, source_target_pairs={{0,8},{8,16},{16,24},{24,0},{1,9},{9,17},{17,25},{25,1},{2,10},{10... | collective-permute-start | bytes 1376264 | tf_op jit(solution)/shard_map/ppermute | solution.py:31
  577.8 18.7 %collective-permute-start.41 = (bf16[256,896]{1,0:T(8,128)(2,1)S(1)}, bf16[256,896]{1,0:T(8,128)(2,1)S(1)}, u32[]{:S(2)}, u32[]{:S(2)}) collective-permute-start(bf16[256,896]{1,0:T(8,128)(2,1)S(1)} %get-tuple-element.64), channel_id=1, source_target_pairs={{0,4},{2,6},{4,0},{6,2},{1,5},{3,7},{5,1},{7,3},{8,12},{10,14},{12... | collective-permute-start | bytes 1376264 | tf_op jit(solution)/shard_map/ppermute | solution.py:31
  579.1 23.1 %collective-permute-start.43 = (bf16[256,896]{1,0:T(8,128)(2,1)S(1)}, bf16[256,896]{1,0:T(8,128)(2,1)S(1)}, u32[]{:S(2)}, u32[]{:S(2)}) collective-permute-start(bf16[256,896]{1,0:T(8,128)(2,1)S(1)} %get-tuple-element.65), channel_id=1, source_target_pairs={{0,6},{2,0},{4,2},{6,4},{1,7},{3,1},{5,3},{7,5},{8,14},{10,8},{12,... | collective-permute-start | bytes 1376264 | tf_op jit(solution)/shard_map/ppermute | solution.py:31
  586.0 17.4 %collective-permute-start.42 = (bf16[256,896]{1,0:T(8,128)(2,1)S(1)}, bf16[256,896]{1,0:T(8,128)(2,1)S(1)}, u32[]{:S(2)}, u32[]{:S(2)}) collective-permute-start(bf16[256,896]{1,0:T(8,128)(2,1)S(1)} %get-tuple-element.66), channel_id=1, source_target_pairs={{0,2},{2,4},{4,6},{6,0},{1,3},{3,5},{5,7},{7,1},{8,10},{10,12},{12... | collective-permute-start | bytes 1376264 | tf_op jit(solution)/shard_map/ppermute | solution.py:31
  595.1 15.0 %collective-permute-start.72 = (bf16[64,3584]{1,0:T(8,128)(2,1)S(1)}, bf16[64,3584]{1,0:T(8,128)(2,1)S(1)}, u32[]{:S(2)}, u32[]{:S(2)}) collective-permute-start(bf16[64,3584]{1,0:T(8,128)(2,1)S(1)} %get-tuple-element.70), channel_id=1, source_target_pairs={{0,64},{32,96},{64,0},{96,32},{1,65},{33,97},{65,1},{97,33},{2,66}... | collective-permute-start | bytes 1376264 | tf_op jit(solution)/shard_map/ppermute | solution.py:31
  596.2 15.5 %collective-permute-start.74 = (bf16[64,3584]{1,0:T(8,128)(2,1)S(1)}, bf16[64,3584]{1,0:T(8,128)(2,1)S(1)}, u32[]{:S(2)}, u32[]{:S(2)}) collective-permute-start(bf16[64,3584]{1,0:T(8,128)(2,1)S(1)} %get-tuple-element.71), channel_id=1, source_target_pairs={{0,96},{32,0},{64,32},{96,64},{1,97},{33,1},{65,33},{97,65},{2,98}... | collective-permute-start | bytes 1376264 | tf_op jit(solution)/shard_map/ppermute | solution.py:31
  596.5 23.0 %collective-permute-start.73 = (bf16[64,3584]{1,0:T(8,128)(2,1)S(1)}, bf16[64,3584]{1,0:T(8,128)(2,1)S(1)}, u32[]{:S(2)}, u32[]{:S(2)}) collective-permute-start(bf16[64,3584]{1,0:T(8,128)(2,1)S(1)} %get-tuple-element.72), channel_id=1, source_target_pairs={{0,32},{32,64},{64,96},{96,0},{1,33},{33,65},{65,97},{97,1},{2,34}... | collective-permute-start | bytes 1376264 | tf_op jit(solution)/shard_map/ppermute | solution.py:31
  602.2 18.3 %collective-permute-start.58 = (bf16[64,896]{1,0:T(8,128)(2,1)S(1)}, bf16[64,896]{1,0:T(8,128)(2,1)S(1)}, u32[]{:S(2)}, u32[]{:S(2)}) collective-permute-start(bf16[64,896]{1,0:T(8,128)(2,1)S(1)} %get-tuple-element.88), channel_id=1, source_target_pairs={{0,4},{2,6},{4,0},{6,2},{1,5},{3,7},{5,1},{7,3},{8,12},{10,14},{12... | collective-permute-start | bytes 344072 | tf_op jit(solution)/shard_map/ppermute | solution.py:31
  603.3 18.8 %collective-permute-start.60 = (bf16[64,896]{1,0:T(8,128)(2,1)S(1)}, bf16[64,896]{1,0:T(8,128)(2,1)S(1)}, u32[]{:S(2)}, u32[]{:S(2)}) collective-permute-start(bf16[64,896]{1,0:T(8,128)(2,1)S(1)} %get-tuple-element.89), channel_id=1, source_target_pairs={{0,6},{2,0},{4,2},{6,4},{1,7},{3,1},{5,3},{7,5},{8,14},{10,8},{12,... | collective-permute-start | bytes 344072 | tf_op jit(solution)/shard_map/ppermute | solution.py:31
  610.1 13.1 %collective-permute-start.59 = (bf16[64,896]{1,0:T(8,128)(2,1)S(1)}, bf16[64,896]{1,0:T(8,128)(2,1)S(1)}, u32[]{:S(2)}, u32[]{:S(2)}) collective-permute-start(bf16[64,896]{1,0:T(8,128)(2,1)S(1)} %get-tuple-element.90), channel_id=1, source_target_pairs={{0,2},{2,4},{4,6},{6,0},{1,3},{3,5},{5,7},{7,1},{8,10},{10,12},{12... | collective-permute-start | bytes 344072 | tf_op jit(solution)/shard_map/ppermute | solution.py:31
  611.7 13.7 %collective-permute-start.44 = (bf16[64,896]{1,0:T(8,128)(2,1)S(1)}, bf16[64,896]{1,0:T(8,128)(2,1)S(1)}, u32[]{:S(2)}, u32[]{:S(2)}) collective-permute-start(bf16[64,896]{1,0:T(8,128)(2,1)S(1)} %get-tuple-element.85), channel_id=1, source_target_pairs={{0,64},{32,96},{64,0},{96,32},{1,65},{33,97},{65,1},{97,33},{2,66}... | collective-permute-start | bytes 344072 | tf_op jit(solution)/shard_map/ppermute | solution.py:31
  625.8 8.3 %collective-permute-start.61 = (bf16[16,896]{1,0:T(8,128)(2,1)S(1)}, bf16[16,896]{1,0:T(8,128)(2,1)S(1)}, u32[]{:S(2)}, u32[]{:S(2)}) collective-permute-start(bf16[16,896]{1,0:T(8,128)(2,1)S(1)} %get-tuple-element.104), channel_id=1, source_target_pairs={{0,64},{32,96},{64,0},{96,32},{1,65},{33,97},{65,1},{97,33},{2,66}... | collective-permute-start | bytes 86024 | tf_op jit(solution)/shard_map/ppermute | solution.py:31
  630.6 7.9 %collective-permute-start.47 = (bf16[16,896]{1,0:T(8,128)(2,1)S(1)}, bf16[16,896]{1,0:T(8,128)(2,1)S(1)}, u32[]{:S(2)}, u32[]{:S(2)}) collective-permute-start(bf16[16,896]{1,0:T(8,128)(2,1)S(1)} %get-tuple-element.101), channel_id=1, source_target_pairs={{0,16},{8,24},{16,0},{24,8},{1,17},{9,25},{17,1},{25,9},{2,18},{10... | collective-permute-start | bytes 86024 | tf_op jit(solution)/shard_map/ppermute | solution.py:31
  (49 other events, 668.7 us)
where the time goes:
time: 652 us; the launch traced here: 644 us
  Pallas kernels  363 us (56%)
  starting transfers between devices  127 us (19%)
  waiting for transfers between devices  81.4 us (12%)
  local copies, waits for them, and re-layouts  29.2 us (4%)
  matrix products  28.3 us (4%)
  other arithmetic  13.4 us (2%)
    pallas_call x1, Pallas kernels, sort_weights(): pl.pallas_call(sort_kernel, out_shape=[jax.ShapeDtypeStruct((model // 2,...  336 us
    ppermute x39, starting transfers between devices, hop(): lax.ppermute(array, axis, [((i + step) % RING, i) for i in range(RING)])  72.5 us
    ppermute x30, starting transfers between devices, send(): lax.ppermute(array, axis, [(i, (i + step) % RING) for i in range(RING)])  41 us
    ppermute x39, waiting for transfers between devices, hop(): lax.ppermute(array, axis, [((i + step) % RING, i) for i in range(RING)])  40.1 us
    ppermute x30, waiting for transfers between devices, send(): lax.ppermute(array, axis, [(i, (i + step) % RING) for i in range(RING)])  34.8 us
    unnamed x59, local copies, waits for them, and re-layouts  26.7 us
    pallas_call x1, Pallas kernels, attend(): pl.pallas_call(attend_kernel, out_shape=jax.ShapeDtypeStruct((count, rows...  25.5 us
  transfers between devices with their start and end apart: 82, of which 25 were waited for; matrix products, arithmetic and copies ran while one was open for 5% of the time, Pallas kernels for 4%

commit v1 on v0

v1 whole, which is shorter than its diff:
```python
import jax
import jax.numpy as jnp
from jax import lax
from jax.experimental import pallas as pl
from jax.experimental.pallas import tpu as pltpu
from jax.sharding import Mesh
from jax.sharding import PartitionSpec as P

LAT = 512
DP = ("y", "z")
HEAD = ("x", "core")
ALL = ("y", "z", "x", "core")
RING = 4
DP_N = 16
HEAD_N = 8
PAGES = 128
CAP = 32

softmax_scale = 192.0 ** (-0.5)
norm_eps = 1e-06
bf16 = jnp.bfloat16
f32 = jnp.float32
i32 = jnp.int32


def hop(array, axis, step):
    return lax.ppermute(array, axis, [((i + step) % RING, i) for i in range(RING)])


def send(array, axis, step):
    return lax.ppermute(array, axis, [(i, (i + step) % RING) for i in range(RING)])


def other_core(array):
    return lax.ppermute(array, "core", [(0, 1), (1, 0)])


def pack_kernel(me_ref, page_ref, held_ref, taken_ref, query_ref, out_ref, who_ref):
    me = me_ref[0]
    width = query_ref.shape[2]
    requests, per = page_ref.shape
    rows = out_ref.shape[1]
    lanes = out_ref.shape[2] - width

    row = lax.broadcasted_iota(i32, (rows, lanes), 0)
    lane = lax.broadcasted_iota(i32, (rows, lanes), 1)

    def clear(i, carry):
        who_ref[i] = -1
        return carry

    lax.fori_loop(0, DP_N, clear, 0)
    lane = jnp.where(row == 0, lane, -1)
    base = jnp.zeros((rows, lanes), f32)
    for r in range(requests):
        lender = page_ref[r, 0] // PAGES
        base = jnp.where(lane == 24 + r, lender.astype(f32), base)

        @pl.when(lender != me)
        def _():
            who_ref[lender] = r

    def one(i, carry):
        found = who_ref[i]
        r = jnp.maximum(found, 0)
        seen = held_ref[r] + taken_ref[r]
        told = [page_ref[r, k] - page_ref[r, 0] // PAGES * PAGES for k in range(per)]
        told += [seen // 2, seen % 2, jnp.where(found >= 0, 1, 0)]
        line = base
        for k, value in enumerate(told):
            line = jnp.where(lane == 8 + k, value.astype(f32), line)
        out_ref[i, :, :width] = query_ref[r]
        out_ref[i, :, width:] = line.astype(bf16)
        return carry

    lax.fori_loop(0, DP_N, one, 0)


def pack(me, page_table, cache_len, accepted, query_rows):
    count, rows, width = query_rows.shape
    scalar, vector = (pl.BlockSpec(memory_space=m) for m in (pltpu.SMEM, pltpu.VMEM))
    return pl.pallas_call(
        pack_kernel,
        out_shape=jax.ShapeDtypeStruct((DP_N, rows, width + 64), bf16),
        in_specs=[scalar] * 4 + [vector],
        out_specs=vector,
        scratch_shapes=[pltpu.SMEM((DP_N,), i32)],
        compiler_params=pltpu.CompilerParams(vmem_limit_bytes=32 * 2**20),
        name="pack",
    )(me, page_table, cache_len, accepted, query_rows)


def plan_kernel(
    me_ref, page_ref, held_ref, taken_ref, told_ref, which_ref, list_ref, seen_ref
):
    me = me_ref[0]
    count, per = page_ref.shape

    def plan(r, found):
        own_at, far_at = found
        mine = page_ref[r, 0] // PAGES == me
        lent = told_ref[r, 10] > 0

        @pl.when(mine)
        def _():
            at = jnp.minimum(own_at, 7)
            which_ref[at] = r
            seen_ref[at] = held_ref[r] + taken_ref[r]
            for k in range(per):
                list_ref[at * per + k] = page_ref[r, k] - me * PAGES

        @pl.when(lent)
        def _():
            at = 8 + jnp.minimum(far_at, 7)
            which_ref[at] = r
            seen_ref[at] = told_ref[r, 8] * 2 + told_ref[r, 9]
            for k in range(per):
                list_ref[at * per + k] = told_ref[r, k]

        return own_at + mine.astype(i32), far_at + lent.astype(i32)

    lax.fori_loop(0, count, plan, (jnp.int32(0), jnp.int32(0)))


def plan(me, page_table, cache_len, accepted, told):
    count, per = page_table.shape
    scalar = pl.BlockSpec(memory_space=pltpu.SMEM)
    return pl.pallas_call(
        plan_kernel,
        out_shape=[
            jax.ShapeDtypeStruct((count,), i32),
            jax.ShapeDtypeStruct((count * per,), i32),
            jax.ShapeDtypeStruct((count,), i32),
        ],
        in_specs=[scalar] * 5,
        out_specs=[scalar] * 3,
        name="plan",
    )(me, page_table, cache_len, accepted, told)


def attend_kernel(pick_ref, page_ref, seen_ref, *refs):
    out_ref = refs[-1]
    step = pl.program_id(0)
    per = (len(refs) - 1) // 2
    for n in range(2):
        own_ref, far_ref, *pages = refs[n * per : (n + 1) * per]
        at = step * 2 + n
        width = own_ref.shape[2]
        queries = jnp.where(at < 8, own_ref[0], far_ref[0, :, :width])
        keys = jnp.concatenate([page[0] for page in pages], axis=0)
        scores = (
            lax.dot_general(queries, keys, (((1,), (1,)), ((), ())), preferred_element_type=f32)
            * softmax_scale
        )
        position = lax.broadcasted_iota(i32, scores.shape, 1)
        draft = lax.broadcasted_iota(i32, scores.shape, 0) // (scores.shape[0] // 3)
        allowed = position <= seen_ref[at] + draft
        highest = jnp.max(jnp.where(allowed, scores, -1e30), axis=-1, keepdims=True)
        weights = jnp.where(allowed, jnp.exp(jnp.where(allowed, scores - highest, 0.0)), 0.0)
        probs = (weights / jnp.sum(weights, axis=-1, keepdims=True)).astype(bf16)
        out_ref[n] = lax.dot_general(
            probs, keys[:, :LAT], (((1,), (0,)), ((), ())), preferred_element_type=f32
        ).astype(bf16)


def attend(pick, pages, seen, own_queries, far_queries, kv_pool):
    count, rows, width = own_queries.shape
    page_rows = kv_pool.shape[1]
    per = pages.shape[0] // count

    def specs(n):
        def own(i, pick, page, seen):
            return (pick[jnp.minimum(i * 2 + n, 6 + n)], 0, 0)

        def far(i, pick, page, seen):
            return (pick[jnp.maximum(i * 2 + n, 8 + n)], 0, 0)

        def page_spec(a):
            return pl.BlockSpec(
                (1, page_rows, width),
                lambda i, pick, page, seen: (page[(i * 2 + n) * per + a], 0, 0),
            )

        return [
            pl.BlockSpec((1, rows, width), own),
            pl.BlockSpec((1, rows, far_queries.shape[2]), far),
        ] + [page_spec(a) for a in range(per)]

    spec = pltpu.PrefetchScalarGridSpec(
        num_scalar_prefetch=3,
        grid=(count // 2,),
        in_specs=specs(0) + specs(1),
        out_specs=pl.BlockSpec((2, rows, LAT), lambda i, pick, page, seen: (i, 0, 0)),
    )
    group = [own_queries, far_queries] + [kv_pool] * per
    return pl.pallas_call(
        attend_kernel,
        out_shape=jax.ShapeDtypeStruct((count, rows, LAT), bf16),
        grid_spec=spec,
        compiler_params=pltpu.CompilerParams(vmem_limit_bytes=32 * 2**20),
        cost_estimate=pl.CostEstimate(
            flops=count * rows * 512 * 1088 * 2, bytes_accessed=12_000_000, transcendentals=0
        ),
        name="attend",
    )(pick, pages, seen, *group, *group)


def cut_kernel(spot_ref, gate_ref, up_ref, down_ref, rows_ref, cols_ref):
    units = gate_ref.shape[2]
    rows_ref[:, :units] = gate_ref[0]
    rows_ref[:, units:] = up_ref[0]
    cols_ref[...] = down_ref[0]


def cut_weights(spots, w_gate, w_up, w_down):
    units, model = w_down.shape[1:]
    wide = model // HEAD_N
    rows = pl.BlockSpec((1, wide, units), lambda i, spot: (0, spot[i], 0))
    spec = pltpu.PrefetchScalarGridSpec(
        num_scalar_prefetch=1,
        grid=(RING,),
        in_specs=[rows, rows, pl.BlockSpec((1, units, wide), lambda i, spot: (0, 0, spot[i]))],
        out_specs=[
            pl.BlockSpec((wide, 2 * units), lambda i, spot: (i, 0)),
            pl.BlockSpec((units, wide), lambda i, spot: (0, i)),
        ],
    )
    return pl.pallas_call(
        cut_kernel,
        out_shape=[
            jax.ShapeDtypeStruct((model // 2, 2 * units), bf16),
            jax.ShapeDtypeStruct((units, model // 2), bf16),
        ],
        grid_spec=spec,
        compiler_params=pltpu.CompilerParams(vmem_limit_bytes=32 * 2**20),
        cost_estimate=pl.CostEstimate(flops=0, bytes_accessed=11_000_000, transcendentals=0),
        name="cut_weights",
    )(spots, w_gate, w_up, w_down)


def before(count):
    at = jnp.arange(count, dtype=i32)
    return at[:, None] < at[None, :]


def shards(
    queries,
    kv_pool,
    page_table,
    cache_len,
    accepted,
    w_uv,
    w_o,
    residual,
    norm_gain,
    expert_ids,
    gate_weights,
    w_gate,
    w_up,
    w_down,
):
    at_x, at_y, at_z = lax.axis_index("x"), lax.axis_index("y"), lax.axis_index("z")
    at_core = lax.axis_index("core")
    dp_index = at_y * RING + at_z
    requests = page_table.shape[0]
    tokens, head_group, width = queries.shape
    query_rows = queries.reshape(requests, 3 * head_group, width)
    dps = jnp.arange(DP_N, dtype=i32)
    me = dp_index.astype(i32)[None]

    packed = pack(me, page_table, cache_len, accepted, query_rows)
    arrived = lax.all_to_all(packed, DP, 0, 0, tiled=True)
    told = arrived[:, 0, width:]
    lenders = told[:, 24:40].astype(i32)
    line = told[:, 8:24].astype(i32)
    latent = attend(
        *plan(me, page_table, cache_len, accepted, line), query_rows, arrived, kv_pool
    )
    values = jnp.einsum(
        "thc,hcv->thv",
        latent.reshape(tokens, head_group, LAT),
        w_uv,
        preferred_element_type=f32,
    ).astype(bf16)
    values = values.reshape(tokens, head_group * w_uv.shape[2])

    values, w_gate, w_up, w_down = lax.optimization_barrier((values, w_gate, w_up, w_down))
    ring_at = (at_x + jnp.arange(RING, dtype=i32)) % RING * 2
    in_give, out_give = cut_weights(ring_at + 1 - at_core, w_gate, w_up, w_down)
    in_own, out_own = cut_weights(ring_at + at_core, w_gate, w_up, w_down)
    in_other, out_other = other_core(in_give), other_core(out_give)

    half = values.shape[1] // 2

    def spread(block, first, second):
        line = jnp.concatenate([block] + [hop(block, first, k) for k in (1, 2, 3)], axis=0)
        return [line] + [hop(line, second, k) for k in (1, 2, 3)]

    zy = spread(values[:, :half], "z", "y")
    yz = spread(values[:, half:], "y", "z")
    part_zy = jnp.concatenate(
        [jnp.dot(a, w_o[:half], preferred_element_type=f32) for a in zy], axis=0
    )
    part_yz = jnp.concatenate(
        [jnp.dot(a, w_o[half:], preferred_element_type=f32) for a in yz], axis=0
    )
    columns = w_o.shape[1]
    part_yz = part_yz.reshape(RING, RING, tokens, columns).transpose(1, 0, 2, 3)
    projected = (part_zy + part_yz.reshape(-1, columns)).astype(bf16)

    is_own = (lenders == dps[:, None]).astype(i32)
    own_slot = jnp.sum(is_own[:, :, None] * before(requests)[None], axis=1)
    at_lender = (lenders[:, :, None] == dps[None, None, :]).astype(i32)
    away = at_lender * (dps[:, None, None] != dps[None, None, :])
    lends = jnp.sum(away, axis=1)
    lend_rank = jnp.sum(before(DP_N)[:, :, None] * lends[:, None, :], axis=0)
    far_slot = 8 + jnp.sum(at_lender * lend_rank[:, None, :], axis=2)
    slot = jnp.where(is_own > 0, own_slot, far_slot)
    turned = ((lenders // RING - at_y) % RING) * RING + (lenders % RING - at_z) % RING
    first_row = (turned * requests + slot) * 3
    source = (first_row[:, :, None] + jnp.arange(3, dtype=i32)).reshape(RING, 2, 2 * tokens)
    source = lax.dynamic_slice_in_dim(jnp.concatenate([source, source], 0), at_x, RING, 0)
    source = lax.dynamic_slice_in_dim(jnp.concatenate([source, source], 1), at_core, 2, 1)
    source = source.transpose(1, 0, 2).reshape(-1)
    rows_all = projected.shape[0]
    moves = (source[:, None] == jnp.arange(rows_all, dtype=i32)[None, :]).astype(bf16)
    homed = jnp.dot(moves, projected, preferred_element_type=f32)
    kept = homed[: rows_all // 2] + other_core(homed[rows_all // 2 :].astype(bf16)).astype(f32)
    kept = kept.reshape(RING, 2 * tokens, columns)
    mine = kept[0]
    for k in (2, 1, 3):
        mine = mine + send(kept[k].astype(bf16), "x", k).astype(f32)
    mine = mine.astype(bf16)

    odd = dp_index % 2
    low, high = mine[:tokens], mine[tokens:]
    got = []
    for turn in (0, 1):
        pairs = []
        for d in range(DP_N):
            for h in range(HEAD_N):
                pairs.append((d * HEAD_N + h, (2 * h + (turn + d) % 2) * HEAD_N + d // 2))
        block = jnp.where((odd + turn) % 2 == 0, low, high)
        got.append(lax.ppermute(block, ALL, pairs))
    attention = jnp.concatenate(
        [jnp.where(odd == 0, got[0], got[1]), jnp.where(odd == 0, got[1], got[0])], axis=1
    )
    wide_piece = 2 * columns
    head_index = at_x * 2 + at_core
    near = lax.dynamic_slice_in_dim(residual, head_index * wide_piece, wide_piece, 1)
    piece = (near.astype(f32) + attention.astype(f32)).astype(bf16)
    piece, in_own, in_other, out_own, out_other = lax.optimization_barrier(
        (piece, in_own, in_other, out_own, out_other)
    )

    here = jnp.concatenate([piece] + [hop(piece, "x", k) for k in (1, 2, 3)], axis=1)
    there = other_core(here)
    wide, wide_there = here.astype(f32), there.astype(f32)
    squares = jnp.sum(wide * wide, axis=1, keepdims=True) + jnp.sum(
        wide_there * wide_there, axis=1, keepdims=True
    )
    gains = jnp.concatenate([norm_gain, norm_gain]).reshape(2 * RING, 2, wide_piece)
    gains = lax.dynamic_slice(gains, (at_x, at_core, 0), (RING, 1, wide_piece)).reshape(1, -1)
    model = residual.shape[1]
    normed = (wide * lax.rsqrt(squares / model + norm_eps) * gains).astype(bf16)
    first = jnp.where(at_core == 0, here, there)
    second = jnp.where(at_core == 0, there, here)
    blocks = []
    for k in range(RING):
        for side in (first, second):
            blocks.append(side[:, k * wide_piece : (k + 1) * wide_piece])
    row = jnp.concatenate(blocks + blocks, axis=1)
    attended = lax.dynamic_slice_in_dim(row, (RING - at_x) % RING * 2 * wide_piece, model, 1)

    chosen = (expert_ids[:, :, None] == dps[None, None, :]).astype(i32)
    named = jnp.sum(chosen, axis=1)
    weight = jnp.sum(chosen.astype(f32) * gate_weights[:, :, None], axis=1)
    rank = jnp.sum(before(tokens)[:, :, None] * named[:, None, :], axis=0)
    rank = jnp.where(named > 0, rank, -1)
    ranks = jnp.arange(CAP, dtype=i32)
    placing = (rank.T[:, None, :] == ranks[None, :, None]).astype(bf16)
    placing = placing.reshape(DP_N * CAP, tokens)
    outgoing = jnp.dot(placing, normed, preferred_element_type=f32).astype(bf16)
    rows = lax.all_to_all(outgoing.reshape(DP_N, CAP, -1), DP, 0, 0, tiled=True)
    rows = rows.reshape(DP_N * CAP, -1)

    units = w_gate.shape[2]
    sums = jnp.dot(rows, in_own, preferred_element_type=f32)
    give = jnp.dot(rows, in_other, preferred_element_type=f32)
    swapped = other_core(jnp.concatenate([give, sums], axis=1).astype(bf16)).astype(f32)
    own_sum = sums + swapped[:, : 2 * units]
    other_sum = give + swapped[:, 2 * units :]
    hidden = [jax.nn.silu(a[:, :units]) * a[:, units:] for a in (own_sum, other_sum)]
    hidden = lax.optimization_barrier([a.astype(bf16) for a in hidden])
    output = jnp.dot(hidden[0], out_own, preferred_element_type=f32) + jnp.dot(
        hidden[1], out_other, preferred_element_type=f32
    )
    output = output.astype(bf16).reshape(DP_N, CAP, -1)
    returned = lax.all_to_all(output, DP, 0, 0, tiled=True).reshape(DP_N * CAP, -1)

    mix = jnp.where(rank[:, :, None] == ranks[None, None, :], weight[:, :, None], 0.0)
    mix = mix.reshape(tokens, DP_N * CAP)
    coarse = lax.reduce_precision(mix, 8, 7)
    both = jnp.concatenate([coarse.astype(bf16), (mix - coarse).astype(bf16)], axis=0)
    both = jnp.dot(both, returned, preferred_element_type=f32)
    mixed = both[:tokens] + both[tokens:]
    routed = mixed[:, :wide_piece]
    for k in (2, 1, 3):
        block = mixed[:, k * wide_piece : (k + 1) * wide_piece].astype(bf16)
        routed = routed + send(block, "x", k).astype(f32)
    return (attended, routed.astype(bf16))


def solution(mesh):
    grid = Mesh(mesh.devices.reshape(RING, RING, RING, 2), ALL)
    return jax.shard_map(
        shards,
        mesh=grid,
        in_specs=(
            P(DP, HEAD, None),
            P(DP, None, None),
            P(DP, None),
            P(DP),
            P(DP),
            P(HEAD, None, None),
            P(HEAD, DP),
            P(DP, None),
            P(),
            P(DP, None),
            P(DP, None),
            P(DP, None, HEAD),
            P(DP, None, HEAD),
            P(DP, HEAD, None),
        ),
        out_specs=(P(DP, None), P(DP, HEAD)),
        check_vma=False,
    )
```

time: 652 us -> 327 us (0.50)
  Pallas kernels: 363 us -> 19.8 us
  waiting for transfers between devices: 81.4 us -> 155 us
  starting transfers between devices: 127 us -> 64.7 us
  local copies, waits for them, and re-layouts: 29.2 us -> 43.5 us
    pallas_call x1 -> x3, Pallas kernels: 336 us -> 7.4 us  [the longest x2 5.02 us: cut_weights(): pl.pallas_call(cut_kernel, out_shape=[jax.ShapeDtypeStruct((model // 2, 2...]
    all_to_all x0 -> x2, waiting for transfers between devices: none -> 102 us  [the longest x1 52.9 us: shards(): lax.all_to_all(output, DP, 0, 0, tiled=True).reshape(DP_N * CAP, -1)]
    ppermute x39 -> x15, starting transfers between devices: 72.5 us -> 25.9 us  [hop(): lax.ppermute(array, axis, [((i + step) % RING, i) for i in range(RING)])]
    ppermute x30 -> x6, starting transfers between devices: 41 us -> 8.62 us  [send(): lax.ppermute(array, axis, [(i, (i + step) % RING) for i in range(RING)])]
    ppermute x30 -> x6, waiting for transfers between devices: 34.8 us -> 9.96 us  [send(): lax.ppermute(array, axis, [(i, (i + step) % RING) for i in range(RING)])]
    all_to_all x0 -> x2, starting transfers between devices: none -> 17.4 us  [the longest x1 12.5 us: shards(): lax.all_to_all(output, DP, 0, 0, tiled=True).reshape(DP_N * CAP, -1)]
    pallas_call x1, Pallas kernels: 25.5 us -> 10.2 us  [attend(): pl.pallas_call(attend_kernel, out_shape=jax.ShapeDtypeStruct((count, rows...]
    unnamed x59 -> x79, local copies, waits for them, and re-layouts: 26.7 us -> 40.6 us
  transfers between devices with their start and end apart: 82 -> 31, of which waited for: 25 -> 17; matrix products, arithmetic and copies ran while one was open for 5% -> 8% of each run, Pallas kernels for 4% -> 2%
where the time goes in v1:
time: 327 us; the launch traced here: 322 us
  waiting for transfers between devices  155 us (47%)
  starting transfers between devices  64.7 us (20%)
  local copies, waits for them, and re-layouts  43.5 us (13%)
  matrix products  28.6 us (9%)
  Pallas kernels  19.8 us (6%)
  other arithmetic  9.15 us (3%)
    all_to_all x1, waiting for transfers between devices, shards(): lax.all_to_all(output, DP, 0, 0, tiled=True).reshape(DP_N * CAP, -1)  52.9 us
    all_to_all x1, waiting for transfers between devices, shards(): rows = lax.all_to_all(outgoing.reshape(DP_N, CAP, -1), DP, 0, 0, tiled=True)  49.5 us
    unnamed x79, local copies, waits for them, and re-layouts  40.6 us
    ppermute x15, waiting for transfers between devices, hop(): lax.ppermute(array, axis, [((i + step) % RING, i) for i in range(RING)])  35.6 us
    ppermute x15, starting transfers between devices, hop(): lax.ppermute(array, axis, [((i + step) % RING, i) for i in range(RING)])  25.9 us
    all_to_all x1, starting transfers between devices, shards(): lax.all_to_all(output, DP, 0, 0, tiled=True).reshape(DP_N * CAP, -1)  12.5 us
    pallas_call x1, Pallas kernels, attend(): pl.pallas_call(attend_kernel, out_shape=jax.ShapeDtypeStruct((count, rows...  10.2 us
    ppermute x6, waiting for transfers between devices, send(): lax.ppermute(array, axis, [(i, (i + step) % RING) for i in range(RING)])  9.96 us
  transfers between devices with their start and end apart: 31, of which 17 were waited for; matrix products, arithmetic and copies ran while one was open for 8% of the time, Pallas kernels for 2%

profile of v1, /device:TPU:0, one launch (start us, length us, event | category | flops | bytes accessed | tf_op | source)
XLA Modules:
  0.0 321.5 jit_solution(5812895483919926491)
XLA Ops:
  4.1 2.3 pack.1
  7.3 8.1 %all-to-all-start = ((bf16[16,48,640]{2,1,0:T(8,128)(2,1)}), bf16[16,48,640]{2,1,0:T(8,128)(2,1)S(1)}, u32[]{:S(2)}, u32[]{:S(2)}) async-start(bf16[16,48,640]{2,1,0:T(8,128)(2,1)} %copy-done.11), calls=%async_computation | async-start | bytes 1966080 | tf_op jit(solution)/shard_map/all_to_all | solution.py:272
  15.4 14.8 %copy.97.refs_2_.refs_3_.refs_4_.refs_5_.refs_6_.refs_7_.refs_8_.refs_9_.refs_12_.refs_13_.refs_14_.refs_15_.refs_16_.refs_17_.refs_18_.refs_19_ = bf16[128,64,576]{2,1,0:T(8,128)(2,1)} copy(bf16[128,64,576]{0,2,1:T(8,128)(2,1)} %param.15) | data formatting | bytes 18874368 | tf_op args[1]
  30.2 2.1 all-to-all-done.refs_1_.refs_11_
  33.1 2.4 plan.1
  35.5 4.0 %copy-done.2 = bf16[128,64,576]{2,1,0:T(8,128)(2,1)S(1)} copy-done((bf16[128,64,576]{2,1,0:T(8,128)(2,1)S(1)}, bf16[128,64,576]{2,1,0:T(8,128)(2,1)}, u32[]{:S(2)}) %copy-start.2) | copy-done | bytes 9437208
  42.6 10.2 %attend.1 = bf16[16,48,512]{2,1,0:T(8,128)(2,1)S(1)} custom-call(s32[16]{0:T(128)S(1)} %copy-done.15, s32[128]{0:T(128)S(1)} %copy-done.16, s32[16]{0:T(128)S(1)} %copy-done.17, bf16[16,48,576]{2,1,0:T(8,128)(2,1)S(1)} %bitcast.45, bf16[16,48,640]{2,1,0:T(8,128)(2,1)S(1)} %all-to-all-done.refs_1_.refs_11_, bf16[128,64,576]{2,1,0:T(8,128)(2,1)S(1)} %copy-done.2, ...), custom_call_target="tpu_custom_call" | custom-call | flops 855638016 | bytes 12000000 | tf_op jit(solution)/shard_map/attend/pallas_call | solution.py:196
  54.5 2.0 collective-permute-start.1
  56.5 1.5 collective-permute-start
  58.0 1.5 collective-permute-start.8
  59.4 2.7 collective-permute-start.7
  63.4 2.0 copy-done.3
  65.4 2.0 copy-done.5
  67.4 2.0 copy-done.7
  69.5 3.6 %cut_weights.3 = (bf16[3584,512]{1,0:T(8,128)(2,1)}, bf16[256,3584]{1,0:T(8,128)(2,1)}) custom-call(s32[4]{0:T(128)S(1)} %get-tuple-element.72.spot_ref, bf16[1,7168,256]{2,1,0:T(8,128)(2,1)S(1)} %copy-done.3, bf16[1,7168,256]{2,1,0:T(8,128)(2,1)S(1)} %copy-done.5, bf16[1,256,7168]{2,1,0:T(8,128)(2,1)S(1)} %copy-done.7), custom_call_target="tpu_custom_call" | custom-call | bytes 11000000 | tf_op jit(solution)/shard_map/cut_weights/pallas_call | solution.py:228
  73.1 1.5 collective-permute-start.6
  76.3 1.8 collective-permute-start.3
  79.6 16.2 %collective-permute-done.5 = bf16[192,1024]{1,0:T(8,128)(2,1)S(1)} collective-permute-done((bf16[192,1024]{1,0:T(8,128)(2,1)S(1)}, bf16[192,1024]{1,0:T(8,128)(2,1)S(1)}, u32[]{:S(2)}, u32[]{:S(2)}) %collective-permute-start.5) | collective-permute-done | bytes 393248 | tf_op jit(solution)/shard_map/ppermute | solution.py:27
  96.9 2.9 collective-permute-start.9
  100.2 7.9 %collective-permute-done.10 = bf16[192,1024]{1,0:T(8,128)(2,1)S(1)} collective-permute-done((bf16[192,1024]{1,0:T(8,128)(2,1)S(1)}, bf16[192,1024]{1,0:T(8,128)(2,1)S(1)}, u32[]{:S(2)}, u32[]{:S(2)}) %collective-permute-start.10) | collective-permute-done | bytes 393248 | tf_op jit(solution)/shard_map/ppermute | solution.py:27
  108.6 5.3 %collective-permute-done.9 = bf16[192,1024]{1,0:T(8,128)(2,1)S(1)} collective-permute-done((bf16[192,1024]{1,0:T(8,128)(2,1)S(1)}, bf16[192,1024]{1,0:T(8,128)(2,1)S(1)}, u32[]{:S(2)}, u32[]{:S(2)}) %collective-permute-start.9) | collective-permute-done | bytes 393248 | tf_op jit(solution)/shard_map/ppermute | solution.py:27
  119.0 2.8 collective-permute-start.15
  121.8 2.3 collective-permute-start.13
  124.5 5.9 %collective-permute-done.14 = bf16[96,448]{0,1:T(8,128)(2,1)S(1)} collective-permute-done((bf16[96,448]{0,1:T(8,128)(2,1)S(1)}, bf16[96,448]{0,1:T(8,128)(2,1)S(1)}, u32[]{:S(2)}, u32[]{:S(2)}) %collective-permute-start.14) | collective-permute-done | bytes 86048 | tf_op jit(solution)/shard_map/ppermute | solution.py:31
  131.2 3.3 %collective-permute-start.17 = (bf16[48,448]{0,1:T(8,128)(2,1)S(1)}, bf16[48,448]{0,1:T(8,128)(2,1)S(1)}, u32[]{:S(2)}, u32[]{:S(2)}) collective-permute-start(bf16[48,448]{0,1:T(8,128)(2,1)S(1)} %get-tuple-element.65), channel_id=1, source_target_pairs={{0,8},{1,24},{2,40},{3,56},{4,72},{5,88},{6,104},{7,120},{8,0},{9,... | collective-permute-start | bytes 129032 | tf_op jit(solution)/shard_map/ppermute | solution.py:344
  134.9 2.0 copy-done.4
  136.9 2.0 copy-done.6
  139.0 2.0 copy-done.8
  141.0 1.4 cut_weights.2
  142.4 1.8 copy-done.18
  145.4 7.0 %collective-permute-start.20 = (bf16[48,896]{1,0:T(8,128)(2,1)S(1)}, bf16[48,896]{1,0:T(8,128)(2,1)S(1)}, u32[]{:S(2)}, u32[]{:S(2)}) collective-permute-start(bf16[48,896]{1,0:T(8,128)(2,1)S(1)} %add_convert_fusion.1), channel_id=1, source_target_pairs={{2,0},{4,2},{6,4},{0,6},{3,1},{5,3},{7,5},{1,7},{10,8},{12,10},{14... | collective-permute-start | bytes 258056 | tf_op jit(solution)/shard_map/ppermute | solution.py:27
  152.8 1.3 collective-permute-start.22
  154.8 4.5 %collective-permute-done.21 = bf16[48,896]{1,0:T(8,128)(2,1)S(1)} collective-permute-done((bf16[48,896]{1,0:T(8,128)(2,1)S(1)}, bf16[48,896]{1,0:T(8,128)(2,1)S(1)}, u32[]{:S(2)}, u32[]{:S(2)}) %collective-permute-start.21) | collective-permute-done | bytes 86048 | tf_op jit(solution)/shard_map/ppermute | solution.py:27
  162.2 3.1 convolution_convert_fusion
  165.3 4.9 %all-to-all-start.1 = ((bf16[16,32,3584]{2,1,0:T(8,128)(2,1)}), bf16[16,32,3584]{2,1,0:T(8,128)(2,1)}, u32[]{:S(2)}, u32[]{:S(2)}) async-start(bf16[16,32,3584]{2,1,0:T(8,128)(2,1)} %bitcast.49), calls=%async_computation.1 | async-start | bytes 7340032 | tf_op jit(solution)/shard_map/all_to_all | solution.py:384
  171.1 49.5 %all-to-all-done.1 = bf16[16,32,3584]{2,1,0:T(8,128)(2,1)} async-done(((bf16[16,32,3584]{2,1,0:T(8,128)(2,1)}), bf16[16,32,3584]{2,1,0:T(8,128)(2,1)}, u32[]{:S(2)}, u32[]{:S(2)}) %all-to-all-start.1) | async-done | bytes 3670048 | tf_op jit(solution)/shard_map/all_to_all | solution.py:384
  220.5 6.4 %fusion.73 = (bf16[512,512]{0,1:T(8,128)(2,1)S(1)}, f32[512,512]{0,1:T(8,128)}) fusion(bf16[512,3584]{1,0:T(8,128)(2,1)} %bitcast.11, bf16[3584,512]{1,0:T(8,128)(2,1)} %collective-permute-done.18), kind=kOutput, calls=%fused_computation.169 | convolution fusion | flops 1879310336 | bytes 8912896 | tf_op jit(solution)/shard_map/dot_general | solution.py:389
  226.9 5.2 %fusion.72 = (bf16[512,512]{0,1:T(8,128)(2,1)S(1)}, f32[512,512]{0,1:T(8,128)}) fusion(bf16[512,3584]{1,0:T(8,128)(2,1)} %bitcast.11, bf16[3584,512]{1,0:T(8,128)(2,1)S(1)} %copy-done.19), kind=kOutput, calls=%fused_computation.168 | convolution fusion | flops 1879310336 | bytes 8912896 | tf_op jit(solution)/shard_map/dot_general | solution.py:388
  233.9 2.3 collective-permute-done.24
  236.2 1.5 convert_element_type.158
  238.5 2.6 fusion.74
  241.2 3.0 add_convert_fusion
  244.2 12.5 %all-to-all-start.2 = ((bf16[16,32,3584]{2,1,0:T(8,128)(2,1)}), bf16[16,32,3584]{2,1,0:T(8,128)(2,1)}, u32[]{:S(2)}, u32[]{:S(2)}) async-start(bf16[16,32,3584]{2,1,0:T(8,128)(2,1)} %bitcast.48), calls=%async_computation.2 | async-start | bytes 7340032 | tf_op jit(solution)/shard_map/all_to_all | solution.py:399
  257.0 52.9 %all-to-all-done.2 = bf16[16,32,3584]{2,1,0:T(8,128)(2,1)} async-done(((bf16[16,32,3584]{2,1,0:T(8,128)(2,1)}), bf16[16,32,3584]{2,1,0:T(8,128)(2,1)}, u32[]{:S(2)}, u32[]{:S(2)}) %all-to-all-start.2) | async-done | bytes 3670048 | tf_op jit(solution)/shard_map/all_to_all | solution.py:399
  309.9 2.8 fusion.36
  314.9 1.4 collective-permute-start.25
  318.0 1.5 collective-permute-done.26
  319.5 1.4 collective-permute-done.25
  (179 shorter events, 36.3 us)
Async XLA Ops:
  0.6 52.1 %copy-start = (bf16[16,512,128]{2,1,0:T(8,128)(2,1)S(1)}, bf16[16,512,128]{2,1,0:T(8,128)(2,1)}, u32[]{:S(2)}) copy-start(bf16[16,512,128]{2,1,0:T(8,128)(2,1)} %param.19) | copy-start | bytes 6291460
  1.6 5.7 %copy-start.12 = (s32[16,8]{1,0:T(8,128)}, s32[16,8]{1,0:T(8,128)S(1)}, u32[]{:S(2)}) copy-start(s32[16,8]{1,0:T(8,128)S(1)} %copy.94.page_ref) | copy-start | bytes 1540
  7.3 25.0 %all-to-all-start = ((bf16[16,48,640]{2,1,0:T(8,128)(2,1)}), bf16[16,48,640]{2,1,0:T(8,128)(2,1)S(1)}, u32[]{:S(2)}, u32[]{:S(2)}) async-start(bf16[16,48,640]{2,1,0:T(8,128)(2,1)} %copy-done.11), calls=%async_computation | async-start | bytes 1966080 | tf_op jit(solution)/shard_map/all_to_all | solution.py:272
  35.5 4.0 %copy-start.2 = (bf16[128,64,576]{2,1,0:T(8,128)(2,1)S(1)}, bf16[128,64,576]{2,1,0:T(8,128)(2,1)}, u32[]{:S(2)}) copy-start(bf16[128,64,576]{2,1,0:T(8,128)(2,1)} %copy.97.refs_2_.refs_3_.refs_4_.refs_5_.refs_6_.refs_7_.refs_8_.refs_9_.refs_12_.refs_13_.refs_14_.refs_15_.refs_16_.refs_17_.refs_18_.refs_19_) | copy-start | bytes 28311556
  53.9 19.2 %collective-permute-start.2 = (bf16[48,1024]{1,0:T(8,128)(2,1)S(1)}, bf16[48,1024]{1,0:T(8,128)(2,1)S(1)}, u32[]{:S(2)}, u32[]{:S(2)}) collective-permute-start(bf16[48,1024]{1,0:T(8,128)(2,1)S(1)} %get-tuple-element.63), channel_id=1, source_target_pairs={{24,0},{0,8},{8,16},{16,24},{25,1},{1,9},{9,17},{17,25},{26,2},{2,... | collective-permute-start | bytes 294920 | tf_op jit(solution)/shard_map/ppermute | solution.py:27
  54.5 20.1 %collective-permute-start.1 = (bf16[48,1024]{1,0:T(8,128)(2,1)S(1)}, bf16[48,1024]{1,0:T(8,128)(2,1)S(1)}, u32[]{:S(2)}, u32[]{:S(2)}) collective-permute-start(bf16[48,1024]{1,0:T(8,128)(2,1)S(1)} %get-tuple-element.63), channel_id=1, source_target_pairs={{16,0},{24,8},{0,16},{8,24},{17,1},{25,9},{1,17},{9,25},{18,2},{26... | collective-permute-start | bytes 294920 | tf_op jit(solution)/shard_map/ppermute | solution.py:27
  56.5 18.1 %collective-permute-start = (bf16[48,1024]{1,0:T(8,128)(2,1)S(1)}, bf16[48,1024]{1,0:T(8,128)(2,1)S(1)}, u32[]{:S(2)}, u32[]{:S(2)}) collective-permute-start(bf16[48,1024]{1,0:T(8,128)(2,1)S(1)} %get-tuple-element.63), channel_id=1, source_target_pairs={{8,0},{16,8},{24,16},{0,24},{9,1},{17,9},{25,17},{1,25},{10,2},{18... | collective-permute-start | bytes 294920 | tf_op jit(solution)/shard_map/ppermute | solution.py:27
  58.0 17.3 %collective-permute-start.8 = (bf16[48,1024]{1,0:T(8,128)(2,1)S(1)}, bf16[48,1024]{1,0:T(8,128)(2,1)S(1)}, u32[]{:S(2)}, u32[]{:S(2)}) collective-permute-start(bf16[48,1024]{1,0:T(8,128)(2,1)S(1)} %get-tuple-element.62), channel_id=1, source_target_pairs={{96,0},{0,32},{32,64},{64,96},{97,1},{1,33},{33,65},{65,97},{98,2}... | collective-permute-start | bytes 294920 | tf_op jit(solution)/shard_map/ppermute | solution.py:27
  59.4 16.8 %collective-permute-start.7 = (bf16[48,1024]{1,0:T(8,128)(2,1)S(1)}, bf16[48,1024]{1,0:T(8,128)(2,1)S(1)}, u32[]{:S(2)}, u32[]{:S(2)}) collective-permute-start(bf16[48,1024]{1,0:T(8,128)(2,1)S(1)} %get-tuple-element.62), channel_id=1, source_target_pairs={{64,0},{96,32},{0,64},{32,96},{65,1},{97,33},{1,65},{33,97},{66,2}... | collective-permute-start | bytes 294920 | tf_op jit(solution)/shard_map/ppermute | solution.py:27
  63.4 2.0 copy-start.3
  65.4 2.0 copy-start.5
  67.4 2.0 copy-start.7
  69.5 9.2 %copy-start.28 = (bf16[2048,448]{0,1:T(8,128)(2,1)S(1)}, bf16[2048,448]{0,1:T(8,128)(2,1)}, u32[]{:S(2)}) copy-start(bf16[2048,448]{0,1:T(8,128)(2,1)} %param.20) | copy-start | bytes 5505028
  73.1 4.9 %collective-permute-start.6 = (bf16[48,1024]{1,0:T(8,128)(2,1)S(1)}, bf16[48,1024]{1,0:T(8,128)(2,1)S(1)}, u32[]{:S(2)}, u32[]{:S(2)}) collective-permute-start(bf16[48,1024]{1,0:T(8,128)(2,1)S(1)} %get-tuple-element.62), channel_id=1, source_target_pairs={{32,0},{64,32},{96,64},{0,96},{33,1},{65,33},{97,65},{1,97},{34,2}... | collective-permute-start | bytes 294920 | tf_op jit(solution)/shard_map/ppermute | solution.py:27
  74.6 70.8 %collective-permute-start.18 = (bf16[3584,512]{1,0:T(8,128)(2,1)}, bf16[3584,512]{1,0:T(8,128)(2,1)}, u32[]{:S(2)}, u32[]{:S(2)}) collective-permute-start(bf16[3584,512]{1,0:T(8,128)(2,1)} %get-tuple-element.28), channel_id=1, source_target_pairs={{0,1},{1,0},{2,3},{3,2},{4,5},{5,4},{6,7},{7,6},{8,9},{9,8},{10,11... | collective-permute-start | bytes 11010056 | tf_op jit(solution)/shard_map/ppermute | solution.py:35
  74.6 21.2 %collective-permute-start.5 = (bf16[192,1024]{1,0:T(8,128)(2,1)S(1)}, bf16[192,1024]{1,0:T(8,128)(2,1)S(1)}, u32[]{:S(2)}, u32[]{:S(2)}) collective-permute-start(bf16[192,1024]{1,0:T(8,128)(2,1)S(1)} %pad_maximum_fusion.2), channel_id=1, source_target_pairs={{96,0},{0,32},{32,64},{64,96},{97,1},{1,33},{33,65},{65,97},{98,2}... | collective-permute-start | bytes 1179656 | tf_op jit(solution)/shard_map/ppermute | solution.py:27
  75.3 39.4 %collective-permute-start.4 = (bf16[192,1024]{1,0:T(8,128)(2,1)S(1)}, bf16[192,1024]{1,0:T(8,128)(2,1)S(1)}, u32[]{:S(2)}, u32[]{:S(2)}) collective-permute-start(bf16[192,1024]{1,0:T(8,128)(2,1)S(1)} %pad_maximum_fusion.2), channel_id=1, source_target_pairs={{64,0},{96,32},{0,64},{32,96},{65,1},{97,33},{1,65},{33,97},{66,2}... | collective-permute-start | bytes 1179656 | tf_op jit(solution)/shard_map/ppermute | solution.py:27
  76.3 38.9 %collective-permute-start.3 = (bf16[192,1024]{1,0:T(8,128)(2,1)S(1)}, bf16[192,1024]{1,0:T(8,128)(2,1)S(1)}, u32[]{:S(2)}, u32[]{:S(2)}) collective-permute-start(bf16[192,1024]{1,0:T(8,128)(2,1)S(1)} %pad_maximum_fusion.2), channel_id=1, source_target_pairs={{32,0},{64,32},{96,64},{0,96},{33,1},{65,33},{97,65},{1,97},{34,2}... | collective-permute-start | bytes 1179656 | tf_op jit(solution)/shard_map/ppermute | solution.py:27
  78.1 18.8 %collective-permute-start.11 = (bf16[192,1024]{1,0:T(8,128)(2,1)S(1)}, bf16[192,1024]{1,0:T(8,128)(2,1)S(1)}, u32[]{:S(2)}, u32[]{:S(2)}) collective-permute-start(bf16[192,1024]{1,0:T(8,128)(2,1)S(1)} %pad_maximum_fusion.3), channel_id=1, source_target_pairs={{24,0},{0,8},{8,16},{16,24},{25,1},{1,9},{9,17},{17,25},{26,2},{2,... | collective-permute-start | bytes 1179656 | tf_op jit(solution)/shard_map/ppermute | solution.py:27
  95.8 12.2 %collective-permute-start.10 = (bf16[192,1024]{1,0:T(8,128)(2,1)S(1)}, bf16[192,1024]{1,0:T(8,128)(2,1)S(1)}, u32[]{:S(2)}, u32[]{:S(2)}) collective-permute-start(bf16[192,1024]{1,0:T(8,128)(2,1)S(1)} %pad_maximum_fusion.3), channel_id=1, source_target_pairs={{16,0},{24,8},{0,16},{8,24},{17,1},{25,9},{1,17},{9,25},{18,2},{26... | collective-permute-start | bytes 1179656 | tf_op jit(solution)/shard_map/ppermute | solution.py:27
  96.9 17.0 %collective-permute-start.9 = (bf16[192,1024]{1,0:T(8,128)(2,1)S(1)}, bf16[192,1024]{1,0:T(8,128)(2,1)S(1)}, u32[]{:S(2)}, u32[]{:S(2)}) collective-permute-start(bf16[192,1024]{1,0:T(8,128)(2,1)S(1)} %pad_maximum_fusion.3), channel_id=1, source_target_pairs={{8,0},{16,8},{24,16},{0,24},{9,1},{17,9},{25,17},{1,25},{10,2},{18... | collective-permute-start | bytes 1179656 | tf_op jit(solution)/shard_map/ppermute | solution.py:27
  117.0 1.7 collective-permute-start.12
  117.1 28.4 %collective-permute-start.19 = (bf16[256,3584]{1,0:T(8,128)(2,1)}, bf16[256,3584]{1,0:T(8,128)(2,1)}, u32[]{:S(2)}, u32[]{:S(2)}) collective-permute-start(bf16[256,3584]{1,0:T(8,128)(2,1)} %get-tuple-element.30), channel_id=1, source_target_pairs={{0,1},{1,0},{2,3},{3,2},{4,5},{5,4},{6,7},{7,6},{8,9},{9,8},{10,11... | collective-permute-start | bytes 5505032 | tf_op jit(solution)/shard_map/ppermute | solution.py:35
  117.7 17.1 %copy-start.25 = (f32[7168]{0:T(1024)S(1)}, f32[7168]{0:T(1024)}, u32[]{:S(2)}) copy-start(f32[7168]{0:T(1024)} %param.22) | copy-start | bytes 86020
  119.0 5.5 %collective-permute-start.15 = (bf16[96,448]{0,1:T(8,128)(2,1)S(1)}, bf16[96,448]{0,1:T(8,128)(2,1)S(1)}, u32[]{:S(2)}, u32[]{:S(2)}) collective-permute-start(bf16[96,448]{0,1:T(8,128)(2,1)S(1)} %get-tuple-element.56), channel_id=1, source_target_pairs={{0,6},{2,0},{4,2},{6,4},{1,7},{3,1},{5,3},{7,5},{8,14},{10,8},{12,... | collective-permute-start | bytes 258056 | tf_op jit(solution)/shard_map/ppermute | solution.py:31
  121.8 8.6 %collective-permute-start.14 = (bf16[96,448]{0,1:T(8,128)(2,1)S(1)}, bf16[96,448]{0,1:T(8,128)(2,1)S(1)}, u32[]{:S(2)}, u32[]{:S(2)}) collective-permute-start(bf16[96,448]{0,1:T(8,128)(2,1)S(1)} %get-tuple-element.57), channel_id=1, source_target_pairs={{0,2},{2,4},{4,6},{6,0},{1,3},{3,5},{5,7},{7,1},{8,10},{10,12},{12... | collective-permute-start | bytes 258056 | tf_op jit(solution)/shard_map/ppermute | solution.py:31
  121.8 8.6 %collective-permute-start.13 = (bf16[96,448]{0,1:T(8,128)(2,1)S(1)}, bf16[96,448]{0,1:T(8,128)(2,1)S(1)}, u32[]{:S(2)}, u32[]{:S(2)}) collective-permute-start(bf16[96,448]{0,1:T(8,128)(2,1)S(1)} %get-tuple-element.55), channel_id=1, source_target_pairs={{0,4},{2,6},{4,0},{6,2},{1,5},{3,7},{5,1},{7,3},{8,12},{10,14},{12... | collective-permute-start | bytes 258056 | tf_op jit(solution)/shard_map/ppermute | solution.py:31
  130.5 13.6 %collective-permute-start.16 = (bf16[48,448]{0,1:T(8,128)(2,1)S(1)}, bf16[48,448]{0,1:T(8,128)(2,1)S(1)}, u32[]{:S(2)}, u32[]{:S(2)}) collective-permute-start(bf16[48,448]{0,1:T(8,128)(2,1)S(1)} %get-tuple-element.64), channel_id=1, source_target_pairs={{0,0},{1,16},{2,32},{3,48},{4,64},{5,80},{6,96},{7,112},{8,8},{9,2... | collective-permute-start | bytes 129032 | tf_op jit(solution)/shard_map/ppermute | solution.py:344
  131.2 13.0 %collective-permute-start.17 = (bf16[48,448]{0,1:T(8,128)(2,1)S(1)}, bf16[48,448]{0,1:T(8,128)(2,1)S(1)}, u32[]{:S(2)}, u32[]{:S(2)}) collective-permute-start(bf16[48,448]{0,1:T(8,128)(2,1)S(1)} %get-tuple-element.65), channel_id=1, source_target_pairs={{0,8},{1,24},{2,40},{3,56},{4,72},{5,88},{6,104},{7,120},{8,0},{9,... | collective-permute-start | bytes 129032 | tf_op jit(solution)/shard_map/ppermute | solution.py:344
  134.9 2.0 copy-start.4
  145.4 9.4 %collective-permute-start.20 = (bf16[48,896]{1,0:T(8,128)(2,1)S(1)}, bf16[48,896]{1,0:T(8,128)(2,1)S(1)}, u32[]{:S(2)}, u32[]{:S(2)}) collective-permute-start(bf16[48,896]{1,0:T(8,128)(2,1)S(1)} %add_convert_fusion.1), channel_id=1, source_target_pairs={{2,0},{4,2},{6,4},{0,6},{3,1},{5,3},{7,5},{1,7},{10,8},{12,10},{14... | collective-permute-start | bytes 258056 | tf_op jit(solution)/shard_map/ppermute | solution.py:27
  152.5 6.8 %collective-permute-start.21 = (bf16[48,896]{1,0:T(8,128)(2,1)S(1)}, bf16[48,896]{1,0:T(8,128)(2,1)S(1)}, u32[]{:S(2)}, u32[]{:S(2)}) collective-permute-start(bf16[48,896]{1,0:T(8,128)(2,1)S(1)} %add_convert_fusion.1), channel_id=1, source_target_pairs={{4,0},{6,2},{0,4},{2,6},{5,1},{7,3},{1,5},{3,7},{12,8},{14,10},{8,... | collective-permute-start | bytes 258056 | tf_op jit(solution)/shard_map/ppermute | solution.py:27
  152.8 7.5 %collective-permute-start.22 = (bf16[48,896]{1,0:T(8,128)(2,1)S(1)}, bf16[48,896]{1,0:T(8,128)(2,1)S(1)}, u32[]{:S(2)}, u32[]{:S(2)}) collective-permute-start(bf16[48,896]{1,0:T(8,128)(2,1)S(1)} %add_convert_fusion.1), channel_id=1, source_target_pairs={{6,0},{0,2},{2,4},{4,6},{7,1},{1,3},{3,5},{5,7},{14,8},{8,10},{10,... | collective-permute-start | bytes 258056 | tf_op jit(solution)/shard_map/ppermute | solution.py:27
  160.3 1.7 collective-permute-start.23
  165.3 5.0 %copy-start.27 = (f32[48,8]{0,1:T(8,128)S(1)}, f32[48,8]{0,1:T(8,128)}, u32[]{:S(2)}) copy-start(f32[48,8]{0,1:T(8,128)} %param.24) | copy-start | bytes 4612
  165.3 55.3 %all-to-all-start.1 = ((bf16[16,32,3584]{2,1,0:T(8,128)(2,1)}), bf16[16,32,3584]{2,1,0:T(8,128)(2,1)}, u32[]{:S(2)}, u32[]{:S(2)}) async-start(bf16[16,32,3584]{2,1,0:T(8,128)(2,1)} %bitcast.49), calls=%async_computation.1 | async-start | bytes 7340032 | tf_op jit(solution)/shard_map/all_to_all | solution.py:384
  220.5 6.4 %copy-start.19 = (bf16[3584,512]{1,0:T(8,128)(2,1)S(1)}, bf16[3584,512]{1,0:T(8,128)(2,1)}, u32[]{:S(2)}) copy-start(bf16[3584,512]{1,0:T(8,128)(2,1)} %copy-done.18) | copy-start | bytes 11010052
  233.2 3.0 collective-permute-start.24
  233.9 3.8 %copy-start.20 = (f32[512,512]{0,1:T(8,128)S(1)}, f32[512,512]{0,1:T(8,128)}, u32[]{:S(2)}) copy-start(f32[512,512]{0,1:T(8,128)} %get-tuple-element.71) | copy-start | bytes 3145732
  233.9 3.8 %copy-start.21 = (f32[512,512]{0,1:T(8,128)S(1)}, f32[512,512]{0,1:T(8,128)}, u32[]{:S(2)}) copy-start(f32[512,512]{0,1:T(8,128)} %get-tuple-element.69) | copy-start | bytes 3145732
  244.2 65.7 %all-to-all-start.2 = ((bf16[16,32,3584]{2,1,0:T(8,128)(2,1)}), bf16[16,32,3584]{2,1,0:T(8,128)(2,1)}, u32[]{:S(2)}, u32[]{:S(2)}) async-start(bf16[16,32,3584]{2,1,0:T(8,128)(2,1)} %bitcast.48), calls=%async_computation.2 | async-start | bytes 7340032 | tf_op jit(solution)/shard_map/all_to_all | solution.py:399
  256.7 53.2 %copy-start.24 = (bf16[48,512]{1,0:T(8,128)(2,1)S(1)}, bf16[48,512]{1,0:T(8,128)(2,1)}, u32[]{:S(2)}) copy-start(bf16[48,512]{1,0:T(8,128)(2,1)} %get-tuple-element.61) | copy-start | bytes 147460
  257.0 52.9 %copy-start.22 = (bf16[48,14336]{1,0:T(8,128)(2,1)}, bf16[48,14336]{1,0:T(8,128)(2,1)S(1)}, u32[]{:S(2)}) copy-start(bf16[48,14336]{1,0:T(8,128)(2,1)S(1)} %slice_dynamic-update-slice_fusion.1) | copy-start | bytes 4128772
  312.6 3.6 %copy-start.23 = (bf16[48,14336]{1,0:T(8,128)(2,1)S(1)}, bf16[48,14336]{1,0:T(8,128)(2,1)}, u32[]{:S(2)}) copy-start(bf16[48,14336]{1,0:T(8,128)(2,1)} %copy-done.22) | copy-start | bytes 4128772
  312.6 8.9 %copy-start.1 = (bf16[16,512,128]{2,1,0:T(8,128)(2,1)S(1)}, bf16[16,512,128]{2,1,0:T(8,128)(2,1)}, u32[]{:S(2)}) copy-start(bf16[16,512,128]{2,1,0:T(8,128)(2,1)} %param.19) | copy-start | bytes 6291460
  312.8 5.2 %collective-permute-start.27 = (bf16[48,896]{1,0:T(8,128)(2,1)S(1)}, bf16[48,896]{1,0:T(8,128)(2,1)S(1)}, u32[]{:S(2)}, u32[]{:S(2)}) collective-permute-start(bf16[48,896]{1,0:T(8,128)(2,1)S(1)} %get-tuple-element.53), channel_id=1, source_target_pairs={{0,6},{2,0},{4,2},{6,4},{1,7},{3,1},{5,3},{7,5},{8,14},{10,8},{12,... | collective-permute-start | bytes 258056 | tf_op jit(solution)/shard_map/ppermute | solution.py:31
  313.7 5.8 %collective-permute-start.26 = (bf16[48,896]{1,0:T(8,128)(2,1)S(1)}, bf16[48,896]{1,0:T(8,128)(2,1)S(1)}, u32[]{:S(2)}, u32[]{:S(2)}) collective-permute-start(bf16[48,896]{1,0:T(8,128)(2,1)S(1)} %get-tuple-element.54), channel_id=1, source_target_pairs={{0,2},{2,4},{4,6},{6,0},{1,3},{3,5},{5,7},{7,1},{8,10},{10,12},{12... | collective-permute-start | bytes 258056 | tf_op jit(solution)/shard_map/ppermute | solution.py:31
  314.9 6.0 %collective-permute-start.25 = (bf16[48,896]{1,0:T(8,128)(2,1)S(1)}, bf16[48,896]{1,0:T(8,128)(2,1)S(1)}, u32[]{:S(2)}, u32[]{:S(2)}) collective-permute-start(bf16[48,896]{1,0:T(8,128)(2,1)S(1)} %get-tuple-element.52), channel_id=1, source_target_pairs={{0,4},{2,6},{4,0},{6,2},{1,5},{3,7},{5,1},{7,3},{8,12},{10,14},{12... | collective-permute-start | bytes 258056 | tf_op jit(solution)/shard_map/ppermute | solution.py:31
  (12 other events, 14.1 us)

commit v2 on v1

--- a/solution.py
+++ b/solution.py
@@ -203,39 +203,6 @@
         ),
         name="attend",
     )(pick, pages, seen, *group, *group)
-
-
-def cut_kernel(spot_ref, gate_ref, up_ref, down_ref, rows_ref, cols_ref):
-    units = gate_ref.shape[2]
-    rows_ref[:, :units] = gate_ref[0]
-    rows_ref[:, units:] = up_ref[0]
-    cols_ref[...] = down_ref[0]
-
-
-def cut_weights(spots, w_gate, w_up, w_down):
-    units, model = w_down.shape[1:]
-    wide = model // HEAD_N
-    rows = pl.BlockSpec((1, wide, units), lambda i, spot: (0, spot[i], 0))
-    spec = pltpu.PrefetchScalarGridSpec(
-        num_scalar_prefetch=1,
-        grid=(RING,),
-        in_specs=[rows, rows, pl.BlockSpec((1, units, wide), lambda i, spot: (0, 0, spot[i]))],
-        out_specs=[
-            pl.BlockSpec((wide, 2 * units), lambda i, spot: (i, 0)),
-            pl.BlockSpec((units, wide), lambda i, spot: (0, i)),
-        ],
-    )
-    return pl.pallas_call(
-        cut_kernel,
-        out_shape=[
-            jax.ShapeDtypeStruct((model // 2, 2 * units), bf16),
-            jax.ShapeDtypeStruct((units, model // 2), bf16),
-        ],
-        grid_spec=spec,
-        compiler_params=pltpu.CompilerParams(vmem_limit_bytes=32 * 2**20),
-        cost_estimate=pl.CostEstimate(flops=0, bytes_accessed=11_000_000, transcendentals=0),
-        name="cut_weights",
-    )(spots, w_gate, w_up, w_down)
 
 
 def before(count):
@@ -284,12 +251,6 @@
     ).astype(bf16)
     values = values.reshape(tokens, head_group * w_uv.shape[2])
 
-    values, w_gate, w_up, w_down = lax.optimization_barrier((values, w_gate, w_up, w_down))
-    ring_at = (at_x + jnp.arange(RING, dtype=i32)) % RING * 2
-    in_give, out_give = cut_weights(ring_at + 1 - at_core, w_gate, w_up, w_down)
-    in_own, out_own = cut_weights(ring_at + at_core, w_gate, w_up, w_down)
-    in_other, out_other = other_core(in_give), other_core(out_give)
-
     half = values.shape[1] // 2
 
     def spread(block, first, second):
@@ -349,9 +310,6 @@
     head_index = at_x * 2 + at_core
     near = lax.dynamic_slice_in_dim(residual, head_index * wide_piece, wide_piece, 1)
     piece = (near.astype(f32) + attention.astype(f32)).astype(bf16)
-    piece, in_own, in_other, out_own, out_other = lax.optimization_barrier(
-        (piece, in_own, in_other, out_own, out_other)
-    )
 
     here = jnp.concatenate([piece] + [hop(piece, "x", k) for k in (1, 2, 3)], axis=1)
     there = other_core(here)
@@ -380,35 +338,94 @@
     ranks = jnp.arange(CAP, dtype=i32)
     placing = (rank.T[:, None, :] == ranks[None, :, None]).astype(bf16)
     placing = placing.reshape(DP_N * CAP, tokens)
-    outgoing = jnp.dot(placing, normed, preferred_element_type=f32).astype(bf16)
-    rows = lax.all_to_all(outgoing.reshape(DP_N, CAP, -1), DP, 0, 0, tiled=True)
-    rows = rows.reshape(DP_N * CAP, -1)
+
+    cut = 3 * wide_piece // 7
+    early = normed[:, :cut]
+    doubled = [normed[:, k * wide_piece + cut : (k + 1) * wide_piece] for k in range(RING)]
+    rest = wide_piece - cut
+    back = (RING - at_x) % RING
+    late = lax.dynamic_slice_in_dim(
+        jnp.concatenate(doubled + doubled, axis=1), back * rest, RING * rest, 1
+    )
+
+    def to_experts(block):
+        block = jnp.dot(placing, block, preferred_element_type=f32).astype(bf16)
+        block = lax.all_to_all(block.reshape(DP_N, CAP, -1), DP, 0, 0, tiled=True)
+        return block.reshape(DP_N * CAP, -1)
+
+    early = to_experts(early)
+    early, late = lax.optimization_barrier((early, late))
+    late = to_experts(late)
+    early = [early] + [hop(early, "x", k) for k in (1, 2, 3)]
+    early = lax.dynamic_slice_in_dim(
+        jnp.concatenate(early + early, axis=1), back * cut, RING * cut, 1
+    )
+
+    def in_rows(core, low, high):
+        blocks = []
+        for weights in (w_gate, w_up):
+            view = weights[0].reshape(RING, 2, wide_piece, -1)
+            view = lax.dynamic_slice_in_dim(view, core, 1, 1)[:, 0, low:high]
+            blocks.append(view.reshape(RING * (high - low), -1))
+        return jnp.concatenate(blocks, axis=1)
+
+    def out_columns(core, low, high):
+        return jnp.concatenate(
+            [
+                lax.dynamic_slice_in_dim(
+                    w_down[0], (2 * k + core) * wide_piece + low, high - low, 1
+                )
+                for k in range(RING)
+            ],
+            axis=1,
+        )
 
     units = w_gate.shape[2]
-    sums = jnp.dot(rows, in_own, preferred_element_type=f32)
-    give = jnp.dot(rows, in_other, preferred_element_type=f32)
-    swapped = other_core(jnp.concatenate([give, sums], axis=1).astype(bf16)).astype(f32)
-    own_sum = sums + swapped[:, : 2 * units]
-    other_sum = give + swapped[:, 2 * units :]
-    hidden = [jax.nn.silu(a[:, :units]) * a[:, units:] for a in (own_sum, other_sum)]
-    hidden = lax.optimization_barrier([a.astype(bf16) for a in hidden])
-    output = jnp.dot(hidden[0], out_own, preferred_element_type=f32) + jnp.dot(
-        hidden[1], out_other, preferred_element_type=f32
-    )
-    output = output.astype(bf16).reshape(DP_N, CAP, -1)
-    returned = lax.all_to_all(output, DP, 0, 0, tiled=True).reshape(DP_N * CAP, -1)
+    away = 1 - at_core
+    sums = (
+        jnp.dot(early, in_rows(at_core, 0, cut), preferred_element_type=f32)
+        + jnp.dot(other_core(early), in_rows(away, 0, cut), preferred_element_type=f32)
+        + jnp.dot(late, in_rows(at_core, cut, wide_piece), preferred_element_type=f32)
+        + jnp.dot(other_core(late), in_rows(away, cut, wide_piece), preferred_element_type=f32)
+    )
+    hidden = (jax.nn.silu(sums[:, :units]) * sums[:, units:]).astype(bf16)
+    hidden = lax.optimization_barrier(hidden)
+
+    def output(low, high):
+        give = jnp.dot(hidden, out_columns(away, low, high), preferred_element_type=f32)
+        keep = jnp.dot(hidden, out_columns(at_core, low, high), preferred_element_type=f32)
+        return keep + other_core(give.astype(bf16)).astype(f32)
+
+    def to_home(block):
+        block = lax.all_to_all(block.reshape(DP_N, CAP, -1), DP, 0, 0, tiled=True)
+        return block.reshape(DP_N * CAP, -1)
+
+    def ring_sum(block, size):
+        block = jnp.concatenate([block, block], axis=1)
+        block = lax.dynamic_slice_in_dim(block, at_x * size, RING * size, 1)
+        total = block[:, :size].astype(f32)
+        for k in (2, 1, 3):
+            total = total + send(block[:, k * size : (k + 1) * size], "x", k).astype(f32)
+        return total
+
+    late = output(cut, wide_piece).astype(bf16)
+    early, late = lax.optimization_barrier((output(0, cut).astype(bf16), late))
+    late = to_home(late)
+    early, late = lax.optimization_barrier((ring_sum(early, cut).astype(bf16), late))
+    early = to_home(early)
 
     mix = jnp.where(rank[:, :, None] == ranks[None, None, :], weight[:, :, None], 0.0)
     mix = mix.reshape(tokens, DP_N * CAP)
     coarse = lax.reduce_precision(mix, 8, 7)
     both = jnp.concatenate([coarse.astype(bf16), (mix - coarse).astype(bf16)], axis=0)
-    both = jnp.dot(both, returned, preferred_element_type=f32)
-    mixed = both[:tokens] + both[tokens:]
-    routed = mixed[:, :wide_piece]
-    for k in (2, 1, 3):
-        block = mixed[:, k * wide_piece : (k + 1) * wide_piece].astype(bf16)
-        routed = routed + send(block, "x", k).astype(f32)
-    return (attended, routed.astype(bf16))
+
+    def mixed(block):
+        block = jnp.dot(both, block, preferred_element_type=f32)
+        return block[:tokens] + block[tokens:]
+
+    late = ring_sum(mixed(late).astype(bf16), rest)
+    routed = jnp.concatenate([mixed(early), late], axis=1).astype(bf16)
+    return (attended, routed)
 
 
 def solution(mesh):

time: 327 us -> 272 us (0.83); the launches traced: 322 us -> 271 us
  waiting for transfers between devices: 155 us -> 81.3 us
  starting transfers between devices: 64.7 us -> 86.3 us
  local copies, waits for them, and re-layouts: 43.5 us -> 53.5 us
  Pallas kernels: 19.8 us -> 14.8 us
  matrix products: 28.6 us -> 25 us
    all_to_all x2 -> x4, waiting for transfers between devices: 102 us -> 23.7 us  [the longest x2 12 us: to_experts(): block = lax.all_to_all(block.reshape(DP_N, CAP, -1), DP, 0, 0, tiled=True)]
    ppermute x15 -> x18, starting transfers between devices: 25.9 us -> 38 us  [hop(): lax.ppermute(array, axis, [((i + step) % RING, i) for i in range(RING)])]
    ppermute x6 -> x9, waiting for transfers between devices: 9.96 us -> 18.9 us  [send(): lax.ppermute(array, axis, [(i, (i + step) % RING) for i in range(RING)])]
    slice x1 -> x4, local copies, waits for them, and re-layouts: 0.02 us -> 8.18 us  [the longest x2 8.04 us: in_rows(): view = lax.dynamic_slice_in_dim(view, core, 1, 1)[:, 0, low:high]]
    ppermute x6 -> x9, starting transfers between devices: 8.62 us -> 14.2 us  [send(): lax.ppermute(array, axis, [(i, (i + step) % RING) for i in range(RING)])]
    pallas_call x2 -> x0, Pallas kernels: 5.02 us -> none  [cut_weights(): pl.pallas_call(cut_kernel, out_shape=[jax.ShapeDtypeStruct((model // 2, 2...]
    dot_general x6 -> x12, matrix products: 23 us -> 18.3 us  [the longest x2 3.83 us: output(): jnp.dot(hidden, out_columns(at_core, low, high), preferred_element_type=f32)]
    ppermute x15 -> x18, waiting for transfers between devices: 35.6 us -> 31 us  [hop(): lax.ppermute(array, axis, [((i + step) % RING, i) for i in range(RING)])]
  transfers between devices with their start and end apart: 31 -> 40, of which waited for: 17 -> 22; matrix products, arithmetic and copies ran while one was open for 8% -> 21% of each run, Pallas kernels for 2% -> 0%
where the time goes in v2:
time: 272 us; the launch traced here: 271 us
  starting transfers between devices  86.3 us (32%)
  waiting for transfers between devices  81.3 us (30%)
  local copies, waits for them, and re-layouts  53.5 us (20%)
  matrix products  25 us (9%)
  Pallas kernels  14.8 us (5%)
  other arithmetic  8.48 us (3%)
    ppermute x18, starting transfers between devices, hop(): lax.ppermute(array, axis, [((i + step) % RING, i) for i in range(RING)])  38 us
    unnamed x110, local copies, waits for them, and re-layouts  36.9 us
    ppermute x18, waiting for transfers between devices, hop(): lax.ppermute(array, axis, [((i + step) % RING, i) for i in range(RING)])  31 us
    ppermute x9, waiting for transfers between devices, send(): lax.ppermute(array, axis, [(i, (i + step) % RING) for i in range(RING)])  18.9 us
    ppermute x9, starting transfers between devices, send(): lax.ppermute(array, axis, [(i, (i + step) % RING) for i in range(RING)])  14.2 us
    all_to_all x2, starting transfers between devices, to_home(): block = lax.all_to_all(block.reshape(DP_N, CAP, -1), DP, 0, 0, tiled=True)  12.3 us
    all_to_all x2, waiting for transfers between devices, to_experts(): block = lax.all_to_all(block.reshape(DP_N, CAP, -1), DP, 0, 0, tiled=True)  12 us
    all_to_all x2, waiting for transfers between devices, to_home(): block = lax.all_to_all(block.reshape(DP_N, CAP, -1), DP, 0, 0, tiled=True)  11.7 us
  transfers between devices with their start and end apart: 40, of which 22 were waited for; matrix products, arithmetic and copies ran while one was open for 21% of the time, Pallas kernels for 0%

profile of v2, /device:TPU:0, one launch (start us, length us, event | category | flops | bytes accessed | tf_op | source)
XLA Modules:
  0.0 271.1 jit_solution(4582185807276736908)
XLA Ops:
  4.1 2.3 pack.1
  7.3 8.1 %all-to-all-start = ((bf16[16,48,640]{2,1,0:T(8,128)(2,1)}), bf16[16,48,640]{2,1,0:T(8,128)(2,1)S(1)}, u32[]{:S(2)}, u32[]{:S(2)}) async-start(bf16[16,48,640]{2,1,0:T(8,128)(2,1)} %copy-done.5), calls=%async_computation | async-start | bytes 1966080 | tf_op jit(solution)/shard_map/all_to_all | solution.py:239
  15.5 14.8 %copy.97.refs_2_.refs_3_.refs_4_.refs_5_.refs_6_.refs_7_.refs_8_.refs_9_.refs_12_.refs_13_.refs_14_.refs_15_.refs_16_.refs_17_.refs_18_.refs_19_ = bf16[128,64,576]{2,1,0:T(8,128)(2,1)} copy(bf16[128,64,576]{0,2,1:T(8,128)(2,1)} %param.15) | data formatting | bytes 18874368 | tf_op args[1]
  30.2 2.1 all-to-all-done.refs_1_.refs_11_
  33.1 2.4 plan.1
  35.5 4.0 %copy-done.2 = bf16[128,64,576]{2,1,0:T(8,128)(2,1)S(1)} copy-done((bf16[128,64,576]{2,1,0:T(8,128)(2,1)S(1)}, bf16[128,64,576]{2,1,0:T(8,128)(2,1)}, u32[]{:S(2)}) %copy-start.2) | copy-done | bytes 9437208
  42.6 10.1 %attend.1 = bf16[16,48,512]{2,1,0:T(8,128)(2,1)S(1)} custom-call(s32[16]{0:T(128)S(1)} %copy-done.9, s32[128]{0:T(128)S(1)} %copy-done.10, s32[16]{0:T(128)S(1)} %copy-done.11, bf16[16,48,576]{2,1,0:T(8,128)(2,1)S(1)} %bitcast.94, bf16[16,48,640]{2,1,0:T(8,128)(2,1)S(1)} %all-to-all-done.refs_1_.refs_11_, bf16[128,64,576]{2,1,0:T(8,128)(2,1)S(1)} %copy-done.2, ...), custom_call_target="tpu_custom_call" | custom-call | flops 855638016 | bytes 12000000 | tf_op jit(solution)/shard_map/attend/pallas_call | solution.py:196
  56.7 2.7 collective-permute-start
  62.4 1.9 collective-permute-start.11
  64.3 2.3 collective-permute-start.10
  68.5 2.0 collective-permute-start.5
  70.4 2.1 collective-permute-start.4
  74.6 1.6 collective-permute-done.11
  76.2 2.8 %collective-permute-start.3 = (bf16[192,1024]{1,0:T(8,128)(2,1)S(1)}, bf16[192,1024]{1,0:T(8,128)(2,1)S(1)}, u32[]{:S(2)}, u32[]{:S(2)}) collective-permute-start(bf16[192,1024]{1,0:T(8,128)(2,1)S(1)} %pad_maximum_fusion.1), channel_id=1, source_target_pairs={{32,0},{64,32},{96,64},{0,96},{33,1},{65,33},{97,65},{1,97},{34,2}... | collective-permute-start | bytes 1179656 | tf_op jit(solution)/shard_map/ppermute | solution.py:27
  79.5 4.0 %collective-permute-done.10 = bf16[192,1024]{1,0:T(8,128)(2,1)S(1)} collective-permute-done((bf16[192,1024]{1,0:T(8,128)(2,1)S(1)}, bf16[192,1024]{1,0:T(8,128)(2,1)S(1)}, u32[]{:S(2)}, u32[]{:S(2)}) %collective-permute-start.10) | collective-permute-done | bytes 393248 | tf_op jit(solution)/shard_map/ppermute | solution.py:27
  84.3 1.7 collective-permute-done.5
  91.2 3.1 %collective-permute-start.13 = (bf16[96,448]{0,1:T(8,128)(2,1)S(1)}, bf16[96,448]{0,1:T(8,128)(2,1)S(1)}, u32[]{:S(2)}, u32[]{:S(2)}) collective-permute-start(bf16[96,448]{0,1:T(8,128)(2,1)S(1)} %get-tuple-element.59), channel_id=1, source_target_pairs={{0,4},{2,6},{4,0},{6,2},{1,5},{3,7},{5,1},{7,3},{8,12},{10,14},{12... | collective-permute-start | bytes 258056 | tf_op jit(solution)/shard_map/ppermute | solution.py:31
  94.9 2.6 collective-permute-start.15
  98.7 2.1 collective-permute-done.14
  101.7 2.8 %collective-permute-start.17 = (bf16[48,448]{0,1:T(8,128)(2,1)S(1)}, bf16[48,448]{0,1:T(8,128)(2,1)S(1)}, u32[]{:S(2)}, u32[]{:S(2)}) collective-permute-start(bf16[48,448]{0,1:T(8,128)(2,1)S(1)} %get-tuple-element.72), channel_id=1, source_target_pairs={{0,8},{1,24},{2,40},{3,56},{4,72},{5,88},{6,104},{7,120},{8,0},{9,... | collective-permute-start | bytes 129032 | tf_op jit(solution)/shard_map/ppermute | solution.py:305
  104.6 3.7 %collective-permute-done.17 = bf16[48,448]{0,1:T(8,128)(2,1)S(1)} collective-permute-done((bf16[48,448]{0,1:T(8,128)(2,1)S(1)}, bf16[48,448]{0,1:T(8,128)(2,1)S(1)}, u32[]{:S(2)}, u32[]{:S(2)}) %collective-permute-start.17) | collective-permute-done | bytes 43040 | tf_op jit(solution)/shard_map/ppermute | solution.py:305
  109.5 14.5 %collective-permute-start.18 = (bf16[48,896]{1,0:T(8,128)(2,1)S(1)}, bf16[48,896]{1,0:T(8,128)(2,1)S(1)}, u32[]{:S(2)}, u32[]{:S(2)}) collective-permute-start(bf16[48,896]{1,0:T(8,128)(2,1)S(1)} %add_convert_fusion.3), channel_id=1, source_target_pairs={{2,0},{4,2},{6,4},{0,6},{3,1},{5,3},{7,5},{1,7},{10,8},{12,10},{14... | collective-permute-start | bytes 258056 | tf_op jit(solution)/shard_map/ppermute | solution.py:27
  125.1 3.5 %collective-permute-done.18 = bf16[48,896]{1,0:T(8,128)(2,1)S(1)} collective-permute-done((bf16[48,896]{1,0:T(8,128)(2,1)S(1)}, bf16[48,896]{1,0:T(8,128)(2,1)S(1)}, u32[]{:S(2)}, u32[]{:S(2)}) %collective-permute-start.18) | collective-permute-done | bytes 86048 | tf_op jit(solution)/shard_map/ppermute | solution.py:27
  128.6 2.4 collective-permute-done.19
  133.8 4.3 %constant_dynamic-slice_fusion.7 = (bf16[4,1,512,256]{3,2,1,0:T(8,128)(2,1)}, bf16[4,1,512,256]{3,2,1,0:T(8,128)(2,1)}, bf16[4,1,512,256]{3,2,1,0:T(8,128)(2,1)}, bf16[4,1,512,256]{3,2,1,0:T(8,128)(2,1)}) fusion(bf16[4,2,896,256]{3,2,1,0:T(8,128)(2,1)} %bitcast.99, s32[]{:T(128)S(6)} %select_n.208, s32[]{:T(128)S(6)} %add.375, s32[]{:T(128)S(6)} %select_n.211, ...), kind=kLoop, calls=%fused_computation.214 | loop fusion | bytes 8388620 | tf_op jit(solution)/shard_map/slice | solution.py:368
  139.6 4.2 %all-to-all-start.1 = ((bf16[16,32,384]{2,1,0:T(8,128)(2,1)}), bf16[16,32,384]{2,1,0:T(8,128)(2,1)S(1)}, u32[]{:S(2)}, u32[]{:S(2)}) async-start(bf16[16,32,384]{2,1,0:T(8,128)(2,1)} %bitcast.10), calls=%async_computation.1 | async-start | bytes 786432 | tf_op jit(solution)/shard_map/all_to_all | solution.py:353
  143.8 10.4 %all-to-all-done.1 = bf16[16,32,384]{2,1,0:T(8,128)(2,1)S(1)} async-done(((bf16[16,32,384]{2,1,0:T(8,128)(2,1)}), bf16[16,32,384]{2,1,0:T(8,128)(2,1)S(1)}, u32[]{:S(2)}, u32[]{:S(2)}) %all-to-all-start.1) | async-done | bytes 393248 | tf_op jit(solution)/shard_map/all_to_all | solution.py:353
  154.2 2.0 convolution_convert_fusion.2
  156.3 4.4 %all-to-all-start.2 = ((bf16[16,32,2048]{2,1,0:T(8,128)(2,1)}), bf16[16,32,2048]{2,1,0:T(8,128)(2,1)}, u32[]{:S(2)}, u32[]{:S(2)}) async-start(bf16[16,32,2048]{2,1,0:T(8,128)(2,1)} %bitcast.18), calls=%async_computation.2 | async-start | bytes 4194304 | tf_op jit(solution)/shard_map/all_to_all | solution.py:353
  160.7 3.7 %constant_dynamic-slice_fusion.1 = (bf16[4,1,384,256]{3,2,1,0:T(8,128)(2,1)}, bf16[4,1,384,256]{3,2,1,0:T(8,128)(2,1)}, bf16[4,1,384,256]{3,2,1,0:T(8,128)(2,1)}, bf16[4,1,384,256]{3,2,1,0:T(8,128)(2,1)}) fusion(bf16[4,2,896,256]{3,2,1,0:T(8,128)(2,1)} %bitcast.100, s32[]{:T(128)S(6)} %select_n.208, s32[]{:T(128)S(6)} %select_n.211, ...), kind=kLoop, calls=%fused_computation.208 | loop fusion | bytes 6291464 | tf_op jit(solution)/shard_map/slice | solution.py:368
  169.8 6.7 %collective-permute-done.22 = bf16[512,384]{1,0:T(8,128)(2,1)S(1)} collective-permute-done((bf16[512,384]{1,0:T(8,128)(2,1)S(1)}, bf16[512,384]{1,0:T(8,128)(2,1)S(1)}, u32[]{:S(2)}, u32[]{:S(2)}) %collective-permute-start.22) | collective-permute-done | bytes 393248 | tf_op jit(solution)/shard_map/ppermute | solution.py:27
  176.7 3.6 %collective-permute-done.23 = bf16[512,384]{1,0:T(8,128)(2,1)S(1)} collective-permute-done((bf16[512,384]{1,0:T(8,128)(2,1)S(1)}, bf16[512,384]{1,0:T(8,128)(2,1)S(1)}, u32[]{:S(2)}, u32[]{:S(2)}) %collective-permute-start.23) | collective-permute-done | bytes 393248 | tf_op jit(solution)/shard_map/ppermute | solution.py:27
  180.3 5.9 %collective-permute-done.24 = bf16[512,384]{1,0:T(8,128)(2,1)S(1)} collective-permute-done((bf16[512,384]{1,0:T(8,128)(2,1)S(1)}, bf16[512,384]{1,0:T(8,128)(2,1)S(1)}, u32[]{:S(2)}, u32[]{:S(2)}) %collective-permute-start.24) | collective-permute-done | bytes 393248 | tf_op jit(solution)/shard_map/ppermute | solution.py:27
  191.8 2.7 %fusion.15 = f32[512,512]{1,0:T(8,128)S(1)} fusion(bf16[512,1536]{1,0:T(8,128)(2,1)} %collective-permute-done.25, bf16[1536,256]{1,0:T(8,128)(2,1)S(1)} %bitcast.117, bf16[1536,256]{1,0:T(8,128)(2,1)} %bitcast.118), kind=kOutput, calls=%fused_computation.25 | convolution fusion | flops 808452096 | bytes 4194304 | tf_op jit(solution)/shard_map/dot_general | solution.py:387
  194.6 3.0 %fusion.1 = f32[512,512]{1,0:T(8,128)S(1)} fusion(bf16[512,2048]{1,0:T(8,128)(2,1)} %bitcast.19, bf16[2048,256]{1,0:T(8,128)(2,1)S(1)} %bitcast.112, bf16[2048,256]{1,0:T(8,128)(2,1)S(1)} %bitcast.113), kind=kOutput, calls=%fused_computation.9 | convolution fusion | flops 1077936128 | bytes 5242880 | tf_op jit(solution)/shard_map/dot_general | solution.py:388
  199.0 2.5 fusion.25
  209.1 1.8 add_convert_fusion.1
  210.9 2.1 add_convert_fusion
  213.0 8.6 %all-to-all-start.3 = ((bf16[16,32,2048]{2,1,0:T(8,128)(2,1)}), bf16[16,32,2048]{2,1,0:T(8,128)(2,1)S(1)}, u32[]{:S(2)}, u32[]{:S(2)}) async-start(bf16[16,32,2048]{2,1,0:T(8,128)(2,1)} %bitcast.108), calls=%async_computation.3 | async-start | bytes 4194304 | tf_op jit(solution)/shard_map/all_to_all | solution.py:400
  224.2 2.0 fusion.9
  227.8 2.4 collective-permute-start.31
  231.5 8.4 %collective-permute-done.29 = bf16[512,384]{1,0:T(8,128)(2,1)S(1)} collective-permute-done((bf16[512,384]{1,0:T(8,128)(2,1)S(1)}, bf16[512,384]{1,0:T(8,128)(2,1)S(1)}, u32[]{:S(2)}, u32[]{:S(2)}) %collective-permute-start.29) | collective-permute-done | bytes 393248 | tf_op jit(solution)/shard_map/ppermute | solution.py:31
  239.9 7.3 %collective-permute-done.30 = bf16[512,384]{1,0:T(8,128)(2,1)S(1)} collective-permute-done((bf16[512,384]{1,0:T(8,128)(2,1)S(1)}, bf16[512,384]{1,0:T(8,128)(2,1)S(1)}, u32[]{:S(2)}, u32[]{:S(2)}) %collective-permute-start.30) | collective-permute-done | bytes 393248 | tf_op jit(solution)/shard_map/ppermute | solution.py:31
  248.1 4.6 %all-to-all-done.3 = bf16[16,32,2048]{2,1,0:T(8,128)(2,1)S(1)} async-done(((bf16[16,32,2048]{2,1,0:T(8,128)(2,1)}), bf16[16,32,2048]{2,1,0:T(8,128)(2,1)S(1)}, u32[]{:S(2)}, u32[]{:S(2)}) %all-to-all-start.3) | async-done | bytes 2097184 | tf_op jit(solution)/shard_map/all_to_all | solution.py:400
  255.0 2.4 collective-permute-start.34
  257.4 3.7 %all-to-all-start.4 = ((bf16[16,32,384]{2,1,0:T(8,128)(2,1)}), bf16[16,32,384]{2,1,0:T(8,128)(2,1)S(1)}, u32[]{:S(2)}, u32[]{:S(2)}) async-start(bf16[16,32,384]{2,1,0:T(8,128)(2,1)} %bitcast.42), calls=%async_computation.4 | async-start | bytes 786432 | tf_op jit(solution)/shard_map/all_to_all | solution.py:400
  261.1 2.0 constant_dynamic-slice_fusion.12
  263.1 7.1 %all-to-all-done.4 = bf16[16,32,384]{2,1,0:T(8,128)(2,1)S(1)} async-done(((bf16[16,32,384]{2,1,0:T(8,128)(2,1)}), bf16[16,32,384]{2,1,0:T(8,128)(2,1)S(1)}, u32[]{:S(2)}, u32[]{:S(2)}) %all-to-all-start.4) | async-done | bytes 393248 | tf_op jit(solution)/shard_map/all_to_all | solution.py:400
  (241 shorter events, 64.2 us)
Async XLA Ops:
  0.6 52.1 %copy-start = (bf16[16,512,128]{2,1,0:T(8,128)(2,1)S(1)}, bf16[16,512,128]{2,1,0:T(8,128)(2,1)}, u32[]{:S(2)}) copy-start(bf16[16,512,128]{2,1,0:T(8,128)(2,1)} %param.19) | copy-start | bytes 6291460
  7.3 25.0 %all-to-all-start = ((bf16[16,48,640]{2,1,0:T(8,128)(2,1)}), bf16[16,48,640]{2,1,0:T(8,128)(2,1)S(1)}, u32[]{:S(2)}, u32[]{:S(2)}) async-start(bf16[16,48,640]{2,1,0:T(8,128)(2,1)} %copy-done.5), calls=%async_computation | async-start | bytes 1966080 | tf_op jit(solution)/shard_map/all_to_all | solution.py:239
  53.9 7.6 %collective-permute-start.6 = (bf16[48,1024]{1,0:T(8,128)(2,1)S(1)}, bf16[48,1024]{1,0:T(8,128)(2,1)S(1)}, u32[]{:S(2)}, u32[]{:S(2)}) collective-permute-start(bf16[48,1024]{1,0:T(8,128)(2,1)S(1)} %get-tuple-element.69), channel_id=1, source_target_pairs={{32,0},{64,32},{96,64},{0,96},{33,1},{65,33},{97,65},{1,97},{34,2}... | collective-permute-start | bytes 294920 | tf_op jit(solution)/shard_map/ppermute | solution.py:27
  55.0 7.4 %collective-permute-start.7 = (bf16[48,1024]{1,0:T(8,128)(2,1)S(1)}, bf16[48,1024]{1,0:T(8,128)(2,1)S(1)}, u32[]{:S(2)}, u32[]{:S(2)}) collective-permute-start(bf16[48,1024]{1,0:T(8,128)(2,1)S(1)} %get-tuple-element.69), channel_id=1, source_target_pairs={{64,0},{96,32},{0,64},{32,96},{65,1},{97,33},{1,65},{33,97},{66,2}... | collective-permute-start | bytes 294920 | tf_op jit(solution)/shard_map/ppermute | solution.py:27
  55.9 6.5 %collective-permute-start.8 = (bf16[48,1024]{1,0:T(8,128)(2,1)S(1)}, bf16[48,1024]{1,0:T(8,128)(2,1)S(1)}, u32[]{:S(2)}, u32[]{:S(2)}) collective-permute-start(bf16[48,1024]{1,0:T(8,128)(2,1)S(1)} %get-tuple-element.69), channel_id=1, source_target_pairs={{96,0},{0,32},{32,64},{64,96},{97,1},{1,33},{33,65},{65,97},{98,2}... | collective-permute-start | bytes 294920 | tf_op jit(solution)/shard_map/ppermute | solution.py:27
  56.7 9.8 %collective-permute-start = (bf16[48,1024]{1,0:T(8,128)(2,1)S(1)}, bf16[48,1024]{1,0:T(8,128)(2,1)S(1)}, u32[]{:S(2)}, u32[]{:S(2)}) collective-permute-start(bf16[48,1024]{1,0:T(8,128)(2,1)S(1)} %get-tuple-element.70), channel_id=1, source_target_pairs={{8,0},{16,8},{24,16},{0,24},{9,1},{17,9},{25,17},{1,25},{10,2},{18... | collective-permute-start | bytes 294920 | tf_op jit(solution)/shard_map/ppermute | solution.py:27
  59.4 8.6 %collective-permute-start.1 = (bf16[48,1024]{1,0:T(8,128)(2,1)S(1)}, bf16[48,1024]{1,0:T(8,128)(2,1)S(1)}, u32[]{:S(2)}, u32[]{:S(2)}) collective-permute-start(bf16[48,1024]{1,0:T(8,128)(2,1)S(1)} %get-tuple-element.70), channel_id=1, source_target_pairs={{16,0},{24,8},{0,16},{8,24},{17,1},{25,9},{1,17},{9,25},{18,2},{26... | collective-permute-start | bytes 294920 | tf_op jit(solution)/shard_map/ppermute | solution.py:27
  61.5 7.0 %collective-permute-start.2 = (bf16[48,1024]{1,0:T(8,128)(2,1)S(1)}, bf16[48,1024]{1,0:T(8,128)(2,1)S(1)}, u32[]{:S(2)}, u32[]{:S(2)}) collective-permute-start(bf16[48,1024]{1,0:T(8,128)(2,1)S(1)} %get-tuple-element.70), channel_id=1, source_target_pairs={{24,0},{0,8},{8,16},{16,24},{25,1},{1,9},{9,17},{17,25},{26,2},{2,... | collective-permute-start | bytes 294920 | tf_op jit(solution)/shard_map/ppermute | solution.py:27
  62.4 11.7 %copy-start.38 = (bf16[2048,448]{0,1:T(8,128)(2,1)S(1)}, bf16[2048,448]{0,1:T(8,128)(2,1)}, u32[]{:S(2)}) copy-start(bf16[2048,448]{0,1:T(8,128)(2,1)} %param.20) | copy-start | bytes 5505028
  62.4 13.8 %collective-permute-start.11 = (bf16[192,1024]{1,0:T(8,128)(2,1)S(1)}, bf16[192,1024]{1,0:T(8,128)(2,1)S(1)}, u32[]{:S(2)}, u32[]{:S(2)}) collective-permute-start(bf16[192,1024]{1,0:T(8,128)(2,1)S(1)} %pad_maximum_fusion.2), channel_id=1, source_target_pairs={{24,0},{0,8},{8,16},{16,24},{25,1},{1,9},{9,17},{17,25},{26,2},{2,... | collective-permute-start | bytes 1179656 | tf_op jit(solution)/shard_map/ppermute | solution.py:27
  64.3 19.1 %collective-permute-start.10 = (bf16[192,1024]{1,0:T(8,128)(2,1)S(1)}, bf16[192,1024]{1,0:T(8,128)(2,1)S(1)}, u32[]{:S(2)}, u32[]{:S(2)}) collective-permute-start(bf16[192,1024]{1,0:T(8,128)(2,1)S(1)} %pad_maximum_fusion.2), channel_id=1, source_target_pairs={{16,0},{24,8},{0,16},{8,24},{17,1},{25,9},{1,17},{9,25},{18,2},{26... | collective-permute-start | bytes 1179656 | tf_op jit(solution)/shard_map/ppermute | solution.py:27
  66.5 17.3 %collective-permute-start.9 = (bf16[192,1024]{1,0:T(8,128)(2,1)S(1)}, bf16[192,1024]{1,0:T(8,128)(2,1)S(1)}, u32[]{:S(2)}, u32[]{:S(2)}) collective-permute-start(bf16[192,1024]{1,0:T(8,128)(2,1)S(1)} %pad_maximum_fusion.2), channel_id=1, source_target_pairs={{8,0},{16,8},{24,16},{0,24},{9,1},{17,9},{25,17},{1,25},{10,2},{18... | collective-permute-start | bytes 1179656 | tf_op jit(solution)/shard_map/ppermute | solution.py:27
  68.5 17.5 %collective-permute-start.5 = (bf16[192,1024]{1,0:T(8,128)(2,1)S(1)}, bf16[192,1024]{1,0:T(8,128)(2,1)S(1)}, u32[]{:S(2)}, u32[]{:S(2)}) collective-permute-start(bf16[192,1024]{1,0:T(8,128)(2,1)S(1)} %pad_maximum_fusion.1), channel_id=1, source_target_pairs={{96,0},{0,32},{32,64},{64,96},{97,1},{1,33},{33,65},{65,97},{98,2}... | collective-permute-start | bytes 1179656 | tf_op jit(solution)/shard_map/ppermute | solution.py:27
  70.4 16.3 %collective-permute-start.4 = (bf16[192,1024]{1,0:T(8,128)(2,1)S(1)}, bf16[192,1024]{1,0:T(8,128)(2,1)S(1)}, u32[]{:S(2)}, u32[]{:S(2)}) collective-permute-start(bf16[192,1024]{1,0:T(8,128)(2,1)S(1)} %pad_maximum_fusion.1), channel_id=1, source_target_pairs={{64,0},{96,32},{0,64},{32,96},{65,1},{97,33},{1,65},{33,97},{66,2}... | collective-permute-start | bytes 1179656 | tf_op jit(solution)/shard_map/ppermute | solution.py:27
  76.2 10.9 %collective-permute-start.3 = (bf16[192,1024]{1,0:T(8,128)(2,1)S(1)}, bf16[192,1024]{1,0:T(8,128)(2,1)S(1)}, u32[]{:S(2)}, u32[]{:S(2)}) collective-permute-start(bf16[192,1024]{1,0:T(8,128)(2,1)S(1)} %pad_maximum_fusion.1), channel_id=1, source_target_pairs={{32,0},{64,32},{96,64},{0,96},{33,1},{65,33},{97,65},{1,97},{34,2}... | collective-permute-start | bytes 1179656 | tf_op jit(solution)/shard_map/ppermute | solution.py:27
  89.0 8.6 %copy-start.36 = (s32[48,8]{0,1:T(8,128)S(1)}, s32[48,8]{0,1:T(8,128)}, u32[]{:S(2)}) copy-start(s32[48,8]{0,1:T(8,128)} %param.23) | copy-start | bytes 4612
  89.1 1.9 collective-permute-start.12
  91.1 41.4 %copy-start.35 = (f32[7168]{0:T(1024)S(1)}, f32[7168]{0:T(1024)}, u32[]{:S(2)}) copy-start(f32[7168]{0:T(1024)} %param.22) | copy-start | bytes 86020
  91.2 7.4 %collective-permute-start.13 = (bf16[96,448]{0,1:T(8,128)(2,1)S(1)}, bf16[96,448]{0,1:T(8,128)(2,1)S(1)}, u32[]{:S(2)}, u32[]{:S(2)}) collective-permute-start(bf16[96,448]{0,1:T(8,128)(2,1)S(1)} %get-tuple-element.59), channel_id=1, source_target_pairs={{0,4},{2,6},{4,0},{6,2},{1,5},{3,7},{5,1},{7,3},{8,12},{10,14},{12... | collective-permute-start | bytes 258056 | tf_op jit(solution)/shard_map/ppermute | solution.py:31
  94.4 6.4 %collective-permute-start.14 = (bf16[96,448]{0,1:T(8,128)(2,1)S(1)}, bf16[96,448]{0,1:T(8,128)(2,1)S(1)}, u32[]{:S(2)}, u32[]{:S(2)}) collective-permute-start(bf16[96,448]{0,1:T(8,128)(2,1)S(1)} %get-tuple-element.61), channel_id=1, source_target_pairs={{0,2},{2,4},{4,6},{6,0},{1,3},{3,5},{5,7},{7,1},{8,10},{10,12},{12... | collective-permute-start | bytes 258056 | tf_op jit(solution)/shard_map/ppermute | solution.py:31
  94.9 5.9 %collective-permute-start.15 = (bf16[96,448]{0,1:T(8,128)(2,1)S(1)}, bf16[96,448]{0,1:T(8,128)(2,1)S(1)}, u32[]{:S(2)}, u32[]{:S(2)}) collective-permute-start(bf16[96,448]{0,1:T(8,128)(2,1)S(1)} %get-tuple-element.60), channel_id=1, source_target_pairs={{0,6},{2,0},{4,2},{6,4},{1,7},{3,1},{5,3},{7,5},{8,14},{10,8},{12,... | collective-permute-start | bytes 258056 | tf_op jit(solution)/shard_map/ppermute | solution.py:31
  100.9 32.3 %copy-start.37 = (f32[48,8]{0,1:T(8,128)S(1)}, f32[48,8]{0,1:T(8,128)}, u32[]{:S(2)}) copy-start(f32[48,8]{0,1:T(8,128)} %param.24) | copy-start | bytes 4612
  101.0 3.6 %collective-permute-start.16 = (bf16[48,448]{0,1:T(8,128)(2,1)S(1)}, bf16[48,448]{0,1:T(8,128)(2,1)S(1)}, u32[]{:S(2)}, u32[]{:S(2)}) collective-permute-start(bf16[48,448]{0,1:T(8,128)(2,1)S(1)} %get-tuple-element.71), channel_id=1, source_target_pairs={{0,0},{1,16},{2,32},{3,48},{4,64},{5,80},{6,96},{7,112},{8,8},{9,2... | collective-permute-start | bytes 129032 | tf_op jit(solution)/shard_map/ppermute | solution.py:305
  101.7 6.6 %collective-permute-start.17 = (bf16[48,448]{0,1:T(8,128)(2,1)S(1)}, bf16[48,448]{0,1:T(8,128)(2,1)S(1)}, u32[]{:S(2)}, u32[]{:S(2)}) collective-permute-start(bf16[48,448]{0,1:T(8,128)(2,1)S(1)} %get-tuple-element.72), channel_id=1, source_target_pairs={{0,8},{1,24},{2,40},{3,56},{4,72},{5,88},{6,104},{7,120},{8,0},{9,... | collective-permute-start | bytes 129032 | tf_op jit(solution)/shard_map/ppermute | solution.py:305
  109.5 19.1 %collective-permute-start.18 = (bf16[48,896]{1,0:T(8,128)(2,1)S(1)}, bf16[48,896]{1,0:T(8,128)(2,1)S(1)}, u32[]{:S(2)}, u32[]{:S(2)}) collective-permute-start(bf16[48,896]{1,0:T(8,128)(2,1)S(1)} %add_convert_fusion.3), channel_id=1, source_target_pairs={{2,0},{4,2},{6,4},{0,6},{3,1},{5,3},{7,5},{1,7},{10,8},{12,10},{14... | collective-permute-start | bytes 258056 | tf_op jit(solution)/shard_map/ppermute | solution.py:27
  124.0 7.0 %collective-permute-start.19 = (bf16[48,896]{1,0:T(8,128)(2,1)S(1)}, bf16[48,896]{1,0:T(8,128)(2,1)S(1)}, u32[]{:S(2)}, u32[]{:S(2)}) collective-permute-start(bf16[48,896]{1,0:T(8,128)(2,1)S(1)} %add_convert_fusion.3), channel_id=1, source_target_pairs={{4,0},{6,2},{0,4},{2,6},{5,1},{7,3},{1,5},{3,7},{12,8},{14,10},{8,... | collective-permute-start | bytes 258056 | tf_op jit(solution)/shard_map/ppermute | solution.py:27
  124.0 8.2 %collective-permute-start.20 = (bf16[48,896]{1,0:T(8,128)(2,1)S(1)}, bf16[48,896]{1,0:T(8,128)(2,1)S(1)}, u32[]{:S(2)}, u32[]{:S(2)}) collective-permute-start(bf16[48,896]{1,0:T(8,128)(2,1)S(1)} %add_convert_fusion.3), channel_id=1, source_target_pairs={{6,0},{0,2},{2,4},{4,6},{7,1},{1,3},{3,5},{5,7},{14,8},{8,10},{10,... | collective-permute-start | bytes 258056 | tf_op jit(solution)/shard_map/ppermute | solution.py:27
  132.4 5.8 %collective-permute-start.21 = (bf16[48,3584]{1,0:T(8,128)(2,1)S(1)}, bf16[48,3584]{1,0:T(8,128)(2,1)S(1)}, u32[]{:S(2)}, u32[]{:S(2)}) collective-permute-start(bf16[48,3584]{1,0:T(8,128)(2,1)S(1)} %get-tuple-element.27), channel_id=1, source_target_pairs={{0,1},{1,0},{2,3},{3,2},{4,5},{5,4},{6,7},{7,6},{8,9},{9,8},{10,11... | collective-permute-start | bytes 1032200 | tf_op jit(solution)/shard_map/ppermute | solution.py:35
  139.6 14.7 %all-to-all-start.1 = ((bf16[16,32,384]{2,1,0:T(8,128)(2,1)}), bf16[16,32,384]{2,1,0:T(8,128)(2,1)S(1)}, u32[]{:S(2)}, u32[]{:S(2)}) async-start(bf16[16,32,384]{2,1,0:T(8,128)(2,1)} %bitcast.10), calls=%async_computation.1 | async-start | bytes 786432 | tf_op jit(solution)/shard_map/all_to_all | solution.py:353
  156.3 33.6 %all-to-all-start.2 = ((bf16[16,32,2048]{2,1,0:T(8,128)(2,1)}), bf16[16,32,2048]{2,1,0:T(8,128)(2,1)}, u32[]{:S(2)}, u32[]{:S(2)}) async-start(bf16[16,32,2048]{2,1,0:T(8,128)(2,1)} %bitcast.18), calls=%async_computation.2 | async-start | bytes 4194304 | tf_op jit(solution)/shard_map/all_to_all | solution.py:353
  164.4 12.1 %collective-permute-start.22 = (bf16[512,384]{1,0:T(8,128)(2,1)S(1)}, bf16[512,384]{1,0:T(8,128)(2,1)S(1)}, u32[]{:S(2)}, u32[]{:S(2)}) collective-permute-start(bf16[512,384]{1,0:T(8,128)(2,1)S(1)} %bitcast.103), channel_id=1, source_target_pairs={{2,0},{4,2},{6,4},{0,6},{3,1},{5,3},{7,5},{1,7},{10,8},{12,10},{14... | collective-permute-start | bytes 1179656 | tf_op jit(solution)/shard_map/ppermute | solution.py:27
  166.7 13.6 %collective-permute-start.23 = (bf16[512,384]{1,0:T(8,128)(2,1)S(1)}, bf16[512,384]{1,0:T(8,128)(2,1)S(1)}, u32[]{:S(2)}, u32[]{:S(2)}) collective-permute-start(bf16[512,384]{1,0:T(8,128)(2,1)S(1)} %bitcast.104), channel_id=1, source_target_pairs={{4,0},{6,2},{0,4},{2,6},{5,1},{7,3},{1,5},{3,7},{12,8},{14,10},{8,... | collective-permute-start | bytes 1179656 | tf_op jit(solution)/shard_map/ppermute | solution.py:27
  167.6 18.7 %collective-permute-start.24 = (bf16[512,384]{1,0:T(8,128)(2,1)S(1)}, bf16[512,384]{1,0:T(8,128)(2,1)S(1)}, u32[]{:S(2)}, u32[]{:S(2)}) collective-permute-start(bf16[512,384]{1,0:T(8,128)(2,1)S(1)} %bitcast.105), channel_id=1, source_target_pairs={{6,0},{0,2},{2,4},{4,6},{7,1},{1,3},{3,5},{5,7},{14,8},{8,10},{10,... | collective-permute-start | bytes 1179656 | tf_op jit(solution)/shard_map/ppermute | solution.py:27
  188.1 3.8 %collective-permute-start.25 = (bf16[512,1536]{1,0:T(8,128)(2,1)}, bf16[512,1536]{1,0:T(8,128)(2,1)}, u32[]{:S(2)}, u32[]{:S(2)}) collective-permute-start(bf16[512,1536]{1,0:T(8,128)(2,1)} %constant_dynamic-slice_fusion.9), channel_id=1, source_target_pairs={{0,1},{1,0},{2,3},{3,2},{4,5},{5,4},{6,7},{7,6},{8,9},{9,8},{10,11... | collective-permute-start | bytes 4718600 | tf_op jit(solution)/shard_map/ppermute | solution.py:35
  189.8 7.8 %collective-permute-start.26 = (bf16[512,2048]{1,0:T(8,128)(2,1)}, bf16[512,2048]{1,0:T(8,128)(2,1)S(1)}, u32[]{:S(2)}, u32[]{:S(2)}) collective-permute-start(bf16[512,2048]{1,0:T(8,128)(2,1)} %bitcast.19), channel_id=1, source_target_pairs={{0,1},{1,0},{2,3},{3,2},{4,5},{5,4},{6,7},{7,6},{8,9},{9,8},{10,11... | collective-permute-start | bytes 6291464 | tf_op jit(solution)/shard_map/ppermute | solution.py:35
  202.5 8.4 %collective-permute-start.28 = (bf16[512,2048]{1,0:T(8,128)(2,1)S(1)}, bf16[512,2048]{1,0:T(8,128)(2,1)S(1)}, u32[]{:S(2)}, u32[]{:S(2)}) collective-permute-start(bf16[512,2048]{1,0:T(8,128)(2,1)S(1)} %convolution_convert_fusion), channel_id=1, source_target_pairs={{0,1},{1,0},{2,3},{3,2},{4,5},{5,4},{6,7},{7,6},{8,9},{9,8},{10,11... | collective-permute-start | bytes 6291464 | tf_op jit(solution)/shard_map/ppermute | solution.py:35
  203.1 6.0 %copy-start.27 = (bf16[256,384]{1,0:T(8,128)(2,1)S(1)}, bf16[256,384]{1,0:T(8,128)(2,1)}, u32[]{:S(2)}) copy-start(bf16[256,384]{1,0:T(8,128)(2,1)} %get-tuple-element.38) | copy-start | bytes 589828
  203.1 6.0 %copy-start.28 = (bf16[256,384]{1,0:T(8,128)(2,1)S(1)}, bf16[256,384]{1,0:T(8,128)(2,1)}, u32[]{:S(2)}) copy-start(bf16[256,384]{1,0:T(8,128)(2,1)} %get-tuple-element.43) | copy-start | bytes 589828
  203.7 5.4 %collective-permute-start.27 = (bf16[512,1536]{1,0:T(8,128)(2,1)S(1)}, bf16[512,1536]{1,0:T(8,128)(2,1)S(1)}, u32[]{:S(2)}, u32[]{:S(2)}) collective-permute-start(bf16[512,1536]{1,0:T(8,128)(2,1)S(1)} %convolution_convert_fusion.1), channel_id=1, source_target_pairs={{0,1},{1,0},{2,3},{3,2},{4,5},{5,4},{6,7},{7,6},{8,9},{9,8},{10,11... | collective-permute-start | bytes 4718600 | tf_op jit(solution)/shard_map/ppermute | solution.py:35
  213.0 39.7 %all-to-all-start.3 = ((bf16[16,32,2048]{2,1,0:T(8,128)(2,1)}), bf16[16,32,2048]{2,1,0:T(8,128)(2,1)S(1)}, u32[]{:S(2)}, u32[]{:S(2)}) async-start(bf16[16,32,2048]{2,1,0:T(8,128)(2,1)} %bitcast.108), calls=%async_computation.3 | async-start | bytes 4194304 | tf_op jit(solution)/shard_map/all_to_all | solution.py:400
  226.3 13.6 %collective-permute-start.29 = (bf16[512,384]{1,0:T(8,128)(2,1)S(1)}, bf16[512,384]{1,0:T(8,128)(2,1)S(1)}, u32[]{:S(2)}, u32[]{:S(2)}) collective-permute-start(bf16[512,384]{1,0:T(8,128)(2,1)S(1)} %get-tuple-element.54), channel_id=1, source_target_pairs={{0,4},{2,6},{4,0},{6,2},{1,5},{3,7},{5,1},{7,3},{8,12},{10,14},{12... | collective-permute-start | bytes 1179656 | tf_op jit(solution)/shard_map/ppermute | solution.py:31
  227.0 20.2 %collective-permute-start.30 = (bf16[512,384]{1,0:T(8,128)(2,1)S(1)}, bf16[512,384]{1,0:T(8,128)(2,1)S(1)}, u32[]{:S(2)}, u32[]{:S(2)}) collective-permute-start(bf16[512,384]{1,0:T(8,128)(2,1)S(1)} %get-tuple-element.55), channel_id=1, source_target_pairs={{0,2},{2,4},{4,6},{6,0},{1,3},{3,5},{5,7},{7,1},{8,10},{10,12},{12... | collective-permute-start | bytes 1179656 | tf_op jit(solution)/shard_map/ppermute | solution.py:31
  227.8 19.3 %collective-permute-start.31 = (bf16[512,384]{1,0:T(8,128)(2,1)S(1)}, bf16[512,384]{1,0:T(8,128)(2,1)S(1)}, u32[]{:S(2)}, u32[]{:S(2)}) collective-permute-start(bf16[512,384]{1,0:T(8,128)(2,1)S(1)} %get-tuple-element.56), channel_id=1, source_target_pairs={{0,6},{2,0},{4,2},{6,4},{1,7},{3,1},{5,3},{7,5},{8,14},{10,8},{12,... | collective-permute-start | bytes 1179656 | tf_op jit(solution)/shard_map/ppermute | solution.py:31
  253.2 17.9 %copy-start.1 = (bf16[16,512,128]{2,1,0:T(8,128)(2,1)S(1)}, bf16[16,512,128]{2,1,0:T(8,128)(2,1)}, u32[]{:S(2)}) copy-start(bf16[16,512,128]{2,1,0:T(8,128)(2,1)} %param.19) | copy-start | bytes 6291460
  253.4 9.7 %collective-permute-start.32 = (bf16[48,512]{1,0:T(8,128)(2,1)S(1)}, bf16[48,512]{1,0:T(8,128)(2,1)S(1)}, u32[]{:S(2)}, u32[]{:S(2)}) collective-permute-start(bf16[48,512]{1,0:T(8,128)(2,1)S(1)} %get-tuple-element.66), channel_id=1, source_target_pairs={{0,4},{2,6},{4,0},{6,2},{1,5},{3,7},{5,1},{7,3},{8,12},{10,14},{12... | collective-permute-start | bytes 147464 | tf_op jit(solution)/shard_map/ppermute | solution.py:31
  254.1 9.0 %collective-permute-start.33 = (bf16[48,512]{1,0:T(8,128)(2,1)S(1)}, bf16[48,512]{1,0:T(8,128)(2,1)S(1)}, u32[]{:S(2)}, u32[]{:S(2)}) collective-permute-start(bf16[48,512]{1,0:T(8,128)(2,1)S(1)} %get-tuple-element.67), channel_id=1, source_target_pairs={{0,2},{2,4},{4,6},{6,0},{1,3},{3,5},{5,7},{7,1},{8,10},{10,12},{12... | collective-permute-start | bytes 147464 | tf_op jit(solution)/shard_map/ppermute | solution.py:31
  255.0 8.1 %collective-permute-start.34 = (bf16[48,512]{1,0:T(8,128)(2,1)S(1)}, bf16[48,512]{1,0:T(8,128)(2,1)S(1)}, u32[]{:S(2)}, u32[]{:S(2)}) collective-permute-start(bf16[48,512]{1,0:T(8,128)(2,1)S(1)} %get-tuple-element.68), channel_id=1, source_target_pairs={{0,6},{2,0},{4,2},{6,4},{1,7},{3,1},{5,3},{7,5},{8,14},{10,8},{12,... | collective-permute-start | bytes 147464 | tf_op jit(solution)/shard_map/ppermute | solution.py:31
  257.4 12.9 %all-to-all-start.4 = ((bf16[16,32,384]{2,1,0:T(8,128)(2,1)}), bf16[16,32,384]{2,1,0:T(8,128)(2,1)S(1)}, u32[]{:S(2)}, u32[]{:S(2)}) async-start(bf16[16,32,384]{2,1,0:T(8,128)(2,1)} %bitcast.42), calls=%async_computation.4 | async-start | bytes 786432 | tf_op jit(solution)/shard_map/all_to_all | solution.py:400
  (31 other events, 73.8 us)

commit v3 on v2

--- a/solution.py
+++ b/solution.py
@@ -90,11 +90,13 @@
     )(me, page_table, cache_len, accepted, query_rows)
 
 
-def plan_kernel(
-    me_ref, page_ref, held_ref, taken_ref, told_ref, which_ref, list_ref, seen_ref
+def attend_kernel(
+    me_ref, page_ref, held_ref, taken_ref, told_ref, own_ref, far_ref, pool_ref, out_ref,
+    which_ref, list_ref, seen_ref,
 ):
     me = me_ref[0]
-    count, per = page_ref.shape
+    count, rows, width = own_ref.shape
+    per = page_ref.shape[1]
 
     def plan(r, found):
         own_at, far_at = found
@@ -121,33 +123,9 @@
 
     lax.fori_loop(0, count, plan, (jnp.int32(0), jnp.int32(0)))
 
-
-def plan(me, page_table, cache_len, accepted, told):
-    count, per = page_table.shape
-    scalar = pl.BlockSpec(memory_space=pltpu.SMEM)
-    return pl.pallas_call(
-        plan_kernel,
-        out_shape=[
-            jax.ShapeDtypeStruct((count,), i32),
-            jax.ShapeDtypeStruct((count * per,), i32),
-            jax.ShapeDtypeStruct((count,), i32),
-        ],
-        in_specs=[scalar] * 5,
-        out_specs=[scalar] * 3,
-        name="plan",
-    )(me, page_table, cache_len, accepted, told)
-
-
-def attend_kernel(pick_ref, page_ref, seen_ref, *refs):
-    out_ref = refs[-1]
-    step = pl.program_id(0)
-    per = (len(refs) - 1) // 2
-    for n in range(2):
-        own_ref, far_ref, *pages = refs[n * per : (n + 1) * per]
-        at = step * 2 + n
-        width = own_ref.shape[2]
-        queries = jnp.where(at < 8, own_ref[0], far_ref[0, :, :width])
-        keys = jnp.concatenate([page[0] for page in pages], axis=0)
+    def one(at, source):
+        queries = source[which_ref[at], :, :width]
+        keys = jnp.concatenate([pool_ref[list_ref[at * per + k]] for k in range(per)], axis=0)
         scores = (
             lax.dot_general(queries, keys, (((1,), (1,)), ((), ())), preferred_element_type=f32)
             * softmax_scale
@@ -158,51 +136,38 @@
         highest = jnp.max(jnp.where(allowed, scores, -1e30), axis=-1, keepdims=True)
         weights = jnp.where(allowed, jnp.exp(jnp.where(allowed, scores - highest, 0.0)), 0.0)
         probs = (weights / jnp.sum(weights, axis=-1, keepdims=True)).astype(bf16)
-        out_ref[n] = lax.dot_general(
+        out_ref[at] = lax.dot_general(
             probs, keys[:, :LAT], (((1,), (0,)), ((), ())), preferred_element_type=f32
         ).astype(bf16)
 
-
-def attend(pick, pages, seen, own_queries, far_queries, kv_pool):
+    def turn(i, carry):
+        one(i, own_ref)
+        one(8 + i, far_ref)
+        return carry
+
+    lax.fori_loop(0, 8, turn, 0)
+
+
+def attend(me, page_table, cache_len, accepted, told, own_queries, far_queries, kv_pool):
     count, rows, width = own_queries.shape
-    page_rows = kv_pool.shape[1]
-    per = pages.shape[0] // count
-
-    def specs(n):
-        def own(i, pick, page, seen):
-            return (pick[jnp.minimum(i * 2 + n, 6 + n)], 0, 0)
-
-        def far(i, pick, page, seen):
-            return (pick[jnp.maximum(i * 2 + n, 8 + n)], 0, 0)
-
-        def page_spec(a):
-            return pl.BlockSpec(
-                (1, page_rows, width),
-                lambda i, pick, page, seen: (page[(i * 2 + n) * per + a], 0, 0),
-            )
-
-        return [
-            pl.BlockSpec((1, rows, width), own),
-            pl.BlockSpec((1, rows, far_queries.shape[2]), far),
-        ] + [page_spec(a) for a in range(per)]
-
-    spec = pltpu.PrefetchScalarGridSpec(
-        num_scalar_prefetch=3,
-        grid=(count // 2,),
-        in_specs=specs(0) + specs(1),
-        out_specs=pl.BlockSpec((2, rows, LAT), lambda i, pick, page, seen: (i, 0, 0)),
-    )
-    group = [own_queries, far_queries] + [kv_pool] * per
+    per = page_table.shape[1]
+    scalar, vector = (pl.BlockSpec(memory_space=m) for m in (pltpu.SMEM, pltpu.VMEM))
     return pl.pallas_call(
         attend_kernel,
         out_shape=jax.ShapeDtypeStruct((count, rows, LAT), bf16),
-        grid_spec=spec,
-        compiler_params=pltpu.CompilerParams(vmem_limit_bytes=32 * 2**20),
+        in_specs=[scalar] * 5 + [vector] * 3,
+        out_specs=vector,
+        scratch_shapes=[
+            pltpu.SMEM((count,), i32),
+            pltpu.SMEM((count * per,), i32),
+            pltpu.SMEM((count,), i32),
+        ],
+        compiler_params=pltpu.CompilerParams(vmem_limit_bytes=40 * 2**20),
         cost_estimate=pl.CostEstimate(
             flops=count * rows * 512 * 1088 * 2, bytes_accessed=12_000_000, transcendentals=0
         ),
         name="attend",
-    )(pick, pages, seen, *group, *group)
+    )(me, page_table, cache_len, accepted, told, own_queries, far_queries, kv_pool)
 
 
 def before(count):
@@ -240,9 +205,7 @@
     told = arrived[:, 0, width:]
     lenders = told[:, 24:40].astype(i32)
     line = told[:, 8:24].astype(i32)
-    latent = attend(
-        *plan(me, page_table, cache_len, accepted, line), query_rows, arrived, kv_pool
-    )
+    latent = attend(me, page_table, cache_len, accepted, line, query_rows, arrived, kv_pool)
     values = jnp.einsum(
         "thc,hcv->thv",
         latent.reshape(tokens, head_group, LAT),
@@ -279,37 +242,25 @@
     slot = jnp.where(is_own > 0, own_slot, far_slot)
     turned = ((lenders // RING - at_y) % RING) * RING + (lenders % RING - at_z) % RING
     first_row = (turned * requests + slot) * 3
-    source = (first_row[:, :, None] + jnp.arange(3, dtype=i32)).reshape(RING, 2, 2 * tokens)
-    source = lax.dynamic_slice_in_dim(jnp.concatenate([source, source], 0), at_x, RING, 0)
-    source = lax.dynamic_slice_in_dim(jnp.concatenate([source, source], 1), at_core, 2, 1)
-    source = source.transpose(1, 0, 2).reshape(-1)
+    source = (first_row[:, :, None] + jnp.arange(3, dtype=i32)).reshape(-1)
     rows_all = projected.shape[0]
     moves = (source[:, None] == jnp.arange(rows_all, dtype=i32)[None, :]).astype(bf16)
-    homed = jnp.dot(moves, projected, preferred_element_type=f32)
-    kept = homed[: rows_all // 2] + other_core(homed[rows_all // 2 :].astype(bf16)).astype(f32)
-    kept = kept.reshape(RING, 2 * tokens, columns)
-    mine = kept[0]
+    homed = jnp.dot(moves, projected, preferred_element_type=f32).astype(bf16)
+    homed = lax.all_to_all(homed.reshape(DP_N, tokens, columns), DP, 0, 0, tiled=True)
+
+    wide_piece = DP_N * columns // HEAD_N
+    homed = homed.reshape(RING, 2, 2, tokens, columns)
+    homed = lax.dynamic_slice_in_dim(jnp.concatenate([homed, homed], 0), at_x, RING, 0)
+    keep = lax.dynamic_slice_in_dim(homed, at_core, 1, 1)[:, 0]
+    give = lax.dynamic_slice_in_dim(homed, 1 - at_core, 1, 1)[:, 0]
+    kept = keep.astype(f32) + other_core(give).astype(f32)
+    attention = kept[0]
     for k in (2, 1, 3):
-        mine = mine + send(kept[k].astype(bf16), "x", k).astype(f32)
-    mine = mine.astype(bf16)
-
-    odd = dp_index % 2
-    low, high = mine[:tokens], mine[tokens:]
-    got = []
-    for turn in (0, 1):
-        pairs = []
-        for d in range(DP_N):
-            for h in range(HEAD_N):
-                pairs.append((d * HEAD_N + h, (2 * h + (turn + d) % 2) * HEAD_N + d // 2))
-        block = jnp.where((odd + turn) % 2 == 0, low, high)
-        got.append(lax.ppermute(block, ALL, pairs))
-    attention = jnp.concatenate(
-        [jnp.where(odd == 0, got[0], got[1]), jnp.where(odd == 0, got[1], got[0])], axis=1
-    )
-    wide_piece = 2 * columns
+        attention = attention + send(kept[k].astype(bf16), "x", k).astype(f32)
+    attention = jnp.concatenate([attention[0], attention[1]], axis=1)
     head_index = at_x * 2 + at_core
     near = lax.dynamic_slice_in_dim(residual, head_index * wide_piece, wide_piece, 1)
-    piece = (near.astype(f32) + attention.astype(f32)).astype(bf16)
+    piece = (near.astype(f32) + attention).astype(bf16)
 
     here = jnp.concatenate([piece] + [hop(piece, "x", k) for k in (1, 2, 3)], axis=1)
     there = other_core(here)

time: 272 us -> 269 us (0.989)
  starting transfers between devices: 86.3 us -> 80.2 us
  waiting for transfers between devices: 81.3 us -> 87.3 us
    all_to_all x0 -> x1, waiting for transfers between devices: none -> 11.5 us  [shards(): lax.all_to_all(homed.reshape(DP_N, tokens, columns), DP, 0, 0, tiled=True)]
    ppermute x18, starting transfers between devices: 38 us -> 26.8 us  [hop(): lax.ppermute(array, axis, [((i + step) % RING, i) for i in range(RING)])]
    all_to_all x0 -> x1, starting transfers between devices: none -> 9.65 us  [shards(): lax.all_to_all(homed.reshape(DP_N, tokens, columns), DP, 0, 0, tiled=True)]
    ppermute x2 -> x0, waiting for transfers between devices: 3.68 us -> none  [shards(): got.append(lax.ppermute(block, ALL, pairs))]
    ppermute x2 -> x0, starting transfers between devices: 3.5 us -> none  [shards(): got.append(lax.ppermute(block, ALL, pairs))]
    unnamed x110 -> x106, local copies, waits for them, and re-layouts: 36.9 us -> 35 us
  transfers between devices with their start and end apart: 40 -> 39, of which waited for: 22 -> 22; matrix products, arithmetic and copies ran while one was open for 21% -> 22% of each run, Pallas kernels for 0% -> 0%
where the time goes in v3:
time: 269 us; the launch traced here: 268 us
  waiting for transfers between devices  87.3 us (32%)
  starting transfers between devices  80.2 us (30%)
  local copies, waits for them, and re-layouts  52.4 us (19%)
  matrix products  25 us (9%)
  Pallas kernels  13.6 us (5%)
  other arithmetic  8.03 us (3%)
    unnamed x106, local copies, waits for them, and re-layouts  35 us
    ppermute x18, waiting for transfers between devices, hop(): lax.ppermute(array, axis, [((i + step) % RING, i) for i in range(RING)])  29.4 us
    ppermute x18, starting transfers between devices, hop(): lax.ppermute(array, axis, [((i + step) % RING, i) for i in range(RING)])  26.8 us
    ppermute x9, waiting for transfers between devices, send(): lax.ppermute(array, axis, [(i, (i + step) % RING) for i in range(RING)])  18.3 us
    ppermute x9, starting transfers between devices, send(): lax.ppermute(array, axis, [(i, (i + step) % RING) for i in range(RING)])  14.1 us
    all_to_all x2, waiting for transfers between devices, to_experts(): block = lax.all_to_all(block.reshape(DP_N, CAP, -1), DP, 0, 0, tiled=True)  12.3 us
    all_to_all x2, starting transfers between devices, to_home(): block = lax.all_to_all(block.reshape(DP_N, CAP, -1), DP, 0, 0, tiled=True)  12.2 us
    all_to_all x2, waiting for transfers between devices, to_home(): block = lax.all_to_all(block.reshape(DP_N, CAP, -1), DP, 0, 0, tiled=True)  11.7 us
  transfers between devices with their start and end apart: 39, of which 22 were waited for; matrix products, arithmetic and copies ran while one was open for 22% of the time, Pallas kernels for 0%

profile of v3, /device:TPU:0, one launch (start us, length us, event | category | flops | bytes accessed | tf_op | source)
XLA Modules:
  0.0 268.2 jit_solution(5819679895649880488)
XLA Ops:
  4.1 2.3 pack.1
  7.3 8.1 %all-to-all-start = ((bf16[16,48,640]{2,1,0:T(8,128)(2,1)}), bf16[16,48,640]{2,1,0:T(8,128)(2,1)S(1)}, u32[]{:S(2)}, u32[]{:S(2)}) async-start(bf16[16,48,640]{2,1,0:T(8,128)(2,1)} %copy-done.3), calls=%async_computation | async-start | bytes 1966080 | tf_op jit(solution)/shard_map/all_to_all | solution.py:204
  15.5 14.8 %copy.35.pool_ref = bf16[128,64,576]{2,1,0:T(8,128)(2,1)} copy(bf16[128,64,576]{0,2,1:T(8,128)(2,1)} %param.15) | data formatting | bytes 18874368 | tf_op args[1]
  30.2 2.1 all-to-all-done.far_ref
  32.5 4.0 %copy-done.2 = bf16[128,64,576]{2,1,0:T(8,128)(2,1)S(1)} copy-done((bf16[128,64,576]{2,1,0:T(8,128)(2,1)S(1)}, bf16[128,64,576]{2,1,0:T(8,128)(2,1)}, u32[]{:S(2)}) %copy-start.2) | copy-done | bytes 9437208
  37.7 11.3 %attend.1 = bf16[16,48,512]{2,1,0:T(8,128)(2,1)S(1)} custom-call(s32[1]{0:T(128)} %bitcast.me_ref, s32[16,8]{1,0:T(8,128)S(1)} %copy.33.page_ref, s32[16]{0:T(128)S(1)} %copy-done.7, s32[16]{0:T(128)S(1)} %copy-done.9, s32[16,16]{1,0:T(8,128)S(1)} %get-tuple-element.62.told_ref, bf16[16,48,576]{2,1,0:T(8,128)(2,1)S(1)} %bitcast.120, ...), custom_call_target="tpu_custom_call" | custom-call | flops 855638016 | bytes 12000000 | tf_op jit(solution)/shard_map/attend/pallas_call | solution.py:155
  52.9 2.7 collective-permute-start
  58.6 1.8 collective-permute-start.11
  60.5 2.3 collective-permute-start.10
  64.7 2.0 collective-permute-start.5
  66.7 2.1 collective-permute-start.4
  70.8 1.6 collective-permute-done.11
  72.5 2.8 %collective-permute-start.3 = (bf16[192,1024]{1,0:T(8,128)(2,1)S(1)}, bf16[192,1024]{1,0:T(8,128)(2,1)S(1)}, u32[]{:S(2)}, u32[]{:S(2)}) collective-permute-start(bf16[192,1024]{1,0:T(8,128)(2,1)S(1)} %pad_maximum_fusion.1), channel_id=1, source_target_pairs={{32,0},{64,32},{96,64},{0,96},{33,1},{65,33},{97,65},{1,97},{34,2}... | collective-permute-start | bytes 1179656 | tf_op jit(solution)/shard_map/ppermute | solution.py:27
  75.7 4.0 %collective-permute-done.10 = bf16[192,1024]{1,0:T(8,128)(2,1)S(1)} collective-permute-done((bf16[192,1024]{1,0:T(8,128)(2,1)S(1)}, bf16[192,1024]{1,0:T(8,128)(2,1)S(1)}, u32[]{:S(2)}, u32[]{:S(2)}) %collective-permute-start.10) | collective-permute-done | bytes 393248 | tf_op jit(solution)/shard_map/ppermute | solution.py:27
  80.6 1.7 collective-permute-done.5
  86.4 9.6 %all-to-all-start.1 = ((bf16[16,48,448]{2,1,0:T(8,128)(2,1)}), bf16[16,48,448]{2,1,0:T(8,128)(2,1)S(1)}, u32[]{:S(2)}, u32[]{:S(2)}) async-start(bf16[16,48,448]{2,1,0:T(8,128)(2,1)} %bitcast.7), calls=%async_computation.1 | async-start | bytes 1572864 | tf_op jit(solution)/shard_map/all_to_all | solution.py:249
  96.1 11.5 %all-to-all-done.1 = bf16[16,48,448]{2,1,0:T(8,128)(2,1)S(1)} async-done(((bf16[16,48,448]{2,1,0:T(8,128)(2,1)}), bf16[16,48,448]{2,1,0:T(8,128)(2,1)S(1)}, u32[]{:S(2)}, u32[]{:S(2)}) %all-to-all-start.1) | async-done | bytes 688160 | tf_op jit(solution)/shard_map/all_to_all | solution.py:249
  109.9 3.1 %collective-permute-start.13 = (bf16[2,48,448]{2,1,0:T(8,128)(2,1)S(1)}, bf16[2,48,448]{2,1,0:T(8,128)(2,1)S(1)}, u32[]{:S(2)}, u32[]{:S(2)}) collective-permute-start(bf16[2,48,448]{2,1,0:T(8,128)(2,1)S(1)} %get-tuple-element.49), channel_id=1, source_target_pairs={{0,4},{2,6},{4,0},{6,2},{1,5},{3,7},{5,1},{7,3},{8,12},{10,14},{12... | collective-permute-start | bytes 258056 | tf_op jit(solution)/shard_map/ppermute | solution.py:31
  113.5 2.6 collective-permute-start.15
  116.6 2.2 collective-permute-done.14
  119.9 3.3 %collective-permute-start.16 = (bf16[48,896]{1,0:T(8,128)(2,1)S(1)}, bf16[48,896]{1,0:T(8,128)(2,1)S(1)}, u32[]{:S(2)}, u32[]{:S(2)}) collective-permute-start(bf16[48,896]{1,0:T(8,128)(2,1)S(1)} %fusion.95), channel_id=1, source_target_pairs={{2,0},{4,2},{6,4},{0,6},{3,1},{5,3},{7,5},{1,7},{10,8},{12,10},{14... | collective-permute-start | bytes 258056 | tf_op jit(solution)/shard_map/ppermute | solution.py:27
  124.3 1.8 collective-permute-done.16
  126.1 3.1 %collective-permute-done.17 = bf16[48,896]{1,0:T(8,128)(2,1)S(1)} collective-permute-done((bf16[48,896]{1,0:T(8,128)(2,1)S(1)}, bf16[48,896]{1,0:T(8,128)(2,1)S(1)}, u32[]{:S(2)}, u32[]{:S(2)}) %collective-permute-start.17) | collective-permute-done | bytes 86048 | tf_op jit(solution)/shard_map/ppermute | solution.py:27
  131.4 4.4 %constant_dynamic-slice_fusion.4 = (bf16[4,1,512,256]{3,2,1,0:T(8,128)(2,1)}, bf16[4,1,512,256]{3,2,1,0:T(8,128)(2,1)}, bf16[4,1,512,256]{3,2,1,0:T(8,128)(2,1)}, bf16[4,1,512,256]{3,2,1,0:T(8,128)(2,1)}) fusion(bf16[4,2,896,256]{3,2,1,0:T(8,128)(2,1)} %bitcast.126, s32[]{:T(128)S(6)} %select_n.160, s32[]{:T(128)S(6)} %add.371, s32[]{:T(128)S(6)} %select_n.162, ...), kind=kLoop, calls=%fused_computation.221 | loop fusion | bytes 8388620 | tf_op jit(solution)/shard_map/slice | solution.py:319
  137.2 3.6 %all-to-all-start.2 = ((bf16[16,32,384]{2,1,0:T(8,128)(2,1)}), bf16[16,32,384]{2,1,0:T(8,128)(2,1)S(1)}, u32[]{:S(2)}, u32[]{:S(2)}) async-start(bf16[16,32,384]{2,1,0:T(8,128)(2,1)} %bitcast.19), calls=%async_computation.2 | async-start | bytes 786432 | tf_op jit(solution)/shard_map/all_to_all | solution.py:304
  140.8 10.7 %all-to-all-done.2 = bf16[16,32,384]{2,1,0:T(8,128)(2,1)S(1)} async-done(((bf16[16,32,384]{2,1,0:T(8,128)(2,1)}), bf16[16,32,384]{2,1,0:T(8,128)(2,1)S(1)}, u32[]{:S(2)}, u32[]{:S(2)}) %all-to-all-start.2) | async-done | bytes 393248 | tf_op jit(solution)/shard_map/all_to_all | solution.py:304
  151.5 2.0 convolution_convert_fusion.2
  153.5 4.4 %all-to-all-start.3 = ((bf16[16,32,2048]{2,1,0:T(8,128)(2,1)}), bf16[16,32,2048]{2,1,0:T(8,128)(2,1)}, u32[]{:S(2)}, u32[]{:S(2)}) async-start(bf16[16,32,2048]{2,1,0:T(8,128)(2,1)} %bitcast.27), calls=%async_computation.3 | async-start | bytes 4194304 | tf_op jit(solution)/shard_map/all_to_all | solution.py:304
  157.9 3.7 %constant_dynamic-slice_fusion = (bf16[4,1,384,256]{3,2,1,0:T(8,128)(2,1)}, bf16[4,1,384,256]{3,2,1,0:T(8,128)(2,1)}, bf16[4,1,384,256]{3,2,1,0:T(8,128)(2,1)}, bf16[4,1,384,256]{3,2,1,0:T(8,128)(2,1)}) fusion(bf16[4,2,896,256]{3,2,1,0:T(8,128)(2,1)} %bitcast.129, s32[]{:T(128)S(6)} %select_n.160, s32[]{:T(128)S(6)} %select_n.162, ...), kind=kLoop, calls=%fused_computation.217 | loop fusion | bytes 6291464 | tf_op jit(solution)/shard_map/slice | solution.py:319
  167.0 6.7 %collective-permute-done.20 = bf16[512,384]{1,0:T(8,128)(2,1)S(1)} collective-permute-done((bf16[512,384]{1,0:T(8,128)(2,1)S(1)}, bf16[512,384]{1,0:T(8,128)(2,1)S(1)}, u32[]{:S(2)}, u32[]{:S(2)}) %collective-permute-start.20) | collective-permute-done | bytes 393248 | tf_op jit(solution)/shard_map/ppermute | solution.py:27
  173.9 3.5 %collective-permute-done.21 = bf16[512,384]{1,0:T(8,128)(2,1)S(1)} collective-permute-done((bf16[512,384]{1,0:T(8,128)(2,1)S(1)}, bf16[512,384]{1,0:T(8,128)(2,1)S(1)}, u32[]{:S(2)}, u32[]{:S(2)}) %collective-permute-start.21) | collective-permute-done | bytes 393248 | tf_op jit(solution)/shard_map/ppermute | solution.py:27
  177.5 5.9 %collective-permute-done.22 = bf16[512,384]{1,0:T(8,128)(2,1)S(1)} collective-permute-done((bf16[512,384]{1,0:T(8,128)(2,1)S(1)}, bf16[512,384]{1,0:T(8,128)(2,1)S(1)}, u32[]{:S(2)}, u32[]{:S(2)}) %collective-permute-start.22) | collective-permute-done | bytes 393248 | tf_op jit(solution)/shard_map/ppermute | solution.py:27
  185.3 1.7 all-to-all-done.3
  189.1 2.7 %fusion.15 = f32[512,512]{1,0:T(8,128)S(1)} fusion(bf16[512,1536]{1,0:T(8,128)(2,1)} %collective-permute-done.23, bf16[1536,256]{1,0:T(8,128)(2,1)} %bitcast.145, bf16[1536,256]{1,0:T(8,128)(2,1)S(1)} %bitcast.144), kind=kOutput, calls=%fused_computation.29 | convolution fusion | flops 808452096 | bytes 4194304 | tf_op jit(solution)/shard_map/dot_general | solution.py:338
  191.8 3.0 %fusion.1 = f32[512,512]{1,0:T(8,128)S(1)} fusion(bf16[512,2048]{1,0:T(8,128)(2,1)} %bitcast.28, bf16[2048,256]{1,0:T(8,128)(2,1)S(1)} %bitcast.139, bf16[2048,256]{1,0:T(8,128)(2,1)S(1)} %bitcast.140), kind=kOutput, calls=%fused_computation.9 | convolution fusion | flops 1077936128 | bytes 5242880 | tf_op jit(solution)/shard_map/dot_general | solution.py:339
  196.2 2.5 fusion.26
  206.4 1.7 add_convert_fusion.1
  208.1 2.1 add_convert_fusion
  210.2 8.5 %all-to-all-start.4 = ((bf16[16,32,2048]{2,1,0:T(8,128)(2,1)}), bf16[16,32,2048]{2,1,0:T(8,128)(2,1)S(1)}, u32[]{:S(2)}, u32[]{:S(2)}) async-start(bf16[16,32,2048]{2,1,0:T(8,128)(2,1)} %bitcast.135), calls=%async_computation.4 | async-start | bytes 4194304 | tf_op jit(solution)/shard_map/all_to_all | solution.py:351
  221.3 2.0 fusion.9
  225.0 2.3 collective-permute-start.29
  228.6 8.4 %collective-permute-done.27 = bf16[512,384]{1,0:T(8,128)(2,1)S(1)} collective-permute-done((bf16[512,384]{1,0:T(8,128)(2,1)S(1)}, bf16[512,384]{1,0:T(8,128)(2,1)S(1)}, u32[]{:S(2)}, u32[]{:S(2)}) %collective-permute-start.27) | collective-permute-done | bytes 393248 | tf_op jit(solution)/shard_map/ppermute | solution.py:31
  237.0 7.3 %collective-permute-done.28 = bf16[512,384]{1,0:T(8,128)(2,1)S(1)} collective-permute-done((bf16[512,384]{1,0:T(8,128)(2,1)S(1)}, bf16[512,384]{1,0:T(8,128)(2,1)S(1)}, u32[]{:S(2)}, u32[]{:S(2)}) %collective-permute-start.28) | collective-permute-done | bytes 393248 | tf_op jit(solution)/shard_map/ppermute | solution.py:31
  245.3 4.6 %all-to-all-done.4 = bf16[16,32,2048]{2,1,0:T(8,128)(2,1)S(1)} async-done(((bf16[16,32,2048]{2,1,0:T(8,128)(2,1)}), bf16[16,32,2048]{2,1,0:T(8,128)(2,1)S(1)}, u32[]{:S(2)}, u32[]{:S(2)}) %all-to-all-start.4) | async-done | bytes 2097184 | tf_op jit(solution)/shard_map/all_to_all | solution.py:351
  252.1 2.4 collective-permute-start.32
  254.4 3.7 %all-to-all-start.5 = ((bf16[16,32,384]{2,1,0:T(8,128)(2,1)}), bf16[16,32,384]{2,1,0:T(8,128)(2,1)S(1)}, u32[]{:S(2)}, u32[]{:S(2)}) async-start(bf16[16,32,384]{2,1,0:T(8,128)(2,1)} %bitcast.51), calls=%async_computation.5 | async-start | bytes 786432 | tf_op jit(solution)/shard_map/all_to_all | solution.py:351
  258.2 2.0 constant_dynamic-slice_fusion.9
  260.2 7.1 %all-to-all-done.5 = bf16[16,32,384]{2,1,0:T(8,128)(2,1)S(1)} async-done(((bf16[16,32,384]{2,1,0:T(8,128)(2,1)}), bf16[16,32,384]{2,1,0:T(8,128)(2,1)S(1)}, u32[]{:S(2)}, u32[]{:S(2)}) %all-to-all-start.5) | async-done | bytes 393248 | tf_op jit(solution)/shard_map/all_to_all | solution.py:351
  (228 shorter events, 58.9 us)
Async XLA Ops:
  0.6 48.3 %copy-start = (bf16[16,512,128]{2,1,0:T(8,128)(2,1)S(1)}, bf16[16,512,128]{2,1,0:T(8,128)(2,1)}, u32[]{:S(2)}) copy-start(bf16[16,512,128]{2,1,0:T(8,128)(2,1)} %param.19) | copy-start | bytes 6291460
  7.3 25.0 %all-to-all-start = ((bf16[16,48,640]{2,1,0:T(8,128)(2,1)}), bf16[16,48,640]{2,1,0:T(8,128)(2,1)S(1)}, u32[]{:S(2)}, u32[]{:S(2)}) async-start(bf16[16,48,640]{2,1,0:T(8,128)(2,1)} %copy-done.3), calls=%async_computation | async-start | bytes 1966080 | tf_op jit(solution)/shard_map/all_to_all | solution.py:204
  15.4 17.0 %copy-start.7 = (s32[16]{0:T(128)S(1)}, s32[16]{0:T(128)}, u32[]{:S(2)}) copy-start(s32[16]{0:T(128)} %held_ref.3) | copy-start | bytes 196
  15.4 17.0 %copy-start.9 = (s32[16]{0:T(128)S(1)}, s32[16]{0:T(128)}, u32[]{:S(2)}) copy-start(s32[16]{0:T(128)} %taken_ref.3) | copy-start | bytes 196
  50.1 7.6 %collective-permute-start.6 = (bf16[48,1024]{1,0:T(8,128)(2,1)S(1)}, bf16[48,1024]{1,0:T(8,128)(2,1)S(1)}, u32[]{:S(2)}, u32[]{:S(2)}) collective-permute-start(bf16[48,1024]{1,0:T(8,128)(2,1)S(1)} %get-tuple-element.59), channel_id=1, source_target_pairs={{32,0},{64,32},{96,64},{0,96},{33,1},{65,33},{97,65},{1,97},{34,2}... | collective-permute-start | bytes 294920 | tf_op jit(solution)/shard_map/ppermute | solution.py:27
  51.2 7.4 %collective-permute-start.7 = (bf16[48,1024]{1,0:T(8,128)(2,1)S(1)}, bf16[48,1024]{1,0:T(8,128)(2,1)S(1)}, u32[]{:S(2)}, u32[]{:S(2)}) collective-permute-start(bf16[48,1024]{1,0:T(8,128)(2,1)S(1)} %get-tuple-element.59), channel_id=1, source_target_pairs={{64,0},{96,32},{0,64},{32,96},{65,1},{97,33},{1,65},{33,97},{66,2}... | collective-permute-start | bytes 294920 | tf_op jit(solution)/shard_map/ppermute | solution.py:27
  52.1 6.5 %collective-permute-start.8 = (bf16[48,1024]{1,0:T(8,128)(2,1)S(1)}, bf16[48,1024]{1,0:T(8,128)(2,1)S(1)}, u32[]{:S(2)}, u32[]{:S(2)}) collective-permute-start(bf16[48,1024]{1,0:T(8,128)(2,1)S(1)} %get-tuple-element.59), channel_id=1, source_target_pairs={{96,0},{0,32},{32,64},{64,96},{97,1},{1,33},{33,65},{65,97},{98,2}... | collective-permute-start | bytes 294920 | tf_op jit(solution)/shard_map/ppermute | solution.py:27
  52.9 9.8 %collective-permute-start = (bf16[48,1024]{1,0:T(8,128)(2,1)S(1)}, bf16[48,1024]{1,0:T(8,128)(2,1)S(1)}, u32[]{:S(2)}, u32[]{:S(2)}) collective-permute-start(bf16[48,1024]{1,0:T(8,128)(2,1)S(1)} %get-tuple-element.60), channel_id=1, source_target_pairs={{8,0},{16,8},{24,16},{0,24},{9,1},{17,9},{25,17},{1,25},{10,2},{18... | collective-permute-start | bytes 294920 | tf_op jit(solution)/shard_map/ppermute | solution.py:27
  55.6 8.6 %collective-permute-start.1 = (bf16[48,1024]{1,0:T(8,128)(2,1)S(1)}, bf16[48,1024]{1,0:T(8,128)(2,1)S(1)}, u32[]{:S(2)}, u32[]{:S(2)}) collective-permute-start(bf16[48,1024]{1,0:T(8,128)(2,1)S(1)} %get-tuple-element.60), channel_id=1, source_target_pairs={{16,0},{24,8},{0,16},{8,24},{17,1},{25,9},{1,17},{9,25},{18,2},{26... | collective-permute-start | bytes 294920 | tf_op jit(solution)/shard_map/ppermute | solution.py:27
  57.7 7.0 %collective-permute-start.2 = (bf16[48,1024]{1,0:T(8,128)(2,1)S(1)}, bf16[48,1024]{1,0:T(8,128)(2,1)S(1)}, u32[]{:S(2)}, u32[]{:S(2)}) collective-permute-start(bf16[48,1024]{1,0:T(8,128)(2,1)S(1)} %get-tuple-element.60), channel_id=1, source_target_pairs={{24,0},{0,8},{8,16},{16,24},{25,1},{1,9},{9,17},{17,25},{26,2},{2,... | collective-permute-start | bytes 294920 | tf_op jit(solution)/shard_map/ppermute | solution.py:27
  58.6 11.7 %copy-start.36 = (bf16[2048,448]{0,1:T(8,128)(2,1)S(1)}, bf16[2048,448]{0,1:T(8,128)(2,1)}, u32[]{:S(2)}) copy-start(bf16[2048,448]{0,1:T(8,128)(2,1)} %param.20) | copy-start | bytes 5505028
  58.6 13.8 %collective-permute-start.11 = (bf16[192,1024]{1,0:T(8,128)(2,1)S(1)}, bf16[192,1024]{1,0:T(8,128)(2,1)S(1)}, u32[]{:S(2)}, u32[]{:S(2)}) collective-permute-start(bf16[192,1024]{1,0:T(8,128)(2,1)S(1)} %pad_maximum_fusion.2), channel_id=1, source_target_pairs={{24,0},{0,8},{8,16},{16,24},{25,1},{1,9},{9,17},{17,25},{26,2},{2,... | collective-permute-start | bytes 1179656 | tf_op jit(solution)/shard_map/ppermute | solution.py:27
  60.5 19.2 %collective-permute-start.10 = (bf16[192,1024]{1,0:T(8,128)(2,1)S(1)}, bf16[192,1024]{1,0:T(8,128)(2,1)S(1)}, u32[]{:S(2)}, u32[]{:S(2)}) collective-permute-start(bf16[192,1024]{1,0:T(8,128)(2,1)S(1)} %pad_maximum_fusion.2), channel_id=1, source_target_pairs={{16,0},{24,8},{0,16},{8,24},{17,1},{25,9},{1,17},{9,25},{18,2},{26... | collective-permute-start | bytes 1179656 | tf_op jit(solution)/shard_map/ppermute | solution.py:27
  62.8 17.3 %collective-permute-start.9 = (bf16[192,1024]{1,0:T(8,128)(2,1)S(1)}, bf16[192,1024]{1,0:T(8,128)(2,1)S(1)}, u32[]{:S(2)}, u32[]{:S(2)}) collective-permute-start(bf16[192,1024]{1,0:T(8,128)(2,1)S(1)} %pad_maximum_fusion.2), channel_id=1, source_target_pairs={{8,0},{16,8},{24,16},{0,24},{9,1},{17,9},{25,17},{1,25},{10,2},{18... | collective-permute-start | bytes 1179656 | tf_op jit(solution)/shard_map/ppermute | solution.py:27
  64.7 17.5 %collective-permute-start.5 = (bf16[192,1024]{1,0:T(8,128)(2,1)S(1)}, bf16[192,1024]{1,0:T(8,128)(2,1)S(1)}, u32[]{:S(2)}, u32[]{:S(2)}) collective-permute-start(bf16[192,1024]{1,0:T(8,128)(2,1)S(1)} %pad_maximum_fusion.1), channel_id=1, source_target_pairs={{96,0},{0,32},{32,64},{64,96},{97,1},{1,33},{33,65},{65,97},{98,2}... | collective-permute-start | bytes 1179656 | tf_op jit(solution)/shard_map/ppermute | solution.py:27
  66.7 16.3 %collective-permute-start.4 = (bf16[192,1024]{1,0:T(8,128)(2,1)S(1)}, bf16[192,1024]{1,0:T(8,128)(2,1)S(1)}, u32[]{:S(2)}, u32[]{:S(2)}) collective-permute-start(bf16[192,1024]{1,0:T(8,128)(2,1)S(1)} %pad_maximum_fusion.1), channel_id=1, source_target_pairs={{64,0},{96,32},{0,64},{32,96},{65,1},{97,33},{1,65},{33,97},{66,2}... | collective-permute-start | bytes 1179656 | tf_op jit(solution)/shard_map/ppermute | solution.py:27
  72.5 10.9 %collective-permute-start.3 = (bf16[192,1024]{1,0:T(8,128)(2,1)S(1)}, bf16[192,1024]{1,0:T(8,128)(2,1)S(1)}, u32[]{:S(2)}, u32[]{:S(2)}) collective-permute-start(bf16[192,1024]{1,0:T(8,128)(2,1)S(1)} %pad_maximum_fusion.1), channel_id=1, source_target_pairs={{32,0},{64,32},{96,64},{0,96},{33,1},{65,33},{97,65},{1,97},{34,2}... | collective-permute-start | bytes 1179656 | tf_op jit(solution)/shard_map/ppermute | solution.py:27
  85.2 22.6 %copy-start.34 = (s32[48,8]{0,1:T(8,128)S(1)}, s32[48,8]{0,1:T(8,128)}, u32[]{:S(2)}) copy-start(s32[48,8]{0,1:T(8,128)} %param.23) | copy-start | bytes 4612
  86.4 21.1 %all-to-all-start.1 = ((bf16[16,48,448]{2,1,0:T(8,128)(2,1)}), bf16[16,48,448]{2,1,0:T(8,128)(2,1)S(1)}, u32[]{:S(2)}, u32[]{:S(2)}) async-start(bf16[16,48,448]{2,1,0:T(8,128)(2,1)} %bitcast.7), calls=%async_computation.1 | async-start | bytes 1572864 | tf_op jit(solution)/shard_map/all_to_all | solution.py:249
  107.8 1.8 collective-permute-start.12
  109.8 20.3 %copy-start.33 = (f32[7168]{0:T(1024)S(1)}, f32[7168]{0:T(1024)}, u32[]{:S(2)}) copy-start(f32[7168]{0:T(1024)} %param.22) | copy-start | bytes 86020
  109.8 20.9 %copy-start.35 = (f32[48,8]{0,1:T(8,128)S(1)}, f32[48,8]{0,1:T(8,128)}, u32[]{:S(2)}) copy-start(f32[48,8]{0,1:T(8,128)} %param.24) | copy-start | bytes 4612
  109.9 6.7 %collective-permute-start.13 = (bf16[2,48,448]{2,1,0:T(8,128)(2,1)S(1)}, bf16[2,48,448]{2,1,0:T(8,128)(2,1)S(1)}, u32[]{:S(2)}, u32[]{:S(2)}) collective-permute-start(bf16[2,48,448]{2,1,0:T(8,128)(2,1)S(1)} %get-tuple-element.49), channel_id=1, source_target_pairs={{0,4},{2,6},{4,0},{6,2},{1,5},{3,7},{5,1},{7,3},{8,12},{10,14},{12... | collective-permute-start | bytes 258056 | tf_op jit(solution)/shard_map/ppermute | solution.py:31
  113.0 5.8 %collective-permute-start.14 = (bf16[2,48,448]{2,1,0:T(8,128)(2,1)S(1)}, bf16[2,48,448]{2,1,0:T(8,128)(2,1)S(1)}, u32[]{:S(2)}, u32[]{:S(2)}) collective-permute-start(bf16[2,48,448]{2,1,0:T(8,128)(2,1)S(1)} %get-tuple-element.51), channel_id=1, source_target_pairs={{0,2},{2,4},{4,6},{6,0},{1,3},{3,5},{5,7},{7,1},{8,10},{10,12},{12... | collective-permute-start | bytes 258056 | tf_op jit(solution)/shard_map/ppermute | solution.py:31
  113.5 5.2 %collective-permute-start.15 = (bf16[2,48,448]{2,1,0:T(8,128)(2,1)S(1)}, bf16[2,48,448]{2,1,0:T(8,128)(2,1)S(1)}, u32[]{:S(2)}, u32[]{:S(2)}) collective-permute-start(bf16[2,48,448]{2,1,0:T(8,128)(2,1)S(1)} %get-tuple-element.50), channel_id=1, source_target_pairs={{0,6},{2,0},{4,2},{6,4},{1,7},{3,1},{5,3},{7,5},{8,14},{10,8},{12,... | collective-permute-start | bytes 258056 | tf_op jit(solution)/shard_map/ppermute | solution.py:31
  119.9 6.3 %collective-permute-start.16 = (bf16[48,896]{1,0:T(8,128)(2,1)S(1)}, bf16[48,896]{1,0:T(8,128)(2,1)S(1)}, u32[]{:S(2)}, u32[]{:S(2)}) collective-permute-start(bf16[48,896]{1,0:T(8,128)(2,1)S(1)} %fusion.95), channel_id=1, source_target_pairs={{2,0},{4,2},{6,4},{0,6},{3,1},{5,3},{7,5},{1,7},{10,8},{12,10},{14... | collective-permute-start | bytes 258056 | tf_op jit(solution)/shard_map/ppermute | solution.py:27
  123.2 6.1 %collective-permute-start.17 = (bf16[48,896]{1,0:T(8,128)(2,1)S(1)}, bf16[48,896]{1,0:T(8,128)(2,1)S(1)}, u32[]{:S(2)}, u32[]{:S(2)}) collective-permute-start(bf16[48,896]{1,0:T(8,128)(2,1)S(1)} %fusion.95), channel_id=1, source_target_pairs={{4,0},{6,2},{0,4},{2,6},{5,1},{7,3},{1,5},{3,7},{12,8},{14,10},{8,... | collective-permute-start | bytes 258056 | tf_op jit(solution)/shard_map/ppermute | solution.py:27
  123.2 6.6 %collective-permute-start.18 = (bf16[48,896]{1,0:T(8,128)(2,1)S(1)}, bf16[48,896]{1,0:T(8,128)(2,1)S(1)}, u32[]{:S(2)}, u32[]{:S(2)}) collective-permute-start(bf16[48,896]{1,0:T(8,128)(2,1)S(1)} %fusion.95), channel_id=1, source_target_pairs={{6,0},{0,2},{2,4},{4,6},{7,1},{1,3},{3,5},{5,7},{14,8},{8,10},{10,... | collective-permute-start | bytes 258056 | tf_op jit(solution)/shard_map/ppermute | solution.py:27
  130.0 5.8 %collective-permute-start.19 = (bf16[48,3584]{1,0:T(8,128)(2,1)S(1)}, bf16[48,3584]{1,0:T(8,128)(2,1)S(1)}, u32[]{:S(2)}, u32[]{:S(2)}) collective-permute-start(bf16[48,3584]{1,0:T(8,128)(2,1)S(1)} %get-tuple-element.17), channel_id=1, source_target_pairs={{0,1},{1,0},{2,3},{3,2},{4,5},{5,4},{6,7},{7,6},{8,9},{9,8},{10,11... | collective-permute-start | bytes 1032200 | tf_op jit(solution)/shard_map/ppermute | solution.py:35
  137.2 14.3 %all-to-all-start.2 = ((bf16[16,32,384]{2,1,0:T(8,128)(2,1)}), bf16[16,32,384]{2,1,0:T(8,128)(2,1)S(1)}, u32[]{:S(2)}, u32[]{:S(2)}) async-start(bf16[16,32,384]{2,1,0:T(8,128)(2,1)} %bitcast.19), calls=%async_computation.2 | async-start | bytes 786432 | tf_op jit(solution)/shard_map/all_to_all | solution.py:304
  153.5 33.5 %all-to-all-start.3 = ((bf16[16,32,2048]{2,1,0:T(8,128)(2,1)}), bf16[16,32,2048]{2,1,0:T(8,128)(2,1)}, u32[]{:S(2)}, u32[]{:S(2)}) async-start(bf16[16,32,2048]{2,1,0:T(8,128)(2,1)} %bitcast.27), calls=%async_computation.3 | async-start | bytes 4194304 | tf_op jit(solution)/shard_map/all_to_all | solution.py:304
  161.7 12.1 %collective-permute-start.20 = (bf16[512,384]{1,0:T(8,128)(2,1)S(1)}, bf16[512,384]{1,0:T(8,128)(2,1)S(1)}, u32[]{:S(2)}, u32[]{:S(2)}) collective-permute-start(bf16[512,384]{1,0:T(8,128)(2,1)S(1)} %bitcast.130), channel_id=1, source_target_pairs={{2,0},{4,2},{6,4},{0,6},{3,1},{5,3},{7,5},{1,7},{10,8},{12,10},{14... | collective-permute-start | bytes 1179656 | tf_op jit(solution)/shard_map/ppermute | solution.py:27
  163.8 13.6 %collective-permute-start.21 = (bf16[512,384]{1,0:T(8,128)(2,1)S(1)}, bf16[512,384]{1,0:T(8,128)(2,1)S(1)}, u32[]{:S(2)}, u32[]{:S(2)}) collective-permute-start(bf16[512,384]{1,0:T(8,128)(2,1)S(1)} %bitcast.131), channel_id=1, source_target_pairs={{4,0},{6,2},{0,4},{2,6},{5,1},{7,3},{1,5},{3,7},{12,8},{14,10},{8,... | collective-permute-start | bytes 1179656 | tf_op jit(solution)/shard_map/ppermute | solution.py:27
  164.4 19.0 %collective-permute-start.22 = (bf16[512,384]{1,0:T(8,128)(2,1)S(1)}, bf16[512,384]{1,0:T(8,128)(2,1)S(1)}, u32[]{:S(2)}, u32[]{:S(2)}) collective-permute-start(bf16[512,384]{1,0:T(8,128)(2,1)S(1)} %bitcast.132), channel_id=1, source_target_pairs={{6,0},{0,2},{2,4},{4,6},{7,1},{1,3},{3,5},{5,7},{14,8},{8,10},{10,... | collective-permute-start | bytes 1179656 | tf_op jit(solution)/shard_map/ppermute | solution.py:27
  185.2 3.8 %collective-permute-start.23 = (bf16[512,1536]{1,0:T(8,128)(2,1)}, bf16[512,1536]{1,0:T(8,128)(2,1)}, u32[]{:S(2)}, u32[]{:S(2)}) collective-permute-start(bf16[512,1536]{1,0:T(8,128)(2,1)} %constant_dynamic-slice_fusion.6), channel_id=1, source_target_pairs={{0,1},{1,0},{2,3},{3,2},{4,5},{5,4},{6,7},{7,6},{8,9},{9,8},{10,11... | collective-permute-start | bytes 4718600 | tf_op jit(solution)/shard_map/ppermute | solution.py:35
  187.0 7.8 %collective-permute-start.24 = (bf16[512,2048]{1,0:T(8,128)(2,1)}, bf16[512,2048]{1,0:T(8,128)(2,1)S(1)}, u32[]{:S(2)}, u32[]{:S(2)}) collective-permute-start(bf16[512,2048]{1,0:T(8,128)(2,1)} %bitcast.28), channel_id=1, source_target_pairs={{0,1},{1,0},{2,3},{3,2},{4,5},{5,4},{6,7},{7,6},{8,9},{9,8},{10,11... | collective-permute-start | bytes 6291464 | tf_op jit(solution)/shard_map/ppermute | solution.py:35
  199.7 8.4 %collective-permute-start.26 = (bf16[512,2048]{1,0:T(8,128)(2,1)S(1)}, bf16[512,2048]{1,0:T(8,128)(2,1)S(1)}, u32[]{:S(2)}, u32[]{:S(2)}) collective-permute-start(bf16[512,2048]{1,0:T(8,128)(2,1)S(1)} %convolution_convert_fusion), channel_id=1, source_target_pairs={{0,1},{1,0},{2,3},{3,2},{4,5},{5,4},{6,7},{7,6},{8,9},{9,8},{10,11... | collective-permute-start | bytes 6291464 | tf_op jit(solution)/shard_map/ppermute | solution.py:35
  200.3 6.0 %copy-start.25 = (bf16[256,384]{1,0:T(8,128)(2,1)S(1)}, bf16[256,384]{1,0:T(8,128)(2,1)}, u32[]{:S(2)}) copy-start(bf16[256,384]{1,0:T(8,128)(2,1)} %get-tuple-element.28) | copy-start | bytes 589828
  200.9 5.4 %collective-permute-start.25 = (bf16[512,1536]{1,0:T(8,128)(2,1)S(1)}, bf16[512,1536]{1,0:T(8,128)(2,1)S(1)}, u32[]{:S(2)}, u32[]{:S(2)}) collective-permute-start(bf16[512,1536]{1,0:T(8,128)(2,1)S(1)} %convolution_convert_fusion.1), channel_id=1, source_target_pairs={{0,1},{1,0},{2,3},{3,2},{4,5},{5,4},{6,7},{7,6},{8,9},{9,8},{10,11... | collective-permute-start | bytes 4718600 | tf_op jit(solution)/shard_map/ppermute | solution.py:35
  210.2 39.6 %all-to-all-start.4 = ((bf16[16,32,2048]{2,1,0:T(8,128)(2,1)}), bf16[16,32,2048]{2,1,0:T(8,128)(2,1)S(1)}, u32[]{:S(2)}, u32[]{:S(2)}) async-start(bf16[16,32,2048]{2,1,0:T(8,128)(2,1)} %bitcast.135), calls=%async_computation.4 | async-start | bytes 4194304 | tf_op jit(solution)/shard_map/all_to_all | solution.py:351
  223.4 13.6 %collective-permute-start.27 = (bf16[512,384]{1,0:T(8,128)(2,1)S(1)}, bf16[512,384]{1,0:T(8,128)(2,1)S(1)}, u32[]{:S(2)}, u32[]{:S(2)}) collective-permute-start(bf16[512,384]{1,0:T(8,128)(2,1)S(1)} %get-tuple-element.44), channel_id=1, source_target_pairs={{0,4},{2,6},{4,0},{6,2},{1,5},{3,7},{5,1},{7,3},{8,12},{10,14},{12... | collective-permute-start | bytes 1179656 | tf_op jit(solution)/shard_map/ppermute | solution.py:31
  224.1 20.2 %collective-permute-start.28 = (bf16[512,384]{1,0:T(8,128)(2,1)S(1)}, bf16[512,384]{1,0:T(8,128)(2,1)S(1)}, u32[]{:S(2)}, u32[]{:S(2)}) collective-permute-start(bf16[512,384]{1,0:T(8,128)(2,1)S(1)} %get-tuple-element.45), channel_id=1, source_target_pairs={{0,2},{2,4},{4,6},{6,0},{1,3},{3,5},{5,7},{7,1},{8,10},{10,12},{12... | collective-permute-start | bytes 1179656 | tf_op jit(solution)/shard_map/ppermute | solution.py:31
  225.0 19.3 %collective-permute-start.29 = (bf16[512,384]{1,0:T(8,128)(2,1)S(1)}, bf16[512,384]{1,0:T(8,128)(2,1)S(1)}, u32[]{:S(2)}, u32[]{:S(2)}) collective-permute-start(bf16[512,384]{1,0:T(8,128)(2,1)S(1)} %get-tuple-element.46), channel_id=1, source_target_pairs={{0,6},{2,0},{4,2},{6,4},{1,7},{3,1},{5,3},{7,5},{8,14},{10,8},{12,... | collective-permute-start | bytes 1179656 | tf_op jit(solution)/shard_map/ppermute | solution.py:31
  250.4 17.8 %copy-start.1 = (bf16[16,512,128]{2,1,0:T(8,128)(2,1)S(1)}, bf16[16,512,128]{2,1,0:T(8,128)(2,1)}, u32[]{:S(2)}) copy-start(bf16[16,512,128]{2,1,0:T(8,128)(2,1)} %param.19) | copy-start | bytes 6291460
  250.5 9.6 %collective-permute-start.30 = (bf16[48,512]{1,0:T(8,128)(2,1)S(1)}, bf16[48,512]{1,0:T(8,128)(2,1)S(1)}, u32[]{:S(2)}, u32[]{:S(2)}) collective-permute-start(bf16[48,512]{1,0:T(8,128)(2,1)S(1)} %get-tuple-element.54), channel_id=1, source_target_pairs={{0,4},{2,6},{4,0},{6,2},{1,5},{3,7},{5,1},{7,3},{8,12},{10,14},{12... | collective-permute-start | bytes 147464 | tf_op jit(solution)/shard_map/ppermute | solution.py:31
  251.2 9.0 %collective-permute-start.31 = (bf16[48,512]{1,0:T(8,128)(2,1)S(1)}, bf16[48,512]{1,0:T(8,128)(2,1)S(1)}, u32[]{:S(2)}, u32[]{:S(2)}) collective-permute-start(bf16[48,512]{1,0:T(8,128)(2,1)S(1)} %get-tuple-element.55), channel_id=1, source_target_pairs={{0,2},{2,4},{4,6},{6,0},{1,3},{3,5},{5,7},{7,1},{8,10},{10,12},{12... | collective-permute-start | bytes 147464 | tf_op jit(solution)/shard_map/ppermute | solution.py:31
  252.1 8.1 %collective-permute-start.32 = (bf16[48,512]{1,0:T(8,128)(2,1)S(1)}, bf16[48,512]{1,0:T(8,128)(2,1)S(1)}, u32[]{:S(2)}, u32[]{:S(2)}) collective-permute-start(bf16[48,512]{1,0:T(8,128)(2,1)S(1)} %get-tuple-element.56), channel_id=1, source_target_pairs={{0,6},{2,0},{4,2},{6,4},{1,7},{3,1},{5,3},{7,5},{8,14},{10,8},{12,... | collective-permute-start | bytes 147464 | tf_op jit(solution)/shard_map/ppermute | solution.py:31
  254.4 12.9 %all-to-all-start.5 = ((bf16[16,32,384]{2,1,0:T(8,128)(2,1)}), bf16[16,32,384]{2,1,0:T(8,128)(2,1)S(1)}, u32[]{:S(2)}, u32[]{:S(2)}) async-start(bf16[16,32,384]{2,1,0:T(8,128)(2,1)} %bitcast.51), calls=%async_computation.5 | async-start | bytes 786432 | tf_op jit(solution)/shard_map/all_to_all | solution.py:351
  (28 other events, 72.1 us)

commit v4 on v3

--- a/solution.py
+++ b/solution.py
@@ -1,3 +1,5 @@
+import functools
+
 import jax
 import jax.numpy as jnp
 from jax import lax
@@ -91,83 +93,255 @@
 
 
 def attend_kernel(
-    me_ref, page_ref, held_ref, taken_ref, told_ref, own_ref, far_ref, pool_ref, out_ref,
-    which_ref, list_ref, seen_ref,
+    me_ref, page_ref, held_ref, taken_ref, told_ref, query_ref, pool_ref, out_ref,
+    which_ref, list_ref, seen_ref, keys_ref, held_pool_ref, sems, own,
 ):
     me = me_ref[0]
-    count, rows, width = own_ref.shape
+    count, rows, _ = query_ref.shape
+    page_rows, width, pages = pool_ref.shape
+    chunks = sems.shape[0]
+    size = page_rows // chunks
+    copies = [
+        pltpu.make_async_copy(
+            pool_ref.at[pl.ds(n * size, size)], held_pool_ref.at[pl.ds(n * size, size)], sems.at[n]
+        )
+        for n in range(chunks)
+    ]
+    for copy in copies:
+        copy.start()
     per = page_ref.shape[1]
-
-    def plan(r, found):
-        own_at, far_at = found
-        mine = page_ref[r, 0] // PAGES == me
-        lent = told_ref[r, 10] > 0
-
-        @pl.when(mine)
+    slots = count // 2
+
+    def plan(r, at):
+        found = page_ref[r, 0] // PAGES == me if own else told_ref[r, 10] > 0
+        spot = jnp.minimum(at, slots - 1)
+
+        @pl.when(found)
         def _():
-            at = jnp.minimum(own_at, 7)
-            which_ref[at] = r
-            seen_ref[at] = held_ref[r] + taken_ref[r]
+            which_ref[spot] = r
+            if own:
+                seen_ref[spot] = held_ref[r] + taken_ref[r]
+            else:
+                seen_ref[spot] = told_ref[r, 8] * 2 + told_ref[r, 9]
             for k in range(per):
-                list_ref[at * per + k] = page_ref[r, k] - me * PAGES
-
-        @pl.when(lent)
-        def _():
-            at = 8 + jnp.minimum(far_at, 7)
-            which_ref[at] = r
-            seen_ref[at] = told_ref[r, 8] * 2 + told_ref[r, 9]
-            for k in range(per):
-                list_ref[at * per + k] = told_ref[r, k]
-
-        return own_at + mine.astype(i32), far_at + lent.astype(i32)
-
-    lax.fori_loop(0, count, plan, (jnp.int32(0), jnp.int32(0)))
-
-    def one(at, source):
-        queries = source[which_ref[at], :, :width]
-        keys = jnp.concatenate([pool_ref[list_ref[at * per + k]] for k in range(per)], axis=0)
+                list_ref[spot * per + k] = page_ref[r, k] - me * PAGES if own else told_ref[r, k]
+
+        return at + found.astype(i32)
+
+    lax.fori_loop(0, count, plan, jnp.int32(0))
+    row = lax.broadcasted_iota(i32, (slots * per, pages), 0)
+    lane = lax.broadcasted_iota(i32, (slots * per, pages), 1)
+    wanted = jnp.zeros((slots * per, pages), i32)
+    for n in range(slots * per):
+        wanted = jnp.where(row == n, list_ref[n], wanted)
+    order = jnp.where(wanted == lane, 1.0, 0.0).astype(bf16)
+
+    def sort(i, carry):
+        sorted_rows = lax.dot_general(
+            order, held_pool_ref[i], (((1,), (1,)), ((), ())), preferred_element_type=f32
+        ).astype(bf16)
+        for pair in range(slots // 2):
+            keys_ref[pair, pl.ds(pl.multiple_of(i * 16, 16), 16), :] = sorted_rows[
+                pair * 16 : (pair + 1) * 16
+            ]
+        return carry
+
+    for n in range(chunks):
+        copies[n].wait()
+        lax.fori_loop(n * size, (n + 1) * size, sort, 0, unroll=True)
+    keys_at = lax.broadcasted_iota(i32, (2 * rows, page_rows * 16), 1)
+    query_at = lax.broadcasted_iota(i32, (2 * rows, page_rows * 16), 0)
+    position = keys_at % 8 * page_rows + keys_at // 16
+    second = query_at >= rows
+    same = (keys_at // 8 % 2 == 1) == second
+    draft = jnp.where(second, query_at - rows, query_at) // (rows // 3)
+    offset = jnp.where(same, position - draft, 1 << 20)
+    for pair in range(slots // 2):
+        queries = jnp.concatenate(
+            [query_ref[which_ref[2 * pair + n], :, :width] for n in range(2)], axis=0
+        )
+        keys = keys_ref[pair]
         scores = (
             lax.dot_general(queries, keys, (((1,), (1,)), ((), ())), preferred_element_type=f32)
             * softmax_scale
         )
-        position = lax.broadcasted_iota(i32, scores.shape, 1)
-        draft = lax.broadcasted_iota(i32, scores.shape, 0) // (scores.shape[0] // 3)
-        allowed = position <= seen_ref[at] + draft
+        allowed = offset <= jnp.where(second, seen_ref[2 * pair + 1], seen_ref[2 * pair])
         highest = jnp.max(jnp.where(allowed, scores, -1e30), axis=-1, keepdims=True)
         weights = jnp.where(allowed, jnp.exp(jnp.where(allowed, scores - highest, 0.0)), 0.0)
         probs = (weights / jnp.sum(weights, axis=-1, keepdims=True)).astype(bf16)
-        out_ref[at] = lax.dot_general(
+        latent = lax.dot_general(
             probs, keys[:, :LAT], (((1,), (0,)), ((), ())), preferred_element_type=f32
         ).astype(bf16)
-
-    def turn(i, carry):
-        one(i, own_ref)
-        one(8 + i, far_ref)
-        return carry
-
-    lax.fori_loop(0, 8, turn, 0)
-
-
-def attend(me, page_table, cache_len, accepted, told, own_queries, far_queries, kv_pool):
-    count, rows, width = own_queries.shape
-    per = page_table.shape[1]
+        out_ref[2 * pair] = latent[:rows]
+        out_ref[2 * pair + 1] = latent[rows:]
+
+
+def attend(own, me, page_table, cache_len, accepted, told, queries, pool):
+    count, rows, _ = queries.shape
+    page_rows, width, pages = pool.shape
+    per, slots = page_table.shape[1], count // 2
     scalar, vector = (pl.BlockSpec(memory_space=m) for m in (pltpu.SMEM, pltpu.VMEM))
     return pl.pallas_call(
-        attend_kernel,
-        out_shape=jax.ShapeDtypeStruct((count, rows, LAT), bf16),
-        in_specs=[scalar] * 5 + [vector] * 3,
+        functools.partial(attend_kernel, own=own),
+        out_shape=jax.ShapeDtypeStruct((slots, rows, LAT), bf16),
+        in_specs=[scalar] * 5 + [vector, pl.BlockSpec(memory_space=pl.ANY)],
         out_specs=vector,
         scratch_shapes=[
-            pltpu.SMEM((count,), i32),
-            pltpu.SMEM((count * per,), i32),
-            pltpu.SMEM((count,), i32),
+            pltpu.SMEM((slots,), i32),
+            pltpu.SMEM((slots * per,), i32),
+            pltpu.SMEM((slots,), i32),
+            pltpu.VMEM((slots // 2, page_rows * 16, width), bf16),
+            pltpu.VMEM((page_rows, width, pages), bf16),
+            pltpu.SemaphoreType.DMA((4,)),
         ],
-        compiler_params=pltpu.CompilerParams(vmem_limit_bytes=40 * 2**20),
+        compiler_params=pltpu.CompilerParams(vmem_limit_bytes=56 * 2**20),
         cost_estimate=pl.CostEstimate(
-            flops=count * rows * 512 * 1088 * 2, bytes_accessed=12_000_000, transcendentals=0
+            flops=4_000_000_000, bytes_accessed=12_000_000, transcendentals=0
         ),
-        name="attend",
-    )(me, page_table, cache_len, accepted, told, own_queries, far_queries, kv_pool)
+        name="attend_own" if own else "attend_far",
+    )(me, page_table, cache_len, accepted, told, queries, pool)
+
+
+def home_kernel(
+    spot_ref, here_ref, there_ref, gain_ref, placing_ref, attended_ref, early_ref, late_ref
+):
+    wide = here_ref.shape[1] // RING
+    cut, rest = early_ref.shape[1], late_ref.shape[1] // RING
+    here, there = here_ref[...], there_ref[...]
+    for k in range(RING):
+        for side, block in enumerate((here, there)):
+            start = pl.multiple_of(spot_ref[side * RING + k] * wide, 128)
+            attended_ref[:, pl.ds(start, wide)] = block[:, k * wide : (k + 1) * wide]
+    rows, rows_there = here.astype(f32), there.astype(f32)
+    squares = jnp.sum(rows * rows, axis=1, keepdims=True) + jnp.sum(
+        rows_there * rows_there, axis=1, keepdims=True
+    )
+    root = lax.rsqrt(squares / attended_ref.shape[1] + norm_eps)
+    normed = (rows * root * gain_ref[...]).astype(bf16)
+    placing = placing_ref[...]
+    early_ref[...] = jnp.dot(placing, normed[:, :cut], preferred_element_type=f32).astype(bf16)
+    for k in range(RING):
+        late_ref[:, k * rest : (k + 1) * rest] = jnp.dot(
+            placing, normed[:, k * wide + cut : (k + 1) * wide], preferred_element_type=f32
+        ).astype(bf16)
+
+
+def home_rows(spots, here, there, gains, placing, cut):
+    tokens, half = here.shape
+    slots = placing.shape[0]
+    vector = pl.BlockSpec(memory_space=pltpu.VMEM)
+    return pl.pallas_call(
+        home_kernel,
+        out_shape=[
+            jax.ShapeDtypeStruct((tokens, 2 * half), bf16),
+            jax.ShapeDtypeStruct((slots, cut), bf16),
+            jax.ShapeDtypeStruct((slots, half - RING * cut), bf16),
+        ],
+        in_specs=[pl.BlockSpec(memory_space=pltpu.SMEM)] + [vector] * 4,
+        out_specs=[vector] * 3,
+        compiler_params=pltpu.CompilerParams(vmem_limit_bytes=32 * 2**20),
+        name="home_rows",
+    )(spots, here, there, gains, placing)
+
+
+def enter_kernel(spot_ref, early_ref, late_ref, gate_ref, up_ref, *refs):
+    out_ref, sum_ref = refs[-2:]
+    units = gate_ref.shape[2]
+    cut = early_ref.shape[1]
+
+    @pl.when(pl.program_id(0) == 0)
+    def _():
+        sum_ref[...] = refs[0][...] if len(refs) == 3 else jnp.zeros_like(sum_ref)
+
+    for n, weights in enumerate((gate_ref, up_ref)):
+        sum_ref[:, n * units : (n + 1) * units] += jnp.dot(
+            early_ref[...], weights[0, :cut], preferred_element_type=f32
+        ) + jnp.dot(late_ref[...], weights[0, cut:], preferred_element_type=f32)
+
+    @pl.when(pl.program_id(0) == RING - 1)
+    def _():
+        if len(refs) == 3:
+            gate = sum_ref[:, :units]
+            out_ref[...] = (gate / (1.0 + jnp.exp(-gate)) * sum_ref[:, units:]).astype(bf16)
+        else:
+            out_ref[...] = sum_ref[...]
+
+
+def enter(spots, early, late, w_gate, w_up, so_far=None):
+    slots = early.shape[0]
+    cut, rest = early.shape[1] // RING, late.shape[1] // RING
+    units = w_gate.shape[2]
+    weights = pl.BlockSpec((1, cut + rest, units), lambda i, spot: (0, spot[i], 0))
+    more = [] if so_far is None else [so_far]
+    whole = pl.BlockSpec((slots, 2 * units), lambda i, spot: (0, 0))
+    spec = pltpu.PrefetchScalarGridSpec(
+        num_scalar_prefetch=1,
+        grid=(RING,),
+        in_specs=[
+            pl.BlockSpec((slots, cut), lambda i, spot: (0, i)),
+            pl.BlockSpec((slots, rest), lambda i, spot: (0, i)),
+            weights,
+            weights,
+        ]
+        + [whole] * len(more),
+        out_specs=pl.BlockSpec((slots, units if more else 2 * units), lambda i, spot: (0, 0)),
+        scratch_shapes=[pltpu.VMEM((slots, 2 * units), f32)],
+    )
+    return pl.pallas_call(
+        enter_kernel,
+        out_shape=jax.ShapeDtypeStruct(
+            (slots, units if more else 2 * units), bf16 if more else f32
+        ),
+        grid_spec=spec,
+        compiler_params=pltpu.CompilerParams(vmem_limit_bytes=56 * 2**20),
+        cost_estimate=pl.CostEstimate(
+            flops=4 * slots * units * RING * (cut + rest), bytes_accessed=8_000_000, transcendentals=0
+        ),
+        name="enter_last" if more else "enter_first",
+    )(spots, early, late, w_gate, w_up, *more)
+
+
+def leave_kernel(spot_ref, hidden_ref, down_ref, *refs):
+    early_ref, late_ref = refs[-2:]
+    cut = early_ref.shape[1]
+    rows = jnp.dot(hidden_ref[...], down_ref[0], preferred_element_type=f32)
+    early, late = rows[:, :cut], rows[:, cut:]
+    if len(refs) == 4:
+        early, late = early + refs[0][...].astype(f32), late + refs[1][...].astype(f32)
+    early_ref[...] = early.astype(bf16)
+    late_ref[...] = late.astype(bf16)
+
+
+def leave(spots, hidden, w_down, cut, *more):
+    slots, units = hidden.shape
+    rest = w_down.shape[2] // HEAD_N - cut
+    sides = [
+        pl.BlockSpec((slots, cut), lambda i, spot: (0, i)),
+        pl.BlockSpec((slots, rest), lambda i, spot: (0, i)),
+    ]
+    spec = pltpu.PrefetchScalarGridSpec(
+        num_scalar_prefetch=1,
+        grid=(RING,),
+        in_specs=[
+            pl.BlockSpec((slots, units), lambda i, spot: (0, 0)),
+            pl.BlockSpec((1, units, cut + rest), lambda i, spot: (0, 0, spot[i])),
+        ]
+        + sides[: len(more)],
+        out_specs=sides,
+    )
+    return pl.pallas_call(
+        leave_kernel,
+        out_shape=[
+            jax.ShapeDtypeStruct((slots, RING * cut), bf16),
+            jax.ShapeDtypeStruct((slots, RING * rest), bf16),
+        ],
+        grid_spec=spec,
+        compiler_params=pltpu.CompilerParams(vmem_limit_bytes=56 * 2**20),
+        cost_estimate=pl.CostEstimate(
+            flops=2 * slots * units * RING * (cut + rest), bytes_accessed=8_000_000, transcendentals=0
+        ),
+        name="leave_last" if more else "leave_first",
+    )(spots, hidden, w_down, *more)
 
 
 def before(count):
@@ -205,7 +379,14 @@
     told = arrived[:, 0, width:]
     lenders = told[:, 24:40].astype(i32)
     line = told[:, 8:24].astype(i32)
-    latent = attend(me, page_table, cache_len, accepted, line, query_rows, arrived, kv_pool)
+    pool = kv_pool.transpose(1, 2, 0)
+    tables = (me, page_table, cache_len, accepted)
+    latent = jnp.concatenate(
+        [
+            attend(True, *tables, jnp.zeros((DP_N, 16), i32), query_rows, pool),
+            attend(False, *tables, line, arrived, pool),
+        ]
+    )
     values = jnp.einsum(
         "thc,hcv->thv",
         latent.reshape(tokens, head_group, LAT),
@@ -264,22 +445,10 @@
 
     here = jnp.concatenate([piece] + [hop(piece, "x", k) for k in (1, 2, 3)], axis=1)
     there = other_core(here)
-    wide, wide_there = here.astype(f32), there.astype(f32)
-    squares = jnp.sum(wide * wide, axis=1, keepdims=True) + jnp.sum(
-        wide_there * wide_there, axis=1, keepdims=True
-    )
+    ring_at = (at_x + jnp.arange(RING, dtype=i32)) % RING * 2
+    spots_here, spots_there = ring_at + at_core, ring_at + 1 - at_core
     gains = jnp.concatenate([norm_gain, norm_gain]).reshape(2 * RING, 2, wide_piece)
     gains = lax.dynamic_slice(gains, (at_x, at_core, 0), (RING, 1, wide_piece)).reshape(1, -1)
-    model = residual.shape[1]
-    normed = (wide * lax.rsqrt(squares / model + norm_eps) * gains).astype(bf16)
-    first = jnp.where(at_core == 0, here, there)
-    second = jnp.where(at_core == 0, there, here)
-    blocks = []
-    for k in range(RING):
-        for side in (first, second):
-            blocks.append(side[:, k * wide_piece : (k + 1) * wide_piece])
-    row = jnp.concatenate(blocks + blocks, axis=1)
-    attended = lax.dynamic_slice_in_dim(row, (RING - at_x) % RING * 2 * wide_piece, model, 1)
 
     chosen = (expert_ids[:, :, None] == dps[None, None, :]).astype(i32)
     named = jnp.sum(chosen, axis=1)
@@ -291,79 +460,34 @@
     placing = placing.reshape(DP_N * CAP, tokens)
 
     cut = 3 * wide_piece // 7
-    early = normed[:, :cut]
-    doubled = [normed[:, k * wide_piece + cut : (k + 1) * wide_piece] for k in range(RING)]
     rest = wide_piece - cut
-    back = (RING - at_x) % RING
-    late = lax.dynamic_slice_in_dim(
-        jnp.concatenate(doubled + doubled, axis=1), back * rest, RING * rest, 1
-    )
-
-    def to_experts(block):
-        block = jnp.dot(placing, block, preferred_element_type=f32).astype(bf16)
+    attended, early, late = home_rows(
+        jnp.concatenate([spots_here, spots_there]), here, there, gains, placing, cut
+    )
+
+    def exchange(block):
         block = lax.all_to_all(block.reshape(DP_N, CAP, -1), DP, 0, 0, tiled=True)
         return block.reshape(DP_N * CAP, -1)
 
-    early = to_experts(early)
+    early = exchange(early)
     early, late = lax.optimization_barrier((early, late))
-    late = to_experts(late)
-    early = [early] + [hop(early, "x", k) for k in (1, 2, 3)]
-    early = lax.dynamic_slice_in_dim(
-        jnp.concatenate(early + early, axis=1), back * cut, RING * cut, 1
-    )
-
-    def in_rows(core, low, high):
-        blocks = []
-        for weights in (w_gate, w_up):
-            view = weights[0].reshape(RING, 2, wide_piece, -1)
-            view = lax.dynamic_slice_in_dim(view, core, 1, 1)[:, 0, low:high]
-            blocks.append(view.reshape(RING * (high - low), -1))
-        return jnp.concatenate(blocks, axis=1)
-
-    def out_columns(core, low, high):
-        return jnp.concatenate(
-            [
-                lax.dynamic_slice_in_dim(
-                    w_down[0], (2 * k + core) * wide_piece + low, high - low, 1
-                )
-                for k in range(RING)
-            ],
-            axis=1,
-        )
-
-    units = w_gate.shape[2]
-    away = 1 - at_core
-    sums = (
-        jnp.dot(early, in_rows(at_core, 0, cut), preferred_element_type=f32)
-        + jnp.dot(other_core(early), in_rows(away, 0, cut), preferred_element_type=f32)
-        + jnp.dot(late, in_rows(at_core, cut, wide_piece), preferred_element_type=f32)
-        + jnp.dot(other_core(late), in_rows(away, cut, wide_piece), preferred_element_type=f32)
-    )
-    hidden = (jax.nn.silu(sums[:, :units]) * sums[:, units:]).astype(bf16)
-    hidden = lax.optimization_barrier(hidden)
-
-    def output(low, high):
-        give = jnp.dot(hidden, out_columns(away, low, high), preferred_element_type=f32)
-        keep = jnp.dot(hidden, out_columns(at_core, low, high), preferred_element_type=f32)
-        return keep + other_core(give.astype(bf16)).astype(f32)
-
-    def to_home(block):
-        block = lax.all_to_all(block.reshape(DP_N, CAP, -1), DP, 0, 0, tiled=True)
-        return block.reshape(DP_N * CAP, -1)
+    late = exchange(late)
+    early = jnp.concatenate([early] + [hop(early, "x", k) for k in (1, 2, 3)], axis=1)
+
+    sums = enter(spots_here, early, late, w_gate, w_up)
+    hidden = enter(spots_there, other_core(early), other_core(late), w_gate, w_up, sums)
+    give = leave(spots_there, hidden, w_down, cut)
+    early, late = leave(spots_here, hidden, w_down, cut, *[other_core(a) for a in give])
 
     def ring_sum(block, size):
-        block = jnp.concatenate([block, block], axis=1)
-        block = lax.dynamic_slice_in_dim(block, at_x * size, RING * size, 1)
         total = block[:, :size].astype(f32)
         for k in (2, 1, 3):
             total = total + send(block[:, k * size : (k + 1) * size], "x", k).astype(f32)
         return total
 
-    late = output(cut, wide_piece).astype(bf16)
-    early, late = lax.optimization_barrier((output(0, cut).astype(bf16), late))
-    late = to_home(late)
+    late = exchange(late)
     early, late = lax.optimization_barrier((ring_sum(early, cut).astype(bf16), late))
-    early = to_home(early)
+    early = exchange(early)
 
     mix = jnp.where(rank[:, :, None] == ranks[None, None, :], weight[:, :, None], 0.0)
     mix = mix.reshape(tokens, DP_N * CAP)

time: 269 us -> 278 us (1.033)
  Pallas kernels: 13.6 us -> 54.3 us
  local copies, waits for them, and re-layouts: 52.4 us -> 13.3 us
  waiting for transfers between devices: 87.3 us -> 111 us
  matrix products: 25 us -> 9.14 us
  starting transfers between devices: 80.2 us -> 66.1 us
  blocking collectives: 0 us -> 13.5 us
    pallas_call x1 -> x7, Pallas kernels: 11.3 us -> 51.1 us  [the longest x2 21.9 us: attend(): pl.pallas_call(functools.partial(attend_kernel, own=own), out_shape=jax.S...]
    unnamed x106 -> x47, local copies, waits for them, and re-layouts: 35 us -> 9.78 us
    dot_general x10 -> x0, matrix products: 17.6 us -> none  [the longest x2 3.81 us: output(): jnp.dot(hidden, out_columns(at_core, low, high), preferred_element_type=f32)]
    all_to_all x0 -> x1, blocking collectives: none -> 13.5 us  [exchange(): block = lax.all_to_all(block.reshape(DP_N, CAP, -1), DP, 0, 0, tiled=True)]
    all_to_all x4 -> x3, waiting for transfers between devices: 24 us -> 35.7 us  [exchange(): block = lax.all_to_all(block.reshape(DP_N, CAP, -1), DP, 0, 0, tiled=True)]
    slice x2 -> x0, local copies, waits for them, and re-layouts: 8.05 us -> none  [in_rows(): view = lax.dynamic_slice_in_dim(view, core, 1, 1)[:, 0, low:high]]
    ppermute x6, waiting for transfers between devices: 2.05 us -> 8.9 us  [other_core(): return lax.ppermute(array, 'core', [(0, 1), (1, 0)])]
    all_to_all x4 -> x3, starting transfers between devices: 20.2 us -> 13.4 us  [exchange(): block = lax.all_to_all(block.reshape(DP_N, CAP, -1), DP, 0, 0, tiled=True)]
  transfers between devices with their start and end apart: 39 -> 38, of which waited for: 22 -> 24; matrix products, arithmetic and copies ran while one was open for 22% -> 5% of each run, Pallas kernels for 0% -> 6%
where the time goes in v4:
time: 278 us; the launch traced here: 277 us
  waiting for transfers between devices  111 us (40%)
  starting transfers between devices  66.1 us (24%)
  Pallas kernels  54.3 us (20%)
  blocking collectives  13.5 us (5%)
  local copies, waits for them, and re-layouts  13.3 us (5%)
  matrix products  9.14 us (3%)
  other arithmetic  8.34 us (3%)
    all_to_all x3, waiting for transfers between devices, exchange(): block = lax.all_to_all(block.reshape(DP_N, CAP, -1), DP, 0, 0, tiled=True)  35.7 us
    ppermute x18, waiting for transfers between devices, hop(): lax.ppermute(array, axis, [((i + step) % RING, i) for i in range(RING)])  28 us
    ppermute x18, starting transfers between devices, hop(): lax.ppermute(array, axis, [((i + step) % RING, i) for i in range(RING)])  22.2 us
    pallas_call x2, Pallas kernels, attend(): pl.pallas_call(functools.partial(attend_kernel, own=own), out_shape=jax.S...  21.9 us
    ppermute x9, waiting for transfers between devices, send(): lax.ppermute(array, axis, [(i, (i + step) % RING) for i in range(RING)])  21.8 us
    pallas_call x2, Pallas kernels, enter(): pl.pallas_call(enter_kernel, out_shape=jax.ShapeDtypeStruct((slots, units...  14.4 us
    all_to_all x1, blocking collectives, exchange(): block = lax.all_to_all(block.reshape(DP_N, CAP, -1), DP, 0, 0, tiled=True)  13.5 us
    all_to_all x3, starting transfers between devices, exchange(): block = lax.all_to_all(block.reshape(DP_N, CAP, -1), DP, 0, 0, tiled=True)  13.4 us
  transfers between devices with their start and end apart: 38, of which 24 were waited for; matrix products, arithmetic and copies ran while one was open for 5% of the time, Pallas kernels for 6%

profile of v4, /device:TPU:0, one launch (start us, length us, event | category | flops | bytes accessed | tf_op | source)
XLA Modules:
  0.0 277.1 jit_solution(12012023697484669583)
XLA Ops:
  1.6 1.2 copy-done.2
  4.1 3.2 %pack.1 = bf16[16,48,640]{2,1,0:T(8,128)(2,1)} custom-call(s32[1]{0:T(128)} %bitcast.me_ref, s32[16,8]{1,0:T(8,128)S(1)} %copy.36.page_ref, s32[16]{0:T(128)S(1)} %copy-done.4, s32[16]{0:T(128)S(1)} %copy-done.5, bf16[16,48,576]{2,1,0:T(8,128)(2,1)S(1)} %bitcast.75), custom_call_target="tpu_custom_call" | custom-call | tf_op jit(solution)/shard_map/pack/pallas_call | solution.py:84
  7.3 8.1 %all-to-all-start = ((bf16[16,48,640]{2,1,0:T(8,128)(2,1)}), bf16[16,48,640]{2,1,0:T(8,128)(2,1)S(1)}, u32[]{:S(2)}, u32[]{:S(2)}) async-start(bf16[16,48,640]{2,1,0:T(8,128)(2,1)} %pack.1), calls=%async_computation | async-start | bytes 1966080 | tf_op jit(solution)/shard_map/all_to_all | solution.py:378
  16.1 10.9 %attend_own.1 = bf16[8,48,512]{2,1,0:T(8,128)(2,1)} custom-call(s32[1]{0:T(128)} %bitcast.me_ref, s32[16,8]{1,0:T(8,128)} %copy-done.3, s32[16]{0:T(128)} %held_ref.5, s32[16]{0:T(128)} %taken_ref.5, s32[16,16]{1,0:T(8,128)} %broadcast.94.told_ref, bf16[16,48,576]{2,1,0:T(8,128)(2,1)} %bitcast.74, bf16[64,576,128]{2,1,0:T(8,128)(2,1)} %bitcast.95), custom_call_target="tpu_custom_call" | custom-call | flops 4000000000 | bytes 12000000 | tf_op jit(solution)/shard_map/attend_own/pallas_call | solution.py:184
  27.0 5.3 %all-to-all-done.query_ref = bf16[16,48,640]{2,1,0:T(8,128)(2,1)S(1)} async-done(((bf16[16,48,640]{2,1,0:T(8,128)(2,1)}), bf16[16,48,640]{2,1,0:T(8,128)(2,1)S(1)}, u32[]{:S(2)}, u32[]{:S(2)}) %all-to-all-start) | async-done | bytes 983072 | tf_op jit(solution)/shard_map/all_to_all | solution.py:378
  33.3 11.0 %attend_far.1 = bf16[8,48,512]{2,1,0:T(8,128)(2,1)} custom-call(s32[1]{0:T(128)} %bitcast.me_ref, s32[16,8]{1,0:T(8,128)} %copy-done.3, s32[16]{0:T(128)} %held_ref.5, s32[16]{0:T(128)} %taken_ref.5, s32[16,16]{1,0:T(8,128)} %get-tuple-element.44.told_ref, bf16[16,48,640]{2,1,0:T(8,128)(2,1)} %copy-done.13, bf16[64,576,128]{2,1,0:T(8,128)(2,1)} %bitcast.96), custom_call_target="tpu_custom_call" | custom-call | flops 4000000000 | bytes 12000000 | tf_op jit(solution)/shard_map/attend_far/pallas_call | solution.py:184
  50.0 1.4 collective-permute-start.1
  54.7 1.4 collective-permute-start.9
  56.8 1.7 collective-permute-start.10
  59.6 2.4 collective-permute-start.5
  61.9 2.0 collective-permute-start.4
  63.9 1.6 fusion.12
  66.0 4.8 %collective-permute-done.9 = bf16[192,1024]{1,0:T(8,128)(2,1)S(1)} collective-permute-done((bf16[192,1024]{1,0:T(8,128)(2,1)S(1)}, bf16[192,1024]{1,0:T(8,128)(2,1)S(1)}, u32[]{:S(2)}, u32[]{:S(2)}) %collective-permute-start.9) | collective-permute-done | bytes 393248 | tf_op jit(solution)/shard_map/ppermute | solution.py:29
  70.9 2.6 collective-permute-start.3
  77.1 1.6 collective-permute-done.3
  80.5 1.2 copy.42
  81.7 8.3 %all-to-all-start.1 = ((bf16[16,48,448]{2,1,0:T(8,128)(2,1)}), bf16[16,48,448]{2,1,0:T(8,128)(2,1)S(1)}, u32[]{:S(2)}, u32[]{:S(2)}) async-start(bf16[16,48,448]{2,1,0:T(8,128)(2,1)} %bitcast.8), calls=%async_computation.1 | async-start | bytes 1572864 | tf_op jit(solution)/shard_map/all_to_all | solution.py:430
  90.0 11.5 %all-to-all-done.1 = bf16[16,48,448]{2,1,0:T(8,128)(2,1)S(1)} async-done(((bf16[16,48,448]{2,1,0:T(8,128)(2,1)}), bf16[16,48,448]{2,1,0:T(8,128)(2,1)S(1)}, u32[]{:S(2)}, u32[]{:S(2)}) %all-to-all-start.1) | async-done | bytes 688160 | tf_op jit(solution)/shard_map/all_to_all | solution.py:430
  101.9 1.6 collective-permute-done.12
  103.8 3.1 %collective-permute-start.13 = (bf16[2,48,448]{2,1,0:T(8,128)(2,1)S(1)}, bf16[2,48,448]{2,1,0:T(8,128)(2,1)S(1)}, u32[]{:S(2)}, u32[]{:S(2)}) collective-permute-start(bf16[2,48,448]{2,1,0:T(8,128)(2,1)S(1)} %get-tuple-element.31), channel_id=1, source_target_pairs={{0,4},{2,6},{4,0},{6,2},{1,5},{3,7},{5,1},{7,3},{8,12},{10,14},{12... | collective-permute-start | bytes 258056 | tf_op jit(solution)/shard_map/ppermute | solution.py:33
  107.4 2.6 collective-permute-start.15
  110.5 2.2 collective-permute-done.14
  113.8 3.3 %collective-permute-start.16 = (bf16[48,896]{1,0:T(8,128)(2,1)S(1)}, bf16[48,896]{1,0:T(8,128)(2,1)S(1)}, u32[]{:S(2)}, u32[]{:S(2)}) collective-permute-start(bf16[48,896]{1,0:T(8,128)(2,1)S(1)} %fusion.31), channel_id=1, source_target_pairs={{2,0},{4,2},{6,4},{0,6},{3,1},{5,3},{7,5},{1,7},{10,8},{12,10},{14... | collective-permute-start | bytes 258056 | tf_op jit(solution)/shard_map/ppermute | solution.py:29
  118.2 1.8 collective-permute-done.16
  120.0 3.1 %collective-permute-done.17 = bf16[48,896]{1,0:T(8,128)(2,1)S(1)} collective-permute-done((bf16[48,896]{1,0:T(8,128)(2,1)S(1)}, bf16[48,896]{1,0:T(8,128)(2,1)S(1)}, u32[]{:S(2)}, u32[]{:S(2)}) %collective-permute-start.17) | collective-permute-done | bytes 86048 | tf_op jit(solution)/shard_map/ppermute | solution.py:29
  124.3 1.2 collective-permute-done.19.there_ref
  125.5 3.1 %home_rows.1 = (bf16[48,7168]{1,0:T(8,128)(2,1)}, bf16[512,384]{1,0:T(8,128)(2,1)S(1)}, bf16[512,2048]{1,0:T(8,128)(2,1)}) custom-call(s32[8]{0:T(128)S(1)} %pad_add_fusion.spot_ref, bf16[48,3584]{1,0:T(8,128)(2,1)S(1)} %pad_maximum_fusion.4.here_ref, bf16[48,3584]{1,0:T(8,128)(2,1)S(1)} %collective-permute-done.19.there_ref, f32[1,3584]{1,0:T(1,128)S(1)} %bitcast.77, ...), custom_call_target="tpu_custom_call" | custom-call | tf_op jit(solution)/shard_map/home_rows/pallas_call | solution.py:233
  128.5 13.5 %all_to_all.30 = bf16[16,32,384]{2,1,0:T(8,128)(2,1)S(1)} all-to-all(bf16[16,32,384]{2,1,0:T(8,128)(2,1)S(1)} %bitcast.76), channel_id=1, replica_groups=mesh['y'=4,'z'=4,'x'=4,'core'=2] {'y','z'}, dimensions={0} | all-to-all | bytes 786432 | tf_op jit(solution)/shard_map/all_to_all | solution.py:469
  142.0 3.7 %all-to-all-start.3 = ((bf16[16,32,2048]{2,1,0:T(8,128)(2,1)}), bf16[16,32,2048]{2,1,0:T(8,128)(2,1)S(1)}, u32[]{:S(2)}, u32[]{:S(2)}) async-start(bf16[16,32,2048]{2,1,0:T(8,128)(2,1)} %bitcast.23), calls=%async_computation.3 | async-start | bytes 4194304 | tf_op jit(solution)/shard_map/all_to_all | solution.py:469
  147.3 27.6 %all-to-all-done.3 = bf16[16,32,2048]{2,1,0:T(8,128)(2,1)S(1)} async-done(((bf16[16,32,2048]{2,1,0:T(8,128)(2,1)}), bf16[16,32,2048]{2,1,0:T(8,128)(2,1)S(1)}, u32[]{:S(2)}, u32[]{:S(2)}) %all-to-all-start.3) | async-done | bytes 2097184 | tf_op jit(solution)/shard_map/all_to_all | solution.py:469
  175.0 12.5 %collective-permute-done.22 = bf16[512,384]{1,0:T(8,128)(2,1)S(1)} collective-permute-done((bf16[512,384]{1,0:T(8,128)(2,1)S(1)}, bf16[512,384]{1,0:T(8,128)(2,1)S(1)}, u32[]{:S(2)}, u32[]{:S(2)}) %collective-permute-start.22) | collective-permute-done | bytes 393248 | tf_op jit(solution)/shard_map/ppermute | solution.py:29
  188.8 7.0 %enter_first.1.refs_0_ = f32[512,512]{1,0:T(8,128)} custom-call(s32[4]{0:T(128)} %copy-done.17, bf16[512,1536]{1,0:T(8,128)(2,1)} %copy-done.7, bf16[512,2048]{1,0:T(8,128)(2,1)} %bitcast.79, bf16[1,7168,256]{2,1,0:T(8,128)(2,1)} %gate_ref.3, bf16[1,7168,256]{2,1,0:T(8,128)(2,1)} %up_ref.3), custom_call_target="tpu_custom_call" | custom-call | flops 1879048192 | bytes 8000000 | tf_op jit(solution)/shard_map/enter_first/pallas_call | solution.py:290
  197.0 1.3 copy-done.8
  198.3 7.4 %enter_last.1.hidden_ref = bf16[512,256]{1,0:T(8,128)(2,1)} custom-call(s32[4]{0:T(128)} %copy-done.18, bf16[512,1536]{1,0:T(8,128)(2,1)} %copy-done.10, bf16[512,2048]{1,0:T(8,128)(2,1)} %copy-done.8, bf16[1,7168,256]{2,1,0:T(8,128)(2,1)} %gate_ref.3, bf16[1,7168,256]{2,1,0:T(8,128)(2,1)} %up_ref.3, f32[512,512]{1,0:T(8,128)} %enter_first.1.refs_0_), custom_call_target="tpu_custom_call" | custom-call | flops 1879048192 | bytes 8000000 | tf_op jit(solution)/shard_map/enter_last/pallas_call | solution.py:290
  205.7 5.5 %leave_first.1 = (bf16[512,1536]{1,0:T(8,128)(2,1)}, bf16[512,2048]{1,0:T(8,128)(2,1)}) custom-call(s32[4]{0:T(128)} %copy-done.18, bf16[512,256]{1,0:T(8,128)(2,1)} %enter_last.1.hidden_ref, bf16[1,256,7168]{2,1,0:T(8,128)(2,1)} %down_ref.3), custom_call_target="tpu_custom_call" | custom-call | flops 939524096 | bytes 8000000 | tf_op jit(solution)/shard_map/leave_first/pallas_call | solution.py:332
  211.6 6.1 %collective-permute-done.25.refs_0_ = bf16[512,1536]{1,0:T(8,128)(2,1)S(1)} collective-permute-done((bf16[512,1536]{1,0:T(8,128)(2,1)}, bf16[512,1536]{1,0:T(8,128)(2,1)S(1)}, u32[]{:S(2)}, u32[]{:S(2)}) %collective-permute-start.25) | collective-permute-done | bytes 1572896 | tf_op jit(solution)/shard_map/ppermute | solution.py:37
  218.9 1.4 copy-done.9
  220.3 6.3 %leave_last.1 = (bf16[512,1536]{1,0:T(8,128)(2,1)}, bf16[512,2048]{1,0:T(8,128)(2,1)}) custom-call(s32[4]{0:T(128)} %copy-done.17, bf16[512,256]{1,0:T(8,128)(2,1)} %enter_last.1.hidden_ref, bf16[1,256,7168]{2,1,0:T(8,128)(2,1)} %down_ref.3, bf16[512,1536]{1,0:T(8,128)(2,1)} %copy-done.12, bf16[512,2048]{1,0:T(8,128)(2,1)} %copy-done.9), custom_call_target="tpu_custom_call" | custom-call | flops 939524096 | bytes 8000000 | tf_op jit(solution)/shard_map/leave_last/pallas_call | solution.py:332
  226.6 4.6 %all-to-all-start.4 = ((bf16[16,32,2048]{2,1,0:T(8,128)(2,1)}), bf16[16,32,2048]{2,1,0:T(8,128)(2,1)}, u32[]{:S(2)}, u32[]{:S(2)}) async-start(bf16[16,32,2048]{2,1,0:T(8,128)(2,1)} %bitcast.84), calls=%async_computation.4 | async-start | bytes 4194304 | tf_op jit(solution)/shard_map/all_to_all | solution.py:469
  231.9 3.0 %collective-permute-start.29 = (bf16[512,384]{1,0:T(8,128)(2,1)S(1)}, bf16[512,384]{1,0:T(8,128)(2,1)}, u32[]{:S(2)}, u32[]{:S(2)}) collective-permute-start(bf16[512,384]{1,0:T(8,128)(2,1)S(1)} %get-tuple-element.29), channel_id=1, source_target_pairs={{0,6},{2,0},{4,2},{6,4},{1,7},{3,1},{5,3},{7,5},{8,14},{10,8},{12,... | collective-permute-start | bytes 1179656 | tf_op jit(solution)/shard_map/ppermute | solution.py:33
  235.8 9.2 %collective-permute-done.27 = bf16[512,384]{1,0:T(8,128)(2,1)} collective-permute-done((bf16[512,384]{1,0:T(8,128)(2,1)S(1)}, bf16[512,384]{1,0:T(8,128)(2,1)}, u32[]{:S(2)}, u32[]{:S(2)}) %collective-permute-start.27) | collective-permute-done | bytes 393248 | tf_op jit(solution)/shard_map/ppermute | solution.py:33
  245.0 7.4 %collective-permute-done.28 = bf16[512,384]{1,0:T(8,128)(2,1)} collective-permute-done((bf16[512,384]{1,0:T(8,128)(2,1)S(1)}, bf16[512,384]{1,0:T(8,128)(2,1)}, u32[]{:S(2)}, u32[]{:S(2)}) %collective-permute-start.28) | collective-permute-done | bytes 393248 | tf_op jit(solution)/shard_map/ppermute | solution.py:33
  252.4 2.2 add_convert_fusion
  254.6 7.3 %all-to-all-done.4 = bf16[16,32,2048]{2,1,0:T(8,128)(2,1)} async-done(((bf16[16,32,2048]{2,1,0:T(8,128)(2,1)}), bf16[16,32,2048]{2,1,0:T(8,128)(2,1)}, u32[]{:S(2)}, u32[]{:S(2)}) %all-to-all-start.4) | async-done | bytes 2097184 | tf_op jit(solution)/shard_map/all_to_all | solution.py:469
  261.8 5.1 %all-to-all-start.5 = ((bf16[16,32,384]{2,1,0:T(8,128)(2,1)}), bf16[16,32,384]{2,1,0:T(8,128)(2,1)S(1)}, u32[]{:S(2)}, u32[]{:S(2)}) async-start(bf16[16,32,384]{2,1,0:T(8,128)(2,1)} %bitcast.27), calls=%async_computation.5 | async-start | bytes 786432 | tf_op jit(solution)/shard_map/all_to_all | solution.py:469
  267.0 2.2 fusion.36
  269.9 2.8 collective-permute-start.32
  272.7 2.3 collective-permute-done.30
  (151 shorter events, 35.2 us)
Async XLA Ops:
  0.6 44.7 %copy-start = (bf16[16,512,128]{2,1,0:T(8,128)(2,1)S(1)}, bf16[16,512,128]{2,1,0:T(8,128)(2,1)}, u32[]{:S(2)}) copy-start(bf16[16,512,128]{2,1,0:T(8,128)(2,1)} %param.19) | copy-start | bytes 6291460
  1.6 5.8 %copy-start.3 = (s32[16,8]{1,0:T(8,128)}, s32[16,8]{1,0:T(8,128)S(1)}, u32[]{:S(2)}) copy-start(s32[16,8]{1,0:T(8,128)S(1)} %copy.36.page_ref) | copy-start | bytes 1540
  7.3 25.0 %all-to-all-start = ((bf16[16,48,640]{2,1,0:T(8,128)(2,1)}), bf16[16,48,640]{2,1,0:T(8,128)(2,1)S(1)}, u32[]{:S(2)}, u32[]{:S(2)}) async-start(bf16[16,48,640]{2,1,0:T(8,128)(2,1)} %pack.1), calls=%async_computation | async-start | bytes 1966080 | tf_op jit(solution)/shard_map/all_to_all | solution.py:378
  33.3 11.0 %copy-start.14 = (bf16[8,48,512]{2,1,0:T(8,128)(2,1)S(1)}, bf16[8,48,512]{2,1,0:T(8,128)(2,1)}, u32[]{:S(2)}) copy-start(bf16[8,48,512]{2,1,0:T(8,128)(2,1)} %attend_own.1) | copy-start | bytes 1179652
  46.5 6.2 %collective-permute-start.6 = (bf16[48,1024]{1,0:T(8,128)(2,1)S(1)}, bf16[48,1024]{1,0:T(8,128)(2,1)S(1)}, u32[]{:S(2)}, u32[]{:S(2)}) collective-permute-start(bf16[48,1024]{1,0:T(8,128)(2,1)S(1)} %get-tuple-element.41), channel_id=1, source_target_pairs={{32,0},{64,32},{96,64},{0,96},{33,1},{65,33},{97,65},{1,97},{34,2}... | collective-permute-start | bytes 294920 | tf_op jit(solution)/shard_map/ppermute | solution.py:29
  47.5 6.2 %collective-permute-start.7 = (bf16[48,1024]{1,0:T(8,128)(2,1)S(1)}, bf16[48,1024]{1,0:T(8,128)(2,1)S(1)}, u32[]{:S(2)}, u32[]{:S(2)}) collective-permute-start(bf16[48,1024]{1,0:T(8,128)(2,1)S(1)} %get-tuple-element.41), channel_id=1, source_target_pairs={{64,0},{96,32},{0,64},{32,96},{65,1},{97,33},{1,65},{33,97},{66,2}... | collective-permute-start | bytes 294920 | tf_op jit(solution)/shard_map/ppermute | solution.py:29
  48.2 6.5 %collective-permute-start.8 = (bf16[48,1024]{1,0:T(8,128)(2,1)S(1)}, bf16[48,1024]{1,0:T(8,128)(2,1)S(1)}, u32[]{:S(2)}, u32[]{:S(2)}) collective-permute-start(bf16[48,1024]{1,0:T(8,128)(2,1)S(1)} %get-tuple-element.41), channel_id=1, source_target_pairs={{96,0},{0,32},{32,64},{64,96},{97,1},{1,33},{33,65},{65,97},{98,2}... | collective-permute-start | bytes 294920 | tf_op jit(solution)/shard_map/ppermute | solution.py:29
  48.9 7.9 %collective-permute-start = (bf16[48,1024]{1,0:T(8,128)(2,1)S(1)}, bf16[48,1024]{1,0:T(8,128)(2,1)S(1)}, u32[]{:S(2)}, u32[]{:S(2)}) collective-permute-start(bf16[48,1024]{1,0:T(8,128)(2,1)S(1)} %get-tuple-element.42), channel_id=1, source_target_pairs={{8,0},{16,8},{24,16},{0,24},{9,1},{17,9},{25,17},{1,25},{10,2},{18... | collective-permute-start | bytes 294920 | tf_op jit(solution)/shard_map/ppermute | solution.py:29
  50.0 8.4 %collective-permute-start.1 = (bf16[48,1024]{1,0:T(8,128)(2,1)S(1)}, bf16[48,1024]{1,0:T(8,128)(2,1)S(1)}, u32[]{:S(2)}, u32[]{:S(2)}) collective-permute-start(bf16[48,1024]{1,0:T(8,128)(2,1)S(1)} %get-tuple-element.42), channel_id=1, source_target_pairs={{16,0},{24,8},{0,16},{8,24},{17,1},{25,9},{1,17},{9,25},{18,2},{26... | collective-permute-start | bytes 294920 | tf_op jit(solution)/shard_map/ppermute | solution.py:29
  52.6 6.9 %collective-permute-start.2 = (bf16[48,1024]{1,0:T(8,128)(2,1)S(1)}, bf16[48,1024]{1,0:T(8,128)(2,1)S(1)}, u32[]{:S(2)}, u32[]{:S(2)}) collective-permute-start(bf16[48,1024]{1,0:T(8,128)(2,1)S(1)} %get-tuple-element.42), channel_id=1, source_target_pairs={{24,0},{0,8},{8,16},{16,24},{25,1},{1,9},{9,17},{17,25},{26,2},{2,... | collective-permute-start | bytes 294920 | tf_op jit(solution)/shard_map/ppermute | solution.py:29
  54.7 16.2 %collective-permute-start.9 = (bf16[192,1024]{1,0:T(8,128)(2,1)S(1)}, bf16[192,1024]{1,0:T(8,128)(2,1)S(1)}, u32[]{:S(2)}, u32[]{:S(2)}) collective-permute-start(bf16[192,1024]{1,0:T(8,128)(2,1)S(1)} %pad_maximum_fusion.3), channel_id=1, source_target_pairs={{8,0},{16,8},{24,16},{0,24},{9,1},{17,9},{25,17},{1,25},{10,2},{18... | collective-permute-start | bytes 1179656 | tf_op jit(solution)/shard_map/ppermute | solution.py:29
  56.1 18.9 %collective-permute-start.11 = (bf16[192,1024]{1,0:T(8,128)(2,1)S(1)}, bf16[192,1024]{1,0:T(8,128)(2,1)S(1)}, u32[]{:S(2)}, u32[]{:S(2)}) collective-permute-start(bf16[192,1024]{1,0:T(8,128)(2,1)S(1)} %pad_maximum_fusion.3), channel_id=1, source_target_pairs={{24,0},{0,8},{8,16},{16,24},{25,1},{1,9},{9,17},{17,25},{26,2},{2,... | collective-permute-start | bytes 1179656 | tf_op jit(solution)/shard_map/ppermute | solution.py:29
  56.8 18.7 %collective-permute-start.10 = (bf16[192,1024]{1,0:T(8,128)(2,1)S(1)}, bf16[192,1024]{1,0:T(8,128)(2,1)S(1)}, u32[]{:S(2)}, u32[]{:S(2)}) collective-permute-start(bf16[192,1024]{1,0:T(8,128)(2,1)S(1)} %pad_maximum_fusion.3), channel_id=1, source_target_pairs={{16,0},{24,8},{0,16},{8,24},{17,1},{25,9},{1,17},{9,25},{18,2},{26... | collective-permute-start | bytes 1179656 | tf_op jit(solution)/shard_map/ppermute | solution.py:29
  59.5 6.0 %copy-start.20 = (bf16[2048,448]{0,1:T(8,128)(2,1)S(1)}, bf16[2048,448]{0,1:T(8,128)(2,1)}, u32[]{:S(2)}) copy-start(bf16[2048,448]{0,1:T(8,128)(2,1)} %param.20) | copy-start | bytes 5505028
  59.6 16.3 %collective-permute-start.5 = (bf16[192,1024]{1,0:T(8,128)(2,1)S(1)}, bf16[192,1024]{1,0:T(8,128)(2,1)S(1)}, u32[]{:S(2)}, u32[]{:S(2)}) collective-permute-start(bf16[192,1024]{1,0:T(8,128)(2,1)S(1)} %pad_maximum_fusion.2), channel_id=1, source_target_pairs={{96,0},{0,32},{32,64},{64,96},{97,1},{1,33},{33,65},{65,97},{98,2}... | collective-permute-start | bytes 1179656 | tf_op jit(solution)/shard_map/ppermute | solution.py:29
  61.9 14.7 %collective-permute-start.4 = (bf16[192,1024]{1,0:T(8,128)(2,1)S(1)}, bf16[192,1024]{1,0:T(8,128)(2,1)S(1)}, u32[]{:S(2)}, u32[]{:S(2)}) collective-permute-start(bf16[192,1024]{1,0:T(8,128)(2,1)S(1)} %pad_maximum_fusion.2), channel_id=1, source_target_pairs={{64,0},{96,32},{0,64},{32,96},{65,1},{97,33},{1,65},{33,97},{66,2}... | collective-permute-start | bytes 1179656 | tf_op jit(solution)/shard_map/ppermute | solution.py:29
  70.9 7.8 %collective-permute-start.3 = (bf16[192,1024]{1,0:T(8,128)(2,1)S(1)}, bf16[192,1024]{1,0:T(8,128)(2,1)S(1)}, u32[]{:S(2)}, u32[]{:S(2)}) collective-permute-start(bf16[192,1024]{1,0:T(8,128)(2,1)S(1)} %pad_maximum_fusion.2), channel_id=1, source_target_pairs={{32,0},{64,32},{96,64},{0,96},{33,1},{65,33},{97,65},{1,97},{34,2}... | collective-permute-start | bytes 1179656 | tf_op jit(solution)/shard_map/ppermute | solution.py:29
  81.7 20.1 %copy-start.16 = (s32[48,8]{0,1:T(8,128)S(1)}, s32[48,8]{0,1:T(8,128)}, u32[]{:S(2)}) copy-start(s32[48,8]{0,1:T(8,128)} %param.23) | copy-start | bytes 4612
  81.7 19.8 %all-to-all-start.1 = ((bf16[16,48,448]{2,1,0:T(8,128)(2,1)}), bf16[16,48,448]{2,1,0:T(8,128)(2,1)S(1)}, u32[]{:S(2)}, u32[]{:S(2)}) async-start(bf16[16,48,448]{2,1,0:T(8,128)(2,1)} %bitcast.8), calls=%async_computation.1 | async-start | bytes 1572864 | tf_op jit(solution)/shard_map/all_to_all | solution.py:430
  101.7 1.8 collective-permute-start.12
  103.7 20.1 %copy-start.15 = (f32[7168]{0:T(1024)S(1)}, f32[7168]{0:T(1024)}, u32[]{:S(2)}) copy-start(f32[7168]{0:T(1024)} %param.22) | copy-start | bytes 86020
  103.8 6.7 %collective-permute-start.13 = (bf16[2,48,448]{2,1,0:T(8,128)(2,1)S(1)}, bf16[2,48,448]{2,1,0:T(8,128)(2,1)S(1)}, u32[]{:S(2)}, u32[]{:S(2)}) collective-permute-start(bf16[2,48,448]{2,1,0:T(8,128)(2,1)S(1)} %get-tuple-element.31), channel_id=1, source_target_pairs={{0,4},{2,6},{4,0},{6,2},{1,5},{3,7},{5,1},{7,3},{8,12},{10,14},{12... | collective-permute-start | bytes 258056 | tf_op jit(solution)/shard_map/ppermute | solution.py:33
  106.9 5.8 %collective-permute-start.14 = (bf16[2,48,448]{2,1,0:T(8,128)(2,1)S(1)}, bf16[2,48,448]{2,1,0:T(8,128)(2,1)S(1)}, u32[]{:S(2)}, u32[]{:S(2)}) collective-permute-start(bf16[2,48,448]{2,1,0:T(8,128)(2,1)S(1)} %get-tuple-element.33), channel_id=1, source_target_pairs={{0,2},{2,4},{4,6},{6,0},{1,3},{3,5},{5,7},{7,1},{8,10},{10,12},{12... | collective-permute-start | bytes 258056 | tf_op jit(solution)/shard_map/ppermute | solution.py:33
  107.4 5.2 %collective-permute-start.15 = (bf16[2,48,448]{2,1,0:T(8,128)(2,1)S(1)}, bf16[2,48,448]{2,1,0:T(8,128)(2,1)S(1)}, u32[]{:S(2)}, u32[]{:S(2)}) collective-permute-start(bf16[2,48,448]{2,1,0:T(8,128)(2,1)S(1)} %get-tuple-element.32), channel_id=1, source_target_pairs={{0,6},{2,0},{4,2},{6,4},{1,7},{3,1},{5,3},{7,5},{8,14},{10,8},{12,... | collective-permute-start | bytes 258056 | tf_op jit(solution)/shard_map/ppermute | solution.py:33
  113.8 6.3 %collective-permute-start.16 = (bf16[48,896]{1,0:T(8,128)(2,1)S(1)}, bf16[48,896]{1,0:T(8,128)(2,1)S(1)}, u32[]{:S(2)}, u32[]{:S(2)}) collective-permute-start(bf16[48,896]{1,0:T(8,128)(2,1)S(1)} %fusion.31), channel_id=1, source_target_pairs={{2,0},{4,2},{6,4},{0,6},{3,1},{5,3},{7,5},{1,7},{10,8},{12,10},{14... | collective-permute-start | bytes 258056 | tf_op jit(solution)/shard_map/ppermute | solution.py:29
  117.1 6.1 %collective-permute-start.17 = (bf16[48,896]{1,0:T(8,128)(2,1)S(1)}, bf16[48,896]{1,0:T(8,128)(2,1)S(1)}, u32[]{:S(2)}, u32[]{:S(2)}) collective-permute-start(bf16[48,896]{1,0:T(8,128)(2,1)S(1)} %fusion.31), channel_id=1, source_target_pairs={{4,0},{6,2},{0,4},{2,6},{5,1},{7,3},{1,5},{3,7},{12,8},{14,10},{8,... | collective-permute-start | bytes 258056 | tf_op jit(solution)/shard_map/ppermute | solution.py:29
  117.1 6.6 %collective-permute-start.18 = (bf16[48,896]{1,0:T(8,128)(2,1)S(1)}, bf16[48,896]{1,0:T(8,128)(2,1)S(1)}, u32[]{:S(2)}, u32[]{:S(2)}) collective-permute-start(bf16[48,896]{1,0:T(8,128)(2,1)S(1)} %fusion.31), channel_id=1, source_target_pairs={{6,0},{0,2},{2,4},{4,6},{7,1},{1,3},{3,5},{5,7},{14,8},{8,10},{10,... | collective-permute-start | bytes 258056 | tf_op jit(solution)/shard_map/ppermute | solution.py:29
  123.7 1.7 collective-permute-start.19
  124.1 17.9 %copy-start.17 = (s32[4]{0:T(128)}, s32[4]{0:T(128)S(1)}, u32[]{:S(2)}) copy-start(s32[4]{0:T(128)S(1)} %get-tuple-element.46.spot_ref) | copy-start | bytes 52
  124.1 17.8 %copy-start.18 = (s32[4]{0:T(128)}, s32[4]{0:T(128)S(1)}, u32[]{:S(2)}) copy-start(s32[4]{0:T(128)S(1)} %get-tuple-element.45.spot_ref) | copy-start | bytes 52
  142.0 32.9 %all-to-all-start.3 = ((bf16[16,32,2048]{2,1,0:T(8,128)(2,1)}), bf16[16,32,2048]{2,1,0:T(8,128)(2,1)S(1)}, u32[]{:S(2)}, u32[]{:S(2)}) async-start(bf16[16,32,2048]{2,1,0:T(8,128)(2,1)} %bitcast.23), calls=%async_computation.3 | async-start | bytes 4194304 | tf_op jit(solution)/shard_map/all_to_all | solution.py:469
  145.7 29.2 %collective-permute-start.20 = (bf16[512,384]{1,0:T(8,128)(2,1)S(1)}, bf16[512,384]{1,0:T(8,128)(2,1)S(1)}, u32[]{:S(2)}, u32[]{:S(2)}) collective-permute-start(bf16[512,384]{1,0:T(8,128)(2,1)S(1)} %bitcast.86), channel_id=1, source_target_pairs={{2,0},{4,2},{6,4},{0,6},{3,1},{5,3},{7,5},{1,7},{10,8},{12,10},{14... | collective-permute-start | bytes 1179656 | tf_op jit(solution)/shard_map/ppermute | solution.py:29
  146.6 28.4 %collective-permute-start.21 = (bf16[512,384]{1,0:T(8,128)(2,1)S(1)}, bf16[512,384]{1,0:T(8,128)(2,1)S(1)}, u32[]{:S(2)}, u32[]{:S(2)}) collective-permute-start(bf16[512,384]{1,0:T(8,128)(2,1)S(1)} %bitcast.87), channel_id=1, source_target_pairs={{4,0},{6,2},{0,4},{2,6},{5,1},{7,3},{1,5},{3,7},{12,8},{14,10},{8,... | collective-permute-start | bytes 1179656 | tf_op jit(solution)/shard_map/ppermute | solution.py:29
  174.8 12.8 %copy-start.6 = (bf16[16,32,2048]{2,1,0:T(8,128)(2,1)}, bf16[16,32,2048]{2,1,0:T(8,128)(2,1)S(1)}, u32[]{:S(2)}) copy-start(bf16[16,32,2048]{2,1,0:T(8,128)(2,1)S(1)} %all-to-all-done.3) | copy-start | bytes 6291460
  174.8 21.0 %collective-permute-start.24 = (bf16[512,2048]{1,0:T(8,128)(2,1)S(1)}, bf16[512,2048]{1,0:T(8,128)(2,1)S(1)}, u32[]{:S(2)}, u32[]{:S(2)}) collective-permute-start(bf16[512,2048]{1,0:T(8,128)(2,1)S(1)} %bitcast.78), channel_id=1, source_target_pairs={{0,1},{1,0},{2,3},{3,2},{4,5},{5,4},{6,7},{7,6},{8,9},{9,8},{10,11... | collective-permute-start | bytes 6291464 | tf_op jit(solution)/shard_map/ppermute | solution.py:37
  174.8 12.7 %collective-permute-start.22 = (bf16[512,384]{1,0:T(8,128)(2,1)S(1)}, bf16[512,384]{1,0:T(8,128)(2,1)S(1)}, u32[]{:S(2)}, u32[]{:S(2)}) collective-permute-start(bf16[512,384]{1,0:T(8,128)(2,1)S(1)} %bitcast.88), channel_id=1, source_target_pairs={{6,0},{0,2},{2,4},{4,6},{7,1},{1,3},{3,5},{5,7},{14,8},{8,10},{10,... | collective-permute-start | bytes 1179656 | tf_op jit(solution)/shard_map/ppermute | solution.py:29
  187.7 8.2 %collective-permute-start.23 = (bf16[512,1536]{1,0:T(8,128)(2,1)S(1)}, bf16[512,1536]{1,0:T(8,128)(2,1)S(1)}, u32[]{:S(2)}, u32[]{:S(2)}) collective-permute-start(bf16[512,1536]{1,0:T(8,128)(2,1)S(1)} %constant_dynamic-update-slice_fusion.early_ref), channel_id=1, source_target_pairs={{0,1},{1,0},{2,3},{3,2},{4,5},{5,4},{6,7},{7,6},{8,9},{9,8},{10,11... | collective-permute-start | bytes 4718600 | tf_op jit(solution)/shard_map/ppermute | solution.py:37
  211.1 6.6 %collective-permute-start.26 = (bf16[512,2048]{1,0:T(8,128)(2,1)}, bf16[512,2048]{1,0:T(8,128)(2,1)S(1)}, u32[]{:S(2)}, u32[]{:S(2)}) collective-permute-start(bf16[512,2048]{1,0:T(8,128)(2,1)} %get-tuple-element.19), channel_id=1, source_target_pairs={{0,1},{1,0},{2,3},{3,2},{4,5},{5,4},{6,7},{7,6},{8,9},{9,8},{10,11... | collective-permute-start | bytes 6291464 | tf_op jit(solution)/shard_map/ppermute | solution.py:37
  211.1 6.6 %collective-permute-start.25 = (bf16[512,1536]{1,0:T(8,128)(2,1)}, bf16[512,1536]{1,0:T(8,128)(2,1)S(1)}, u32[]{:S(2)}, u32[]{:S(2)}) collective-permute-start(bf16[512,1536]{1,0:T(8,128)(2,1)} %get-tuple-element.18), channel_id=1, source_target_pairs={{0,1},{1,0},{2,3},{3,2},{4,5},{5,4},{6,7},{7,6},{8,9},{9,8},{10,11... | collective-permute-start | bytes 4718600 | tf_op jit(solution)/shard_map/ppermute | solution.py:37
  226.6 35.3 %all-to-all-start.4 = ((bf16[16,32,2048]{2,1,0:T(8,128)(2,1)}), bf16[16,32,2048]{2,1,0:T(8,128)(2,1)}, u32[]{:S(2)}, u32[]{:S(2)}) async-start(bf16[16,32,2048]{2,1,0:T(8,128)(2,1)} %bitcast.84), calls=%async_computation.4 | async-start | bytes 4194304 | tf_op jit(solution)/shard_map/all_to_all | solution.py:469
  231.3 13.7 %collective-permute-start.27 = (bf16[512,384]{1,0:T(8,128)(2,1)S(1)}, bf16[512,384]{1,0:T(8,128)(2,1)}, u32[]{:S(2)}, u32[]{:S(2)}) collective-permute-start(bf16[512,384]{1,0:T(8,128)(2,1)S(1)} %get-tuple-element.28), channel_id=1, source_target_pairs={{0,4},{2,6},{4,0},{6,2},{1,5},{3,7},{5,1},{7,3},{8,12},{10,14},{12... | collective-permute-start | bytes 1179656 | tf_op jit(solution)/shard_map/ppermute | solution.py:33
  231.6 20.8 %collective-permute-start.28 = (bf16[512,384]{1,0:T(8,128)(2,1)S(1)}, bf16[512,384]{1,0:T(8,128)(2,1)}, u32[]{:S(2)}, u32[]{:S(2)}) collective-permute-start(bf16[512,384]{1,0:T(8,128)(2,1)S(1)} %get-tuple-element.30), channel_id=1, source_target_pairs={{0,2},{2,4},{4,6},{6,0},{1,3},{3,5},{5,7},{7,1},{8,10},{10,12},{12... | collective-permute-start | bytes 1179656 | tf_op jit(solution)/shard_map/ppermute | solution.py:33
  231.9 20.5 %collective-permute-start.29 = (bf16[512,384]{1,0:T(8,128)(2,1)S(1)}, bf16[512,384]{1,0:T(8,128)(2,1)}, u32[]{:S(2)}, u32[]{:S(2)}) collective-permute-start(bf16[512,384]{1,0:T(8,128)(2,1)S(1)} %get-tuple-element.29), channel_id=1, source_target_pairs={{0,6},{2,0},{4,2},{6,4},{1,7},{3,1},{5,3},{7,5},{8,14},{10,8},{12,... | collective-permute-start | bytes 1179656 | tf_op jit(solution)/shard_map/ppermute | solution.py:33
  261.8 14.3 %all-to-all-start.5 = ((bf16[16,32,384]{2,1,0:T(8,128)(2,1)}), bf16[16,32,384]{2,1,0:T(8,128)(2,1)S(1)}, u32[]{:S(2)}, u32[]{:S(2)}) async-start(bf16[16,32,384]{2,1,0:T(8,128)(2,1)} %bitcast.27), calls=%async_computation.5 | async-start | bytes 786432 | tf_op jit(solution)/shard_map/all_to_all | solution.py:469
  266.9 10.1 %copy-start.1 = (bf16[16,512,128]{2,1,0:T(8,128)(2,1)S(1)}, bf16[16,512,128]{2,1,0:T(8,128)(2,1)}, u32[]{:S(2)}) copy-start(bf16[16,512,128]{2,1,0:T(8,128)(2,1)} %param.19) | copy-start | bytes 6291460
  269.2 5.8 %collective-permute-start.30 = (bf16[48,512]{1,0:T(8,128)(2,1)S(1)}, bf16[48,512]{1,0:T(8,128)(2,1)S(1)}, u32[]{:S(2)}, u32[]{:S(2)}) collective-permute-start(bf16[48,512]{1,0:T(8,128)(2,1)S(1)} %get-tuple-element.36), channel_id=1, source_target_pairs={{0,4},{2,6},{4,0},{6,2},{1,5},{3,7},{5,1},{7,3},{8,12},{10,14},{12... | collective-permute-start | bytes 147464 | tf_op jit(solution)/shard_map/ppermute | solution.py:33
  269.5 5.8 %collective-permute-start.31 = (bf16[48,512]{1,0:T(8,128)(2,1)S(1)}, bf16[48,512]{1,0:T(8,128)(2,1)S(1)}, u32[]{:S(2)}, u32[]{:S(2)}) collective-permute-start(bf16[48,512]{1,0:T(8,128)(2,1)S(1)} %get-tuple-element.38), channel_id=1, source_target_pairs={{0,2},{2,4},{4,6},{6,0},{1,3},{3,5},{5,7},{7,1},{8,10},{10,12},{12... | collective-permute-start | bytes 147464 | tf_op jit(solution)/shard_map/ppermute | solution.py:33
  269.9 5.4 %collective-permute-start.32 = (bf16[48,512]{1,0:T(8,128)(2,1)S(1)}, bf16[48,512]{1,0:T(8,128)(2,1)S(1)}, u32[]{:S(2)}, u32[]{:S(2)}) collective-permute-start(bf16[48,512]{1,0:T(8,128)(2,1)S(1)} %get-tuple-element.37), channel_id=1, source_target_pairs={{0,6},{2,0},{4,2},{6,4},{1,7},{3,1},{5,3},{7,5},{8,14},{10,8},{12,... | collective-permute-start | bytes 147464 | tf_op jit(solution)/shard_map/ppermute | solution.py:33
  (11 other events, 18.4 us)
